TPU v7x, 512 devices: a whole 4x8x8 slice. The times are simulated.
512 devices in a mesh: section: 8 (over y_lo, core), ctx: 64 (over z, y_hi, x).
Axes of the slice: x: 4, y: 8 (y_hi: 2, y_lo: 4; y = y_hi * 4 + y_lo), z: 8, core: 2. Of those that a mesh axis runs over, the one named last changes fastest.
Arguments:
- queries: bfloat16 [8, 8192, 2560], P('section', 'ctx'), may hold values from -6 to 6
- keys: bfloat16 [8192, 512], P('ctx'), may hold values from -6 to 6
- values: bfloat16 [8192, 512], P('ctx'), may hold values from -6 to 6
- cotangent: bfloat16 [8, 8192, 2560], P('section', 'ctx'), may hold values from -6 to 6
- segment_ids: int32 [8192], P('ctx'), may hold values from 0 to 95, never falling along the last dimension, each value on 1 to 256 neighbouring positions
Outputs:
- grad_queries: bfloat16 [8, 8192, 2560], P('section', 'ctx')
- grad_keys: float32 [8192, 512], P('ctx', 'section')
- grad_values: float32 [8192, 512], P('ctx', 'section')
Inputs may be any that keep to these rules, and one draw needn't show every extreme that they name: `segment_ids`: ids never fall; each document covers 1 to 256 tokens, one exactly 256.
All inputs are finite; a program needn't handle non-finite values.
Results may differ from a plain program's by a relative error of at most 0.007.
Values may be sent and summed in bfloat16 or wider, within the bound.
No kernel may reach another device: no remote copies, remote signals or barrier semaphores. Data moves between devices by JAX's collectives and lax.ppermute only.
A program may use at most 64 MiB of HBM per device.

v0:
```python
import jax
import jax.numpy as jnp
from jax import lax
from jax.sharding import PartitionSpec as P

DH = 128
DOC_SHARDS = 2


def shifted(shard, axis, by):
    size = lax.axis_size(axis)
    pairs = [(i, i + by) for i in range(size) if 0 <= i + by < size]
    return lax.ppermute(shard, axis, pairs)


def as_sent(shard):

    def short(part):
        return part.astype(jnp.bfloat16) if part.dtype == jnp.float32 else part

    return jax.tree.map(short, shard)


def by_group(rows, groups):
    count, width = rows.shape
    head_ratio = width // (groups * DH)
    return (
        rows.reshape(count, groups, head_ratio, DH)
        .transpose(1, 2, 0, 3)
        .reshape(groups, head_ratio * count, DH)
    )


def add_pair(first, second):
    return (first[0] + second[0], first[1] + second[1])


def on_device(queries, keys, values, cotangent, segment_ids):
    tok_rows = keys.shape[0]
    groups = keys.shape[1] // DH
    heads = queries.shape[2] // DH
    head_ratio = heads // groups
    score_scale = DH ** (-0.5)
    cycle_size = lax.axis_size("ctx")
    my_index = lax.axis_index("ctx")
    query_rows = by_group(queries[0], groups)
    grad_rows = by_group(cotangent[0], groups)
    row_pos = my_index * tok_rows + jnp.tile(jnp.arange(tok_rows, dtype=jnp.int32), head_ratio)
    row_seg = jnp.tile(segment_ids, head_ratio)
    blocks = []
    current = (keys, values, segment_ids)
    for shard_step in range(DOC_SHARDS + 1):
        if shard_step > 0:
            current = shifted((current[0], current[1], current[2]), "ctx", 1)
        key_block, value_block, key_seg = current
        key_rows = key_block.reshape(tok_rows, groups, DH).transpose(1, 0, 2)
        value_rows = value_block.reshape(tok_rows, groups, DH).transpose(1, 0, 2)
        key_pos = (my_index - shard_step) % cycle_size * tok_rows + jnp.arange(
            tok_rows, dtype=jnp.int32
        )
        allowed = (row_seg[:, None] == key_seg[None, :]) & (key_pos[None, :] <= row_pos[:, None])
        if shard_step == 0:
            is_live = jnp.array(True)
        else:
            is_live = (my_index >= shard_step) & (key_seg[-1] >= segment_ids[0])
        blocks.append((key_rows, value_rows, allowed, is_live))
    row_count = head_ratio * tok_rows
    row_max = jnp.full((groups, row_count, 1), -1e30, jnp.float32)
    row_sum = jnp.zeros((groups, row_count, 1), jnp.float32)
    kept_scores = []
    for key_rows, value_rows, allowed, is_live in blocks:

        def running_stats(key_rows=key_rows, allowed=allowed, row_max=row_max, row_sum=row_sum):
            scores = (
                jnp.einsum("grd,gkd->grk", query_rows, key_rows, preferred_element_type=jnp.float32)
                * score_scale
            )
            block_max = jnp.max(jnp.where(allowed, scores, -1e30), -1, keepdims=True)
            new_max = jnp.maximum(row_max, block_max)
            added = jnp.sum(jnp.where(allowed, jnp.exp(scores - new_max), 0.0), -1, keepdims=True)
            return (new_max, row_sum * jnp.exp(row_max - new_max) + added, scores)

        row_max, row_sum, scores = running_stats()
        kept_scores.append(scores)
    log_total = row_max + jnp.log(row_sum)

    def block_probs(scores, allowed):
        return jnp.where(allowed, jnp.exp(scores - log_total), 0.0)

    output_rows = jnp.zeros((groups, row_count, DH), jnp.float32)
    for (key_rows, value_rows, allowed, is_live), scores in zip(blocks, kept_scores):

        def output_part(scores=scores, value_rows=value_rows, allowed=allowed):
            probs_low = block_probs(scores, allowed).astype(jnp.bfloat16)
            return jnp.einsum(
                "grk,gkd->grd", probs_low, value_rows, preferred_element_type=jnp.float32
            )

        output_rows = output_rows + output_part()
    row_dot = jnp.sum(grad_rows.astype(jnp.float32) * output_rows, -1, keepdims=True)
    grad_query = jnp.zeros((groups, row_count, DH), jnp.float32)
    partials = []
    for (key_rows, value_rows, allowed, is_live), scores in zip(blocks, kept_scores):

        def backward_part(scores=scores, key_rows=key_rows, value_rows=value_rows, allowed=allowed):
            probs = block_probs(scores, allowed)
            probs_low = probs.astype(jnp.bfloat16)
            grad_probs = jnp.einsum(
                "grd,gkd->grk", grad_rows, value_rows, preferred_element_type=jnp.float32
            )
            scaled_low = (probs * (grad_probs - row_dot) * score_scale).astype(jnp.bfloat16)
            query_part = jnp.einsum(
                "grk,gkd->grd", scaled_low, key_rows, preferred_element_type=jnp.float32
            )
            key_part = jnp.einsum(
                "grk,grd->gkd", scaled_low, query_rows, preferred_element_type=jnp.float32
            )
            value_part = jnp.einsum(
                "grk,grd->gkd", probs_low, grad_rows, preferred_element_type=jnp.float32
            )
            key_flat = key_part.transpose(1, 0, 2).reshape(tok_rows, groups * DH)
            value_flat = value_part.transpose(1, 0, 2).reshape(tok_rows, groups * DH)
            return (query_part, key_flat, value_flat)

        query_part, key_flat, value_flat = backward_part()
        grad_query = grad_query + query_part
        partials.append((key_flat, value_flat))
    summed = partials[0]
    for shard_step in range(1, DOC_SHARDS + 1):
        arrived = shifted(as_sent(partials[shard_step]), "ctx", -shard_step)
        summed = add_pair(summed, arrived)
    summed = lax.psum_scatter(summed, "section", scatter_dimension=1, tiled=True)
    query_out = (
        grad_query.reshape(groups, head_ratio, tok_rows, DH)
        .transpose(2, 0, 1, 3)
        .reshape(1, tok_rows, heads * DH)
    )
    return (query_out.astype(jnp.bfloat16), summed[0], summed[1])


def solution(mesh):
    placed = (
        P("section", "ctx", None),
        P("ctx", None),
        P("ctx", None),
        P("section", "ctx", None),
        P("ctx"),
    )
    return jax.shard_map(
        on_device,
        mesh=mesh,
        in_specs=placed,
        out_specs=(P("section", "ctx", None), P("ctx", "section"), P("ctx", "section")),
        check_vma=False,
    )
```

profile of v0, /device:TPU:2, one launch (start us, length us, event | category | flops | bytes accessed | tf_op | source)
XLA Modules:
  0.0 186.2 jit_solution(4993455840856612003)
XLA Ops:
  7.2 0.0 reduce-scatter.5.cloned.1.call-start
  7.2 3.4 %collective-permute-start = (s32[128]{0:T(128)}, s32[128]{0:T(128)S(1)}, u32[]{:S(2)}, u32[]{:S(2)}) collective-permute-start(s32[128]{0:T(128)} %param.9), channel_id=1, source_target_pairs={{0,1},{1,2},{2,3},{3,4},{4,5},{5,6},{6,7},{7,8},{8,9},{9,10},{10,1... | collective-permute-start | bytes 1544 | tf_op jit(solution)/shard_map/ppermute | solution.py:13
  10.6 1.0 copy.42
  11.6 3.1 %collective-permute-start.1 = (bf16[128,512]{0,1:T(8,128)(2,1)S(1)}, bf16[128,512]{0,1:T(8,128)(2,1)}, u32[]{:S(2)}, u32[]{:S(2)}) collective-permute-start(bf16[128,512]{0,1:T(8,128)(2,1)S(1)} %copy.42), channel_id=1, source_target_pairs={{0,1},{1,2},{2,3},{3,4},{4,5},{5,6},{6,7},{7,8},{8,9},{9,10},{10,1... | collective-permute-start | bytes 393224 | tf_op jit(solution)/shard_map/ppermute | solution.py:13
  14.8 7.7 %collective-permute-start.4 = (bf16[128,512]{1,0:T(8,128)(2,1)}, bf16[128,512]{1,0:T(8,128)(2,1)}, u32[]{:S(2)}, u32[]{:S(2)}) collective-permute-start(bf16[128,512]{1,0:T(8,128)(2,1)} %param.7), channel_id=1, source_target_pairs={{0,1},{1,2},{2,3},{3,4},{4,5},{5,6},{6,7},{7,8},{8,9},{9,10},{10,1... | collective-permute-start | bytes 393224 | tf_op jit(solution)/shard_map/ppermute | solution.py:13
  22.5 0.7 broadcast_bitcast_fusion
  23.1 1.7 copy.101
  24.8 3.5 %collective-permute-start.2 = (s32[128]{0:T(128)S(1)}, s32[128]{0:T(128)S(1)}, u32[]{:S(2)}, u32[]{:S(2)}) collective-permute-start(s32[128]{0:T(128)S(1)} %collective-permute-done), channel_id=1, source_target_pairs={{0,1},{1,2},{2,3},{3,4},{4,5},{5,6},{6,7},{7,8},{8,9},{9,10},{10,1... | collective-permute-start | bytes 1544 | tf_op jit(solution)/shard_map/ppermute | solution.py:13
  28.3 1.4 copy.39
  29.8 0.3 copy.40
  30.1 0.3 copy.45
  30.5 0.3 copy.46
  30.8 1.1 copy.49
  31.9 0.3 compare_and_fusion.2
  32.2 0.4 select_reduce_fusion.5
  32.6 1.7 copy.43
  34.3 3.4 %collective-permute-start.3 = (bf16[128,512]{0,1:T(8,128)(2,1)}, bf16[128,512]{0,1:T(8,128)(2,1)}, u32[]{:S(2)}, u32[]{:S(2)}) collective-permute-start(bf16[128,512]{0,1:T(8,128)(2,1)} %collective-permute-done.1), channel_id=1, source_target_pairs={{0,1},{1,2},{2,3},{3,4},{4,5},{5,6},{6,7},{7,8},{8,9},{9,10},{10,1... | collective-permute-start | bytes 393224 | tf_op jit(solution)/shard_map/ppermute | solution.py:13
  37.7 1.3 select_reduce_fusion.4
  39.1 1.6 copy.51
  40.7 3.1 %collective-permute-start.5 = (bf16[128,512]{1,0:T(8,128)(2,1)}, bf16[128,512]{1,0:T(8,128)(2,1)}, u32[]{:S(2)}, u32[]{:S(2)}) collective-permute-start(bf16[128,512]{1,0:T(8,128)(2,1)} %collective-permute-done.4), channel_id=1, source_target_pairs={{0,1},{1,2},{2,3},{3,4},{4,5},{5,6},{6,7},{7,8},{8,9},{9,10},{10,1... | collective-permute-start | bytes 393224 | tf_op jit(solution)/shard_map/ppermute | solution.py:13
  43.8 1.7 copy.44
  45.5 1.3 select_reduce_fusion.3
  46.8 0.3 select_reduce_fusion.2
  47.1 0.5 select_reduce_fusion
  47.7 0.7 copy-done.3
  48.4 1.2 convolution_convert_fusion.1
  49.5 1.2 fusion.28
  50.7 0.4 fusion.30
  51.1 0.5 copy-done.17
  51.6 1.4 convolution_add_fusion.1
  53.1 1.2 convolution_convert_fusion
  54.3 1.7 copy.53
  55.9 2.4 %fusion.11 = f32[4,640]{1,0:T(4,128)S(1)} fusion(f32[4,640,128]{1,2,0:T(8,128)} %convolution_add_fusion.1, bf16[4,128,128]{1,2,0:T(8,128)(2,1)} %bitcast.129, bf16[4,640,128]{1,2,0:T(8,128)(2,1)} %copy.49, f32[4,640,128]{1,2,0:T(8,128)} %copy-done, f32[4,640]{1,0:T(4,128)S(1)} %log_add_fusion, pred[640,128]{0,1:T(8,128)(4,1)S(1)} %get-tuple-element.11), kind=kOutput, calls=%fused_computation.30 | convolution fusion | flops 86177280 | bytes 3510272 | tf_op jit(solution)/shard_map/grk,gkd->grd/dot_general | solution.py:95
  58.4 0.6 fusion.8
  58.9 0.7 copy-done.1
  59.7 0.6 fusion.7
  60.2 0.4 copy-done.16
  60.7 0.6 fusion.9
  61.3 0.4 copy-done.22
  61.7 1.3 collective-permute-start.9
  63.0 3.5 %collective-permute-start.8 = (bf16[128,512]{0,1:T(8,128)(2,1)S(1)}, bf16[128,512]{0,1:T(8,128)(2,1)S(1)}, u32[]{:S(2)}, u32[]{:S(2)}) collective-permute-start(bf16[128,512]{0,1:T(8,128)(2,1)S(1)} %bitcast.131), channel_id=1, source_target_pairs={{1,0},{2,1},{3,2},{4,3},{5,4},{6,5},{7,6},{8,7},{9,8},{10,9},{11,1... | collective-permute-start | bytes 393224 | tf_op jit(solution)/shard_map/ppermute | solution.py:13
  66.6 1.1 convolution_convert_fusion.3
  67.6 2.0 %collective-permute-start.6 = (bf16[128,512]{0,1:T(8,128)(2,1)}, bf16[128,512]{0,1:T(8,128)(2,1)}, u32[]{:S(2)}, u32[]{:S(2)}) collective-permute-start(bf16[128,512]{0,1:T(8,128)(2,1)} %bitcast.28), channel_id=1, source_target_pairs={{1,0},{2,1},{3,2},{4,3},{5,4},{6,5},{7,6},{8,7},{9,8},{10,9},{11,1... | collective-permute-start | bytes 393224 | tf_op jit(solution)/shard_map/ppermute | solution.py:13
  69.7 1.1 convolution_convert_fusion.2
  70.8 1.3 collective-permute-start.7
  72.1 0.9 collective-permute-done.9
  73.0 3.0 %collective-permute-done.8 = bf16[128,512]{0,1:T(8,128)(2,1)S(1)} collective-permute-done((bf16[128,512]{0,1:T(8,128)(2,1)S(1)}, bf16[128,512]{0,1:T(8,128)(2,1)S(1)}, u32[]{:S(2)}, u32[]{:S(2)}) %collective-permute-start.8) | collective-permute-done | bytes 131104 | tf_op jit(solution)/shard_map/ppermute | solution.py:13
  76.0 0.7 fusion.15
  76.7 0.0 reduce-scatter.5.cloned.1.call-update
  76.8 0.0 reduce-scatter.3.cloned.1.call-start
  76.8 0.4 fusion.17
  77.2 0.4 fusion.41
  77.6 1.5 collective-permute-done.6
  79.2 3.3 %collective-permute-done.7 = bf16[128,512]{0,1:T(8,128)(2,1)} collective-permute-done((bf16[128,512]{0,1:T(8,128)(2,1)}, bf16[128,512]{0,1:T(8,128)(2,1)}, u32[]{:S(2)}, u32[]{:S(2)}) %collective-permute-start.7) | collective-permute-done | bytes 131104 | tf_op jit(solution)/shard_map/ppermute | solution.py:13
  82.5 1.7 fusion.16
  84.2 0.0 reduce-scatter.3.cloned.1.call-update
  84.3 0.4 convolution_add_fusion.3
  84.7 0.7 copy-done.8
  85.4 0.0 copy-done.12
  85.4 0.4 fusion.10
  85.8 0.3 copy.63
  86.1 1.1 copy.76
  87.2 51.7 %reduce-scatter.5.cloned.1.call-done = f32[128,64]{0,1:T(8,128)} async-done(((f32[128,512]{0,1:T(8,128)}), f32[128,64]{0,1:T(8,128)}) %reduce-scatter.5.cloned.1.call-update) | async-done | bytes 32784 | tf_op jit(solution)/shard_map/reduce_scatter | solution.py:132
  138.9 40.5 %reduce-scatter.3.cloned.1.call-done = f32[128,64]{0,1:T(8,128)} async-done(((f32[128,512]{0,1:T(8,128)}), f32[128,64]{0,1:T(8,128)}) %reduce-scatter.3.cloned.1.call-update) | async-done | bytes 32784 | tf_op jit(solution)/shard_map/reduce_scatter | solution.py:132
  (51 shorter events, 0.2 us)
Async XLA Ops:
  7.2 131.7 %reduce-scatter.5.cloned.1.call-start = ((), (), s32[]{:S(2)}) async-start(), calls=%async_computation.3 | async-start | bytes 294912 | tf_op jit(solution)/shard_map/reduce_scatter | solution.py:132
  7.2 17.6 %collective-permute-start = (s32[128]{0:T(128)}, s32[128]{0:T(128)S(1)}, u32[]{:S(2)}, u32[]{:S(2)}) collective-permute-start(s32[128]{0:T(128)} %param.9), channel_id=1, source_target_pairs={{0,1},{1,2},{2,3},{3,4},{4,5},{5,6},{6,7},{7,8},{8,9},{9,10},{10,1... | collective-permute-start | bytes 1544 | tf_op jit(solution)/shard_map/ppermute | solution.py:13
  11.6 21.0 %collective-permute-start.1 = (bf16[128,512]{0,1:T(8,128)(2,1)S(1)}, bf16[128,512]{0,1:T(8,128)(2,1)}, u32[]{:S(2)}, u32[]{:S(2)}) collective-permute-start(bf16[128,512]{0,1:T(8,128)(2,1)S(1)} %copy.42), channel_id=1, source_target_pairs={{0,1},{1,2},{2,3},{3,4},{4,5},{5,6},{6,7},{7,8},{8,9},{9,10},{10,1... | collective-permute-start | bytes 393224 | tf_op jit(solution)/shard_map/ppermute | solution.py:13
  14.8 24.3 %collective-permute-start.4 = (bf16[128,512]{1,0:T(8,128)(2,1)}, bf16[128,512]{1,0:T(8,128)(2,1)}, u32[]{:S(2)}, u32[]{:S(2)}) collective-permute-start(bf16[128,512]{1,0:T(8,128)(2,1)} %param.7), channel_id=1, source_target_pairs={{0,1},{1,2},{2,3},{3,4},{4,5},{5,6},{6,7},{7,8},{8,9},{9,10},{10,1... | collective-permute-start | bytes 393224 | tf_op jit(solution)/shard_map/ppermute | solution.py:13
  24.8 5.3 %copy-start.14 = (bf16[1,128,2560]{2,1,0:T(8,128)(2,1)S(1)}, bf16[1,128,2560]{2,1,0:T(8,128)(2,1)}, u32[]{:S(2)}) copy-start(bf16[1,128,2560]{2,1,0:T(8,128)(2,1)} %param.8) | copy-start | bytes 1966084
  24.8 7.1 %collective-permute-start.2 = (s32[128]{0:T(128)S(1)}, s32[128]{0:T(128)S(1)}, u32[]{:S(2)}, u32[]{:S(2)}) collective-permute-start(s32[128]{0:T(128)S(1)} %collective-permute-done), channel_id=1, source_target_pairs={{0,1},{1,2},{2,3},{3,4},{4,5},{5,6},{6,7},{7,8},{8,9},{9,10},{10,1... | collective-permute-start | bytes 1544 | tf_op jit(solution)/shard_map/ppermute | solution.py:13
  30.4 1.5 copy-start.20
  30.5 1.7 copy-start.9
  30.8 1.4 copy-start.2
  34.3 9.5 %collective-permute-start.3 = (bf16[128,512]{0,1:T(8,128)(2,1)}, bf16[128,512]{0,1:T(8,128)(2,1)}, u32[]{:S(2)}, u32[]{:S(2)}) collective-permute-start(bf16[128,512]{0,1:T(8,128)(2,1)} %collective-permute-done.1), channel_id=1, source_target_pairs={{0,1},{1,2},{2,3},{3,4},{4,5},{5,6},{6,7},{7,8},{8,9},{9,10},{10,1... | collective-permute-start | bytes 393224 | tf_op jit(solution)/shard_map/ppermute | solution.py:13
  40.7 13.6 %collective-permute-start.5 = (bf16[128,512]{1,0:T(8,128)(2,1)}, bf16[128,512]{1,0:T(8,128)(2,1)}, u32[]{:S(2)}, u32[]{:S(2)}) collective-permute-start(bf16[128,512]{1,0:T(8,128)(2,1)} %collective-permute-done.4), channel_id=1, source_target_pairs={{0,1},{1,2},{2,3},{3,4},{4,5},{5,6},{6,7},{7,8},{8,9},{9,10},{10,1... | collective-permute-start | bytes 393224 | tf_op jit(solution)/shard_map/ppermute | solution.py:13
  46.8 6.3 %copy-start = (f32[4,640,128]{1,2,0:T(8,128)}, f32[4,640,128]{1,2,0:T(8,128)S(1)}, u32[]{:S(2)}) copy-start(f32[4,640,128]{1,2,0:T(8,128)S(1)} %get-tuple-element.13) | copy-start | bytes 3932164
  47.1 1.3 copy-start.3
  49.5 1.2 copy-start.15
  50.7 0.9 copy-start.17
  55.9 2.4 %copy-start.4 = (bf16[4,5,128,128]{3,2,1,0:T(8,128)(2,1)S(1)}, bf16[4,5,128,128]{3,2,1,0:T(8,128)(2,1)}, u32[]{:S(2)}) copy-start(bf16[4,5,128,128]{3,2,1,0:T(8,128)(2,1)} %copy-done.2) | copy-start | bytes 1966084
  55.9 2.4 %copy-start.18 = (bf16[128,512]{0,1:T(8,128)(2,1)S(1)}, bf16[128,512]{0,1:T(8,128)(2,1)}, u32[]{:S(2)}) copy-start(bf16[128,512]{0,1:T(8,128)(2,1)} %copy.51) | copy-start | bytes 393220
  58.3 1.3 copy-start.1
  58.3 1.3 copy-start.19
  59.7 6.9 %copy-start.5 = (bf16[4,640,128]{1,2,0:T(8,128)(2,1)}, bf16[4,640,128]{1,2,0:T(8,128)(2,1)S(1)}, u32[]{:S(2)}) copy-start(bf16[4,640,128]{1,2,0:T(8,128)(2,1)S(1)} %fusion.8) | copy-start | bytes 1966084
  59.7 1.0 copy-start.16
  60.7 9.0 %copy-start.7 = (bf16[4,640,128]{1,2,0:T(8,128)(2,1)}, bf16[4,640,128]{1,2,0:T(8,128)(2,1)S(1)}, u32[]{:S(2)}) copy-start(bf16[4,640,128]{1,2,0:T(8,128)(2,1)S(1)} %fusion.7) | copy-start | bytes 1966084
  60.7 1.0 copy-start.22
  60.7 2.3 %copy-start.21 = (bf16[4,128,128]{1,2,0:T(8,128)(2,1)S(1)}, bf16[4,128,128]{1,2,0:T(8,128)(2,1)}, u32[]{:S(2)}) copy-start(bf16[4,128,128]{1,2,0:T(8,128)(2,1)} %convolution_convert_fusion.1) | copy-start | bytes 393220
  61.7 11.3 %collective-permute-start.9 = (bf16[128,512]{0,1:T(8,128)(2,1)S(1)}, bf16[128,512]{0,1:T(8,128)(2,1)S(1)}, u32[]{:S(2)}, u32[]{:S(2)}) collective-permute-start(bf16[128,512]{0,1:T(8,128)(2,1)S(1)} %bitcast.132), channel_id=1, source_target_pairs={{2,0},{3,1},{4,2},{5,3},{6,4},{7,5},{8,6},{9,7},{10,8},{11,9},{12,... | collective-permute-start | bytes 393224 | tf_op jit(solution)/shard_map/ppermute | solution.py:13
  63.0 13.0 %copy-start.13 = (f32[4,128,128]{1,2,0:T(8,128)S(1)}, f32[4,128,128]{1,2,0:T(8,128)}, u32[]{:S(2)}) copy-start(f32[4,128,128]{1,2,0:T(8,128)} %fusion.28) | copy-start | bytes 786436
  63.0 13.0 %collective-permute-start.8 = (bf16[128,512]{0,1:T(8,128)(2,1)S(1)}, bf16[128,512]{0,1:T(8,128)(2,1)S(1)}, u32[]{:S(2)}, u32[]{:S(2)}) collective-permute-start(bf16[128,512]{0,1:T(8,128)(2,1)S(1)} %bitcast.131), channel_id=1, source_target_pairs={{1,0},{2,1},{3,2},{4,3},{5,4},{6,5},{7,6},{8,7},{9,8},{10,9},{11,1... | collective-permute-start | bytes 393224 | tf_op jit(solution)/shard_map/ppermute | solution.py:13
  67.6 9.2 %copy-start.10 = (bf16[128,512]{1,0:T(8,128)(2,1)S(1)}, bf16[128,512]{1,0:T(8,128)(2,1)}, u32[]{:S(2)}) copy-start(bf16[128,512]{1,0:T(8,128)(2,1)} %param.6) | copy-start | bytes 393220
  67.6 11.6 %collective-permute-start.6 = (bf16[128,512]{0,1:T(8,128)(2,1)}, bf16[128,512]{0,1:T(8,128)(2,1)}, u32[]{:S(2)}, u32[]{:S(2)}) collective-permute-start(bf16[128,512]{0,1:T(8,128)(2,1)} %bitcast.28), channel_id=1, source_target_pairs={{1,0},{2,1},{3,2},{4,3},{5,4},{6,5},{7,6},{8,7},{9,8},{10,9},{11,1... | collective-permute-start | bytes 393224 | tf_op jit(solution)/shard_map/ppermute | solution.py:13
  70.8 11.7 %collective-permute-start.7 = (bf16[128,512]{0,1:T(8,128)(2,1)}, bf16[128,512]{0,1:T(8,128)(2,1)}, u32[]{:S(2)}, u32[]{:S(2)}) collective-permute-start(bf16[128,512]{0,1:T(8,128)(2,1)} %bitcast.30), channel_id=1, source_target_pairs={{2,0},{3,1},{4,2},{5,3},{6,4},{7,5},{8,6},{9,7},{10,8},{11,9},{12,... | collective-permute-start | bytes 393224 | tf_op jit(solution)/shard_map/ppermute | solution.py:13
  76.8 102.6 %reduce-scatter.3.cloned.1.call-start = ((), (), s32[]{:S(2)}) async-start(), calls=%async_computation.2 | async-start | bytes 294912 | tf_op jit(solution)/shard_map/reduce_scatter | solution.py:132
  77.2 7.0 %copy-start.6 = (bf16[4,640,128]{1,2,0:T(8,128)(2,1)S(1)}, bf16[4,640,128]{1,2,0:T(8,128)(2,1)}, u32[]{:S(2)}) copy-start(bf16[4,640,128]{1,2,0:T(8,128)(2,1)} %copy-done.5) | copy-start | bytes 1966084
  77.2 7.0 %copy-start.11 = (bf16[128,4,128]{2,0,1:T(8,128)(2,1)S(1)}, bf16[128,4,128]{2,0,1:T(8,128)(2,1)}, u32[]{:S(2)}) copy-start(bf16[128,4,128]{2,0,1:T(8,128)(2,1)} %copy.43) | copy-start | bytes 393220
  84.3 1.1 copy-start.8
  84.3 1.1 copy-start.12
Sparse Core Ops, SparseCore 0:
  76.9 61.9 reduce-scatter.4
  142.5 36.8 reduce-scatter.2
where the time goes:
time: 187 us; the launch traced here: 186 us
  waiting for transfers between devices  101 us (54%)
  starting transfers between devices  32.4 us (17%)
  local copies, waits for them, and re-layouts  18.5 us (10%)
  matrix products  16.2 us (9%)
  between operations  14.5 us (8%)
  other arithmetic  3.57 us (2%)
    reduce_scatter x2, waiting for transfers between devices, on_device(): lax.psum_scatter(summed, 'section', scatter_dimension=1, tiled=True)  92.2 us
    ppermute x10, starting transfers between devices, shifted(): return lax.ppermute(shard, axis, pairs)  32.3 us
    ppermute x10, waiting for transfers between devices, shifted(): return lax.ppermute(shard, axis, pairs)  8.82 us
    unnamed x50, local copies, waits for them, and re-layouts  7.43 us
    dot_general x3, matrix products, output_part(): jnp.einsum('grk,gkd->grd', probs_low, value_rows, preferred_element_type=...  4.21 us
  transfers between devices with their start and end apart: 12, of which 6 were waited for; matrix products, arithmetic and copies ran while one was open for 16% of the time, Pallas kernels for 0%

commit v1 on v0

v1 whole, which is shorter than its diff:
```python
import jax
import jax.numpy as jnp
from jax import lax
from jax.experimental import pallas as pl
from jax.experimental.pallas import tpu as pltpu
from jax.sharding import PartitionSpec as P

DH = 128
TOK = 128
GROUPS = 4
RATIO = 5
ROW = 4
ID_ROWS = 16
SCALE = DH ** (-0.5)
LOG2E = 1.4426950408889634
NEG = -1e30
AXES = ("section", "ctx")
NT = (((1,), (1,)), ((), ()))
TN = (((0,), (0,)), ((), ()))


def pairs(target):
    sections, cycle = lax.axis_size("section"), lax.axis_size("ctx")
    out = []
    for s in range(sections):
        for c in range(cycle):
            to = target(s, c)
            if 0 <= to[1] < cycle:
                out.append((s * cycle + c, to[0] * cycle + to[1]))
    return out


def shifted(x, by):
    sections = lax.axis_size("section")

    def target(s, c):
        mirror = (c // ROW) != ((c + by) // ROW)
        return ((sections // 2 - 1 - s // 2) * 2 + s % 2 if mirror else s, c + by)

    return lax.ppermute(x, AXES, pairs(target))


def other_core(x):
    return lax.ppermute(x, AXES, pairs(lambda s, c: (s ^ 1, c)))


def small_shift(x, by):
    return lax.ppermute(x, AXES, pairs(lambda s, c: (s, c + by)))


def attend(core_ref, ids_ref, q_ref, c_ref, k_ref, v_ref, hk_ref, hv_ref, ok_ref, ov_ref, id_ref, dq_ref, part_ref):
    group = pl.program_id(0)
    mine = core_ref[0] == group // 2
    ids = ids_ref[...].astype(jnp.float32)
    first = ids[:, 0:1]
    bound = 2 * TOK
    k_halo = jnp.where(mine, hk_ref[...], ok_ref[...])
    v_halo = jnp.where(mine, hv_ref[...], ov_ref[...])
    keys = jnp.concatenate([k_ref[...], k_halo[:TOK], k_halo[TOK:bound]], 0)
    values = jnp.concatenate([v_ref[...], v_halo[:TOK], v_halo[TOK:bound]], 0)
    row = lax.broadcasted_iota(jnp.int32, (TOK, TOK), 0)
    col = lax.broadcasted_iota(jnp.int32, (TOK, TOK), 1)
    wide = jnp.broadcast_to(ids, (TOK, TOK))
    own = jnp.where((wide.T == wide) & (row <= col), 0.0, NEG)
    biases = [own]
    rowf = row.astype(jnp.float32)
    for d in range(2):
        before = id_ref[d * ID_ROWS : d * ID_ROWS + 1, :].astype(jnp.float32)
        held = jnp.sum(jnp.where(before == first + 1.0, 1.0, 0.0), -1, keepdims=True)
        biases.append(jnp.where((wide == first) & (rowf >= TOK - held), 0.0, NEG))
    bias = jnp.concatenate(biases, 0)
    queries = jnp.concatenate([q_ref[:, h * DH : (h + 1) * DH] for h in range(RATIO)], 0)
    cots = jnp.concatenate([c_ref[:, h * DH : (h + 1) * DH] for h in range(RATIO)], 0)
    scores = lax.dot_general(keys, queries, NT, preferred_element_type=jnp.float32)
    grad_probs = lax.dot_general(values, cots, NT, preferred_element_type=jnp.float32)
    probs_low, scaled_low = [], []
    for h in range(RATIO):
        at = slice(h * TOK, (h + 1) * TOK)
        s = scores[:, at] * (SCALE * LOG2E) + bias
        e = jnp.exp2(s - jnp.max(s, 0, keepdims=True))
        p = e * (1.0 / jnp.sum(e, 0, keepdims=True))
        low = p.astype(jnp.bfloat16)
        g = grad_probs[:, at]
        dot = jnp.sum(low.astype(jnp.float32) * g, 0, keepdims=True)
        probs_low.append(low)
        scaled_low.append((p * (g - dot) * SCALE).astype(jnp.bfloat16))
    probs_low = jnp.concatenate(probs_low, 1)
    scaled_low = jnp.concatenate(scaled_low, 1)
    grad_v = jnp.dot(probs_low, cots, preferred_element_type=jnp.float32).astype(jnp.bfloat16)
    grad_k = jnp.dot(scaled_low, queries, preferred_element_type=jnp.float32).astype(jnp.bfloat16)
    grad_q = lax.dot_general(keys, scaled_low, TN, preferred_element_type=jnp.float32)
    for h in range(RATIO):
        at = slice(h * TOK, (h + 1) * TOK)
        dq_ref[:, at] = grad_q[:, at].T.astype(jnp.bfloat16)
    half = DH // 2
    part_ref[0] = jnp.concatenate([grad_k[:, :half], grad_v[:, :half]], 1)
    part_ref[1] = jnp.concatenate([grad_k[:, half:], grad_v[:, half:]], 1)


def on_device(queries, keys, values, cotangent, segment_ids):
    core = lax.axis_index("section") % 2
    groups = keys.shape[1] // DH
    width = keys.shape[1] // 2
    tok = keys.shape[0]
    ids = jnp.broadcast_to((segment_ids + 1).astype(jnp.bfloat16)[None], (ID_ROWS, tok))
    ids = jnp.pad(ids, ((0, 0), (0, 2 * width - tok)))
    mine = jnp.concatenate(
        [
            jnp.where(core == 0, keys[:, :width], keys[:, width:]),
            jnp.where(core == 0, values[:, :width], values[:, width:]),
        ],
        1,
    )
    sent = jnp.concatenate([mine, ids], 0)
    one, two = shifted(sent, 1), shifted(sent, 2)
    halo = jnp.concatenate([one[:tok], two[:tok]], 0)
    halo_ids = jnp.concatenate([one[tok:, :tok], two[tok:, :tok]], 0)
    other = other_core(halo)
    per = width // DH
    grad_q, part = pl.pallas_call(
        attend,
        grid=(groups,),
        out_shape=(
            jax.ShapeDtypeStruct((tok, queries.shape[2]), jnp.bfloat16),
            jax.ShapeDtypeStruct((2 * groups, 3 * tok, DH), jnp.bfloat16),
        ),
        in_specs=[
            pl.BlockSpec(memory_space=pltpu.SMEM),
            pl.BlockSpec((1, tok), lambda g: (0, 0)),
            pl.BlockSpec((tok, RATIO * DH), lambda g: (0, g)),
            pl.BlockSpec((tok, RATIO * DH), lambda g: (0, g)),
            pl.BlockSpec((tok, DH), lambda g: (0, g)),
            pl.BlockSpec((tok, DH), lambda g: (0, g)),
            pl.BlockSpec((2 * tok, DH), lambda g: (0, g % per)),
            pl.BlockSpec((2 * tok, DH), lambda g: (0, per + g % per)),
            pl.BlockSpec((2 * tok, DH), lambda g: (0, g % per)),
            pl.BlockSpec((2 * tok, DH), lambda g: (0, per + g % per)),
            pl.BlockSpec((2 * ID_ROWS, tok), lambda g: (0, 0)),
        ],
        out_specs=(
            pl.BlockSpec((tok, RATIO * DH), lambda g: (0, g)),
            pl.BlockSpec((2, 3 * tok, DH), lambda g: (g, 0, 0)),
        ),
        compiler_params=pltpu.CompilerParams(vmem_limit_bytes=40 * 1024 * 1024),
        name="attend",
    )(
        core.astype(jnp.int32).reshape(1),
        segment_ids.reshape(1, tok),
        queries[0],
        cotangent[0],
        keys,
        values,
        halo,
        halo,
        other,
        other,
        halo_ids,
    )
    shares = lax.all_to_all(part, "section", 0, 0)
    total = jnp.sum(shares.astype(jnp.float32), 0)
    back_one = small_shift(total[tok : 2 * tok].astype(jnp.bfloat16), -1)
    back_two = small_shift(total[2 * tok :].astype(jnp.bfloat16), -2)
    total = total[:tok] + back_one.astype(jnp.float32) + back_two.astype(jnp.float32)
    half = DH // 2
    return (grad_q[None], total[:, :half], total[:, half:])


def solution(mesh):
    placed = (
        P("section", "ctx", None),
        P("ctx", None),
        P("ctx", None),
        P("section", "ctx", None),
        P("ctx"),
    )
    return jax.shard_map(
        on_device,
        mesh=mesh,
        in_specs=placed,
        out_specs=(P("section", "ctx", None), P("ctx", "section"), P("ctx", "section")),
        check_vma=False,
    )
```

time: 187 us -> 74.7 us (0.40)
  the two profiles are of different devices: /device:TPU:2 before, /device:TPU:260 now
where the time goes in v1:
time: 74.7 us; the launch traced here: 74.5 us
  blocking collectives  26.1 us (35%)
  starting transfers between devices  25.6 us (34%)
  waiting for transfers between devices  12.5 us (17%)
  Pallas kernels  6.13 us (8%)
  other arithmetic  1.82 us (2%)
  local copies, waits for them, and re-layouts  1.55 us (2%)
  between operations  0.82 us (1%)
    all_to_all x1, blocking collectives, on_device(): shares = lax.all_to_all(part, 'section', 0, 0)  26.1 us
    ppermute x2, starting transfers between devices, small_shift(): return lax.ppermute(x, AXES, pairs(lambda s, c: (s, c + by)))  14.2 us
    ppermute x2, starting transfers between devices, shifted(): return lax.ppermute(x, AXES, pairs(target))  9.46 us
    ppermute x2, waiting for transfers between devices, small_shift(): return lax.ppermute(x, AXES, pairs(lambda s, c: (s, c + by)))  7.02 us
    pallas_call x1, Pallas kernels, on_device(): pl.pallas_call(attend, grid=(groups,), out_shape=(jax.ShapeDtypeStruct((t...  6.13 us
    ppermute x2, waiting for transfers between devices, shifted(): return lax.ppermute(x, AXES, pairs(target))  3.97 us
    ppermute x1, starting transfers between devices, other_core(): return lax.ppermute(x, AXES, pairs(lambda s, c: (s ^ 1, c)))  1.92 us
  transfers between devices with their start and end apart: 5, of which 4 were waited for; matrix products, arithmetic and copies ran while one was open for 0% of the time, Pallas kernels for 0%

profile of v1, /device:TPU:260, one launch (start us, length us, event | category | flops | bytes accessed | tf_op | source)
XLA Modules:
  0.0 74.5 jit_solution(5469250723231069143)
XLA Ops:
  0.6 0.7 add_convert_fusion
  1.3 0.0 copy-start.2
  1.3 0.0 copy-start.3
  1.3 1.0 %slice_select_fusion = (bf16[128,256]{1,0:T(8,128)(2,1)S(1)}, bf16[128,256]{1,0:T(8,128)(2,1)S(1)}) fusion(bf16[128,512]{1,0:T(8,128)(2,1)} %v_ref.1, pred[]{:T(512)S(6)} %eq.6, bf16[128,512]{1,0:T(8,128)(2,1)} %k_ref.1), kind=kLoop, calls=%fused_computation.5 | loop fusion | flops 65536 | bytes 393217 | tf_op jit(solution)/shard_map/jit(_where)/select_n | solution.py:110
  2.3 0.0 copy-start
  2.3 0.0 copy-start.1
  2.3 0.0 copy-start.4
  2.4 5.5 %collective-permute-start.1 = (bf16[144,512]{1,0:T(8,128)(2,1)S(1)}, bf16[144,512]{1,0:T(8,128)(2,1)S(1)}, u32[]{:S(2)}, u32[]{:S(2)}) collective-permute-start(bf16[144,512]{1,0:T(8,128)(2,1)S(1)} %pad_maximum_fusion.1), channel_id=1, source_target_pairs={{0,2},{1,3},{2,388},{3,389},{4,6},{5,7},{6,392},{7,393},{8,10},{9,... | collective-permute-start | bytes 442376 | tf_op jit(solution)/shard_map/ppermute | solution.py:40
  7.9 4.0 %collective-permute-start = (bf16[144,512]{1,0:T(8,128)(2,1)S(1)}, bf16[144,512]{1,0:T(8,128)(2,1)S(1)}, u32[]{:S(2)}, u32[]{:S(2)}) collective-permute-start(bf16[144,512]{1,0:T(8,128)(2,1)S(1)} %pad_maximum_fusion.1), channel_id=1, source_target_pairs={{0,1},{1,2},{2,3},{3,388},{4,5},{5,6},{6,7},{7,392},{8,9},{9,10},{... | collective-permute-start | bytes 442376 | tf_op jit(solution)/shard_map/ppermute | solution.py:40
  11.9 2.2 %collective-permute-done.1 = bf16[144,512]{1,0:T(8,128)(2,1)S(1)} collective-permute-done((bf16[144,512]{1,0:T(8,128)(2,1)S(1)}, bf16[144,512]{1,0:T(8,128)(2,1)S(1)}, u32[]{:S(2)}, u32[]{:S(2)}) %collective-permute-start.1) | collective-permute-done | bytes 147488 | tf_op jit(solution)/shard_map/ppermute | solution.py:40
  14.1 1.7 %collective-permute-done = bf16[144,512]{1,0:T(8,128)(2,1)S(1)} collective-permute-done((bf16[144,512]{1,0:T(8,128)(2,1)S(1)}, bf16[144,512]{1,0:T(8,128)(2,1)S(1)}, u32[]{:S(2)}, u32[]{:S(2)}) %collective-permute-start) | collective-permute-done | bytes 147488 | tf_op jit(solution)/shard_map/ppermute | solution.py:40
  15.9 1.9 %collective-permute-start.2 = (bf16[256,512]{1,0:T(8,128)(2,1)S(1)}, bf16[256,512]{1,0:T(8,128)(2,1)S(1)}, u32[]{:S(2)}, u32[]{:S(2)}) collective-permute-start(bf16[256,512]{1,0:T(8,128)(2,1)S(1)} %pad_maximum_fusion.hk_ref.hv_ref), channel_id=1, source_target_pairs={{0,64},{1,65},{2,66},{3,67},{4,68},{5,69},{6,70},{7,71},{8,72},{9,... | collective-permute-start | bytes 786440 | tf_op jit(solution)/shard_map/ppermute | solution.py:44
  17.9 1.5 %collective-permute-done.2.ok_ref.ov_ref = bf16[256,512]{1,0:T(8,128)(2,1)S(1)} collective-permute-done((bf16[256,512]{1,0:T(8,128)(2,1)S(1)}, bf16[256,512]{1,0:T(8,128)(2,1)S(1)}, u32[]{:S(2)}, u32[]{:S(2)}) %collective-permute-start.2) | collective-permute-done | bytes 262176 | tf_op jit(solution)/shard_map/ppermute | solution.py:44
  19.3 0.0 copy-done.2
  19.3 0.0 copy-done.3
  19.3 0.0 copy-done
  19.3 0.0 copy-done.1
  19.3 0.0 copy-done.4
  19.3 6.1 %attend.1 = (bf16[128,2560]{1,0:T(8,128)(2,1)}, bf16[8,384,128]{2,1,0:T(8,128)(2,1)S(1)}) custom-call(s32[1]{0:T(128)} %bitcast.core_ref, s32[1,128]{1,0:T(1,128)S(1)} %bitcast.7, bf16[128,2560]{1,0:T(8,128)(2,1)S(1)} %bitcast.5, bf16[128,2560]{1,0:T(8,128)(2,1)S(1)} %bitcast.6, bf16[128,512]{1,0:T(8,128)(2,1)S(1)} %copy-done.2, ...), custom_call_target="tpu_custom_call" | custom-call | tf_op jit(solution)/shard_map/attend/pallas_call | solution.py:120
  25.5 26.1 %all_to_all.5 = bf16[8,384,128]{2,1,0:T(8,128)(2,1)S(1)} all-to-all(bf16[8,384,128]{2,1,0:T(8,128)(2,1)S(1)} %get-tuple-element.6), channel_id=1, replica_groups=mesh['section'=8,'ctx'=64] {'section'}, dimensions={0} | all-to-all | bytes 1572864 | tf_op jit(solution)/shard_map/all_to_all | solution.py:159
  51.6 0.1 convert_reduce_fusion
  51.7 9.1 %collective-permute-start.3 = (bf16[128,128]{1,0:T(8,128)(2,1)S(1)}, bf16[128,128]{1,0:T(8,128)(2,1)S(1)}, u32[]{:S(2)}, u32[]{:S(2)}) collective-permute-start(bf16[128,128]{1,0:T(8,128)(2,1)S(1)} %get-tuple-element.10), channel_id=1, source_target_pairs={{1,0},{2,1},{3,2},{4,3},{5,4},{6,5},{7,6},{8,7},{9,8},{10,9},{11,1... | collective-permute-start | bytes 98312 | tf_op jit(solution)/shard_map/ppermute | solution.py:48
  60.8 5.1 %collective-permute-start.4 = (bf16[128,128]{1,0:T(8,128)(2,1)S(1)}, bf16[128,128]{1,0:T(8,128)(2,1)S(1)}, u32[]{:S(2)}, u32[]{:S(2)}) collective-permute-start(bf16[128,128]{1,0:T(8,128)(2,1)S(1)} %get-tuple-element.11), channel_id=1, source_target_pairs={{2,0},{3,1},{4,2},{5,3},{6,4},{7,5},{8,6},{9,7},{10,8},{11,9},{12,... | collective-permute-start | bytes 98312 | tf_op jit(solution)/shard_map/ppermute | solution.py:48
  65.9 0.0 collective-permute-done.3
  65.9 7.0 %collective-permute-done.4 = bf16[128,128]{1,0:T(8,128)(2,1)S(1)} collective-permute-done((bf16[128,128]{1,0:T(8,128)(2,1)S(1)}, bf16[128,128]{1,0:T(8,128)(2,1)S(1)}, u32[]{:S(2)}, u32[]{:S(2)}) %collective-permute-start.4) | collective-permute-done | bytes 32800 | tf_op jit(solution)/shard_map/ppermute | solution.py:48
  73.0 0.1 fusion.2
  73.1 0.7 copy.9
  73.8 0.7 copy.8
  (12 shorter events, 0.1 us)
Async XLA Ops:
  1.3 18.0 %copy-start.2 = (bf16[128,512]{1,0:T(8,128)(2,1)S(1)}, bf16[128,512]{1,0:T(8,128)(2,1)}, u32[]{:S(2)}) copy-start(bf16[128,512]{1,0:T(8,128)(2,1)} %k_ref.1) | copy-start | bytes 393220
  1.3 18.0 %copy-start.3 = (bf16[128,512]{1,0:T(8,128)(2,1)S(1)}, bf16[128,512]{1,0:T(8,128)(2,1)}, u32[]{:S(2)}) copy-start(bf16[128,512]{1,0:T(8,128)(2,1)} %v_ref.1) | copy-start | bytes 393220
  2.3 17.0 %copy-start = (bf16[1,128,2560]{2,1,0:T(8,128)(2,1)S(1)}, bf16[1,128,2560]{2,1,0:T(8,128)(2,1)}, u32[]{:S(2)}) copy-start(bf16[1,128,2560]{2,1,0:T(8,128)(2,1)} %param.5) | copy-start | bytes 1966084
  2.3 17.0 %copy-start.1 = (bf16[1,128,2560]{2,1,0:T(8,128)(2,1)S(1)}, bf16[1,128,2560]{2,1,0:T(8,128)(2,1)}, u32[]{:S(2)}) copy-start(bf16[1,128,2560]{2,1,0:T(8,128)(2,1)} %param.8) | copy-start | bytes 1966084
  2.3 17.0 %copy-start.4 = (s32[128]{0:T(128)S(1)}, s32[128]{0:T(128)}, u32[]{:S(2)}) copy-start(s32[128]{0:T(128)} %param.9) | copy-start | bytes 1540
  2.4 11.7 %collective-permute-start.1 = (bf16[144,512]{1,0:T(8,128)(2,1)S(1)}, bf16[144,512]{1,0:T(8,128)(2,1)S(1)}, u32[]{:S(2)}, u32[]{:S(2)}) collective-permute-start(bf16[144,512]{1,0:T(8,128)(2,1)S(1)} %pad_maximum_fusion.1), channel_id=1, source_target_pairs={{0,2},{1,3},{2,388},{3,389},{4,6},{5,7},{6,392},{7,393},{8,10},{9,... | collective-permute-start | bytes 442376 | tf_op jit(solution)/shard_map/ppermute | solution.py:40
  7.9 8.0 %collective-permute-start = (bf16[144,512]{1,0:T(8,128)(2,1)S(1)}, bf16[144,512]{1,0:T(8,128)(2,1)S(1)}, u32[]{:S(2)}, u32[]{:S(2)}) collective-permute-start(bf16[144,512]{1,0:T(8,128)(2,1)S(1)} %pad_maximum_fusion.1), channel_id=1, source_target_pairs={{0,1},{1,2},{2,3},{3,388},{4,5},{5,6},{6,7},{7,392},{8,9},{9,10},{... | collective-permute-start | bytes 442376 | tf_op jit(solution)/shard_map/ppermute | solution.py:40
  15.9 3.4 %collective-permute-start.2 = (bf16[256,512]{1,0:T(8,128)(2,1)S(1)}, bf16[256,512]{1,0:T(8,128)(2,1)S(1)}, u32[]{:S(2)}, u32[]{:S(2)}) collective-permute-start(bf16[256,512]{1,0:T(8,128)(2,1)S(1)} %pad_maximum_fusion.hk_ref.hv_ref), channel_id=1, source_target_pairs={{0,64},{1,65},{2,66},{3,67},{4,68},{5,69},{6,70},{7,71},{8,72},{9,... | collective-permute-start | bytes 786440 | tf_op jit(solution)/shard_map/ppermute | solution.py:44
  51.7 14.2 %collective-permute-start.3 = (bf16[128,128]{1,0:T(8,128)(2,1)S(1)}, bf16[128,128]{1,0:T(8,128)(2,1)S(1)}, u32[]{:S(2)}, u32[]{:S(2)}) collective-permute-start(bf16[128,128]{1,0:T(8,128)(2,1)S(1)} %get-tuple-element.10), channel_id=1, source_target_pairs={{1,0},{2,1},{3,2},{4,3},{5,4},{6,5},{7,6},{8,7},{9,8},{10,9},{11,1... | collective-permute-start | bytes 98312 | tf_op jit(solution)/shard_map/ppermute | solution.py:48
  60.8 12.1 %collective-permute-start.4 = (bf16[128,128]{1,0:T(8,128)(2,1)S(1)}, bf16[128,128]{1,0:T(8,128)(2,1)S(1)}, u32[]{:S(2)}, u32[]{:S(2)}) collective-permute-start(bf16[128,128]{1,0:T(8,128)(2,1)S(1)} %get-tuple-element.11), channel_id=1, source_target_pairs={{2,0},{3,1},{4,2},{5,3},{6,4},{7,5},{8,6},{9,7},{10,8},{11,9},{12,... | collective-permute-start | bytes 98312 | tf_op jit(solution)/shard_map/ppermute | solution.py:48

commit v2 on v1

v2 whole, which is shorter than its diff:
```python
import jax
import jax.numpy as jnp
from jax import lax
from jax.experimental import pallas as pl
from jax.experimental.pallas import tpu as pltpu
from jax.sharding import PartitionSpec as P

DH = 128
TOK = 128
RATIO = 5
WIDE = RATIO * DH
ROW = 4
ID_ROWS = 16
SCALE = DH ** (-0.5)
LOG2E = 1.4426950408889634
NEG = -1e30
AXES = ("section", "ctx")
NT = (((1,), (1,)), ((), ()))
TN = (((0,), (0,)), ((), ()))


def permuted(x, target):
    sections, cycle = lax.axis_size("section"), lax.axis_size("ctx")
    found = []
    for s in range(sections):
        for c in range(cycle):
            to = target(s, c)
            if 0 <= to[1] < cycle:
                found.append((s * cycle + c, to[0] * cycle + to[1]))
    return lax.ppermute(x, AXES, found)


def shifted(x, by):
    def target(s, c):
        leaves = (c // ROW) != ((c + by) // ROW)
        return ((3 - s // 2) * 2 + s % 2 if leaves else s, c + by)

    return permuted(x, target)


def other_core(x):
    return permuted(x, lambda s, c: (s ^ 1, c))


def group_of(core, slot):
    return core + slot * (3 - 2 * core)


def to_owner(x, step):
    def target(s, c):
        share = (s // 2) ^ step
        return (group_of(s % 2, share // 2) * 2 + share % 2, c)

    return permuted(x, target)


def attend(
    place_ref, ids_ref, q_ref, c_ref, oq_ref, oc_ref, k_ref, v_ref, k1_ref, v1_ref, k2_ref, v2_ref,
    id1_ref, id2_ref, dq_ref, odq_ref, part_ref,
):
    slot = pl.program_id(0)
    ids = ids_ref[...].astype(jnp.float32)
    first = ids[:, 0:1]
    keys = jnp.concatenate([k_ref[...], k1_ref[...], k2_ref[...]], 0)
    values = jnp.concatenate([v_ref[...], v1_ref[...], v2_ref[...]], 0)
    row = lax.broadcasted_iota(jnp.int32, (TOK, TOK), 0)
    col = lax.broadcasted_iota(jnp.int32, (TOK, TOK), 1)
    wide = jnp.broadcast_to(ids, (TOK, TOK))
    biases = [jnp.where((wide.T == wide) & (row <= col), 0.0, NEG)]
    for id_ref in (id1_ref, id2_ref):
        before = id_ref[0:1, :].astype(jnp.float32)
        held = jnp.sum(jnp.where(before == first + 1.0, 1.0, 0.0), -1, keepdims=True)
        biases.append(jnp.where((wide == first) & (row.astype(jnp.float32) >= TOK - held), 0.0, NEG))
    bias = jnp.concatenate(biases, 0)
    grad_k = jnp.zeros((3 * TOK, DH), jnp.float32)
    grad_v = jnp.zeros((3 * TOK, DH), jnp.float32)
    for layer_q, layer_c, out in ((q_ref, c_ref, dq_ref), (oq_ref, oc_ref, odq_ref)):
        queries = jnp.concatenate([layer_q[:, h * DH : (h + 1) * DH] for h in range(RATIO)], 0)
        cots = jnp.concatenate([layer_c[:, h * DH : (h + 1) * DH] for h in range(RATIO)], 0)
        scores = lax.dot_general(keys, queries, NT, preferred_element_type=jnp.float32)
        grad_probs = lax.dot_general(values, cots, NT, preferred_element_type=jnp.float32)
        probs_low, scaled_low = [], []
        for h in range(RATIO):
            at = slice(h * TOK, (h + 1) * TOK)
            s = scores[:, at] * (SCALE * LOG2E) + bias
            e = jnp.exp2(s - jnp.max(s, 0, keepdims=True))
            p = e * (1.0 / jnp.sum(e, 0, keepdims=True))
            low = p.astype(jnp.bfloat16)
            g = grad_probs[:, at]
            dot = jnp.sum(low.astype(jnp.float32) * g, 0, keepdims=True)
            probs_low.append(low)
            scaled_low.append((p * (g - dot) * SCALE).astype(jnp.bfloat16))
        probs_low = jnp.concatenate(probs_low, 1)
        scaled_low = jnp.concatenate(scaled_low, 1)
        grad_v += jnp.dot(probs_low, cots, preferred_element_type=jnp.float32)
        grad_k += jnp.dot(scaled_low, queries, preferred_element_type=jnp.float32)
        grad_q = lax.dot_general(keys, scaled_low, TN, preferred_element_type=jnp.float32)
        for h in range(RATIO):
            at = slice(h * TOK, (h + 1) * TOK)
            out[:, at] = grad_q[:, at].T.astype(jnp.bfloat16)
    half = DH // 2
    grad_k = grad_k.astype(jnp.bfloat16)
    grad_v = grad_v.astype(jnp.bfloat16)
    shares = (
        jnp.concatenate([grad_k[:, :half], grad_v[:, :half]], 1),
        jnp.concatenate([grad_k[:, half:], grad_v[:, half:]], 1),
    )
    for block in range(3):
        mirror = place_ref[2 + block]
        rows = slice(block * TOK, (block + 1) * TOK)
        for side in range(2):
            share = 2 * (slot ^ mirror) + side
            part_ref[share ^ place_ref[1], rows, :] = shares[side][rows]


def finish(own_ref, one_ref, two_ref, dk_ref, dv_ref):
    total = own_ref[...] + one_ref[...].astype(jnp.float32) + two_ref[...].astype(jnp.float32)
    total = total.T
    dk_ref[...] = total[: DH // 2]
    dv_ref[...] = total[DH // 2 :]


def on_device(queries, keys, values, cotangent, segment_ids):
    section, me = lax.axis_index("section"), lax.axis_index("ctx")
    core, y_lo = section % 2, section // 2
    tok = keys.shape[0]
    q, c = queries[0], cotangent[0]

    def of_core(x, unit, which):
        outer = jnp.concatenate([x[:, :unit], x[:, 3 * unit :]], 1)
        return jnp.where(which == 0, outer, x[:, unit : 3 * unit])

    ids = jnp.broadcast_to((segment_ids + 1).astype(jnp.bfloat16)[None], (ID_ROWS, tok))
    ids = jnp.pad(ids, ((0, 0), (0, 4 * DH - tok)))
    sent = jnp.concatenate([of_core(keys, DH, core), of_core(values, DH, core)], 1)
    sent = jnp.concatenate([sent, ids], 0)
    one, two = shifted(sent, 1), shifted(sent, 2)
    q, c, _ = lax.optimization_barrier((q, c, sent))
    swapped = other_core(jnp.concatenate([of_core(q, WIDE, 1 - core), of_core(c, WIDE, 1 - core)], 0))
    place = jnp.stack(
        [core, y_lo, jnp.zeros_like(core), (me % ROW < 1).astype(core.dtype), (me % ROW < 2).astype(core.dtype)]
    ).astype(jnp.int32)

    def own(g, at):
        return (0, group_of(at[0], g))

    def halo(row, lane):
        return lambda g, at: (row, lane + g)

    grad_q, other_q, part = pl.pallas_call(
        attend,
        grid_spec=pltpu.PrefetchScalarGridSpec(
            num_scalar_prefetch=1,
            grid=(2,),
            in_specs=[
                pl.BlockSpec((1, tok), lambda g, at: (0, 0)),
                pl.BlockSpec((tok, WIDE), own),
                pl.BlockSpec((tok, WIDE), own),
                pl.BlockSpec((tok, WIDE), halo(0, 0)),
                pl.BlockSpec((tok, WIDE), halo(1, 0)),
                pl.BlockSpec((tok, DH), own),
                pl.BlockSpec((tok, DH), own),
                pl.BlockSpec((tok, DH), halo(0, 0)),
                pl.BlockSpec((tok, DH), halo(0, 2)),
                pl.BlockSpec((tok, DH), halo(0, 0)),
                pl.BlockSpec((tok, DH), halo(0, 2)),
                pl.BlockSpec((ID_ROWS, tok), lambda g, at: (tok // ID_ROWS, 0)),
                pl.BlockSpec((ID_ROWS, tok), lambda g, at: (tok // ID_ROWS, 0)),
            ],
            out_specs=(
                pl.BlockSpec((tok, WIDE), own),
                pl.BlockSpec((tok, WIDE), halo(0, 0)),
                pl.BlockSpec((4, 3 * tok, DH), lambda g, at: (0, 0, 0)),
            ),
        ),
        out_shape=(
            jax.ShapeDtypeStruct(q.shape, jnp.bfloat16),
            jax.ShapeDtypeStruct((tok, 2 * WIDE), jnp.bfloat16),
            jax.ShapeDtypeStruct((4, 3 * tok, DH), jnp.bfloat16),
        ),
        compiler_params=pltpu.CompilerParams(vmem_limit_bytes=24 * 1024 * 1024),
        name="attend",
    )(place, segment_ids.reshape(1, tok), q, c, swapped, swapped, keys, values, one, one, two, two, one, two)
    total = sum(to_owner(part[step], step).astype(jnp.float32) for step in range(4))
    back_one = shifted(total[tok : 2 * tok].astype(jnp.bfloat16), -1)
    back_two = shifted(total[2 * tok :].astype(jnp.bfloat16), -2)
    back_q = other_core(other_q)
    outer = jnp.concatenate([back_q[:, :WIDE], grad_q[:, WIDE : 3 * WIDE], back_q[:, WIDE:]], 1)
    inner = jnp.concatenate([grad_q[:, :WIDE], back_q, grad_q[:, 3 * WIDE :]], 1)
    grad_q = jnp.where(core == 0, inner, outer)
    grad_k, grad_v = pl.pallas_call(
        finish,
        out_shape=(jax.ShapeDtypeStruct((DH // 2, tok), jnp.float32),) * 2,
        name="finish",
    )(total[:tok], back_one, back_two)
    return (grad_q[None], grad_k.T, grad_v.T)


def solution(mesh):
    placed = (
        P("section", "ctx", None),
        P("ctx", None),
        P("ctx", None),
        P("section", "ctx", None),
        P("ctx"),
    )
    return jax.shard_map(
        on_device,
        mesh=mesh,
        in_specs=placed,
        out_specs=(P("section", "ctx", None), P("ctx", "section"), P("ctx", "section")),
        check_vma=False,
    )
```

time: 74.7 us -> 69.3 us (0.928)
  the two profiles are of different devices: /device:TPU:260 before, /device:TPU:244 now
where the time goes in v2:
time: 69.3 us; the launch traced here: 68.8 us
  starting transfers between devices  35.8 us (52%)
  waiting for transfers between devices  18.8 us (27%)
  Pallas kernels  7.15 us (10%)
  local copies, waits for them, and re-layouts  3.25 us (5%)
  other arithmetic  2.92 us (4%)
  between operations  0.92 us (1%)
    ppermute x10, starting transfers between devices, permuted(): return lax.ppermute(x, AXES, found)  35.8 us
    ppermute x10, waiting for transfers between devices, permuted(): return lax.ppermute(x, AXES, found)  18.8 us
    pallas_call x1, Pallas kernels, on_device(): pl.pallas_call(attend, grid_spec=pltpu.PrefetchScalarGridSpec(num_scalar_...  5.57 us
    slice x4, local copies, waits for them, and re-layouts, of_core(): outer = jnp.concatenate([x[:, :unit], x[:, 3 * unit:]], 1)  1.68 us
    pallas_call x1, Pallas kernels, on_device(): pl.pallas_call(finish, out_shape=(jax.ShapeDtypeStruct((DH // 2, tok), jn...  1.58 us
  transfers between devices with their start and end apart: 10, of which 4 were waited for; matrix products, arithmetic and copies ran while one was open for 1% of the time, Pallas kernels for 2%

profile of v2, /device:TPU:244, one launch (start us, length us, event | category | flops | bytes accessed | tf_op | source)
XLA Modules:
  0.0 68.8 jit_solution(5528654824898725121)
XLA Ops:
  0.6 0.0 copy-start
  0.7 0.8 %fusion.3 = (bf16[128,128]{1,0:T(8,128)(2,1)S(1)}, bf16[128,128]{1,0:T(8,128)(2,1)S(1)}) fusion(bf16[128,512]{1,0:T(8,128)(2,1)} %k_ref.1), kind=kLoop, calls=%fused_computation.21 | loop fusion | bytes 131072 | tf_op jit(solution)/shard_map/slice | solution.py:130
  1.5 0.8 %fusion.4 = (bf16[128,128]{1,0:T(8,128)(2,1)S(1)}, bf16[128,128]{1,0:T(8,128)(2,1)S(1)}) fusion(bf16[128,512]{1,0:T(8,128)(2,1)} %v_ref.1), kind=kLoop, calls=%fused_computation.22 | loop fusion | bytes 131072 | tf_op jit(solution)/shard_map/slice | solution.py:130
  2.3 0.7 add_convert_fusion
  2.9 0.0 copy-start.1
  3.0 1.0 %maximum_select_fusion.3 = (bf16[128,256]{1,0:T(8,128)(2,1)S(1)}, bf16[128,256]{1,0:T(8,128)(2,1)S(1)}) fusion(bf16[128,128]{1,0:T(8,128)(2,1)S(1)} %get-tuple-element.32, bf16[128,128]{1,0:T(8,128)(2,1)S(1)} %get-tuple-element.31, bf16[128,512]{1,0:T(8,128)(2,1)} %k_ref.1, pred[]{:T(512)S(6)} %eq.13, bf16[128,512]{1,0:T(8,128)(2,1)} %v_ref.1, ...), kind=kLoop, calls=%fused_computation.15 | loop fusion | flops 327680 | bytes 393217 | tf_op jit(solution)/shard_map/jit(_where)/select_n | solution.py:131
  4.0 0.0 copy-done
  4.0 0.1 copy-done.1
  4.1 0.1 maximum_select_fusion.1
  4.2 0.1 maximum_select_fusion.2
  4.3 0.0 copy-start.2
  4.3 0.0 copy-start.3
  4.3 0.0 copy-start.4
  4.4 2.1 %collective-permute-start = (bf16[256,1280]{1,0:T(8,128)(2,1)S(1)}, bf16[256,1280]{1,0:T(8,128)(2,1)S(1)}, u32[]{:S(2)}, u32[]{:S(2)}) collective-permute-start(bf16[256,1280]{1,0:T(8,128)(2,1)S(1)} %pad_maximum_fusion), channel_id=1, source_target_pairs={{0,64},{1,65},{2,66},{3,67},{4,68},{5,69},{6,70},{7,71},{8,72},{9,... | collective-permute-start | bytes 1966088 | tf_op jit(solution)/shard_map/ppermute | solution.py:30
  6.5 3.1 %collective-permute-start.1 = (bf16[144,512]{1,0:T(8,128)(2,1)S(1)}, bf16[144,512]{1,0:T(8,128)(2,1)S(1)}, u32[]{:S(2)}, u32[]{:S(2)}) collective-permute-start(bf16[144,512]{1,0:T(8,128)(2,1)S(1)} %pad_maximum_fusion.1), channel_id=1, source_target_pairs={{0,1},{1,2},{2,3},{3,388},{4,5},{5,6},{6,7},{7,392},{8,9},{9,10},{... | collective-permute-start | bytes 442376 | tf_op jit(solution)/shard_map/ppermute | solution.py:30
  9.6 6.1 %collective-permute-start.2 = (bf16[144,512]{1,0:T(8,128)(2,1)S(1)}, bf16[144,512]{1,0:T(8,128)(2,1)S(1)}, u32[]{:S(2)}, u32[]{:S(2)}) collective-permute-start(bf16[144,512]{1,0:T(8,128)(2,1)S(1)} %pad_maximum_fusion.1), channel_id=1, source_target_pairs={{0,2},{1,3},{2,388},{3,389},{4,6},{5,7},{6,392},{7,393},{8,10},{9,... | collective-permute-start | bytes 442376 | tf_op jit(solution)/shard_map/ppermute | solution.py:30
  15.7 0.1 stack.27.place_ref
  15.8 0.0 collective-permute-done.1.k1_ref.v1_ref.id1_ref
  15.8 3.4 %collective-permute-done.2.k2_ref.v2_ref.id2_ref = bf16[144,512]{1,0:T(8,128)(2,1)S(1)} collective-permute-done((bf16[144,512]{1,0:T(8,128)(2,1)S(1)}, bf16[144,512]{1,0:T(8,128)(2,1)S(1)}, u32[]{:S(2)}, u32[]{:S(2)}) %collective-permute-start.2) | collective-permute-done | bytes 147488 | tf_op jit(solution)/shard_map/ppermute | solution.py:30
  19.1 0.0 collective-permute-done.oq_ref.oc_ref
  19.2 0.0 copy-done.2
  19.2 0.0 copy-done.3
  19.2 0.0 copy-done.4
  19.2 5.6 %attend.1 = (bf16[128,2560]{1,0:T(8,128)(2,1)S(1)}, bf16[128,1280]{1,0:T(8,128)(2,1)S(1)}, bf16[4,384,128]{2,1,0:T(8,128)(2,1)S(1)}) custom-call(s32[5]{0:T(128)S(1)} %stack.27.place_ref, s32[1,128]{1,0:T(1,128)S(1)} %bitcast.34, bf16[128,2560]{1,0:T(8,128)(2,1)S(1)} %bitcast.30, bf16[128,2560]{1,0:T(8,128)(2,1)S(1)} %bitcast.33, ...), custom_call_target="tpu_custom_call" | custom-call | tf_op jit(solution)/shard_map/attend/pallas_call | solution.py:150
  24.8 4.6 %collective-permute-start.4 = (bf16[384,128]{1,0:T(8,128)(2,1)S(1)}, bf16[384,128]{1,0:T(8,128)(2,1)S(1)}, u32[]{:S(2)}, u32[]{:S(2)}) collective-permute-start(bf16[384,128]{1,0:T(8,128)(2,1)S(1)} %get-tuple-element.25), channel_id=1, source_target_pairs={{0,0},{1,1},{2,2},{3,3},{4,4},{5,5},{6,6},{7,7},{8,8},{9,9},{10,10... | collective-permute-start | bytes 294920 | tf_op jit(solution)/shard_map/ppermute | solution.py:30
  29.4 1.9 %collective-permute-start.5 = (bf16[384,128]{1,0:T(8,128)(2,1)S(1)}, bf16[384,128]{1,0:T(8,128)(2,1)S(1)}, u32[]{:S(2)}, u32[]{:S(2)}) collective-permute-start(bf16[384,128]{1,0:T(8,128)(2,1)S(1)} %get-tuple-element.28), channel_id=1, source_target_pairs={{0,64},{1,65},{2,66},{3,67},{4,68},{5,69},{6,70},{7,71},{8,72},{9,... | collective-permute-start | bytes 294920 | tf_op jit(solution)/shard_map/ppermute | solution.py:30
  31.3 3.4 %collective-permute-start.6 = (bf16[384,128]{1,0:T(8,128)(2,1)S(1)}, bf16[384,128]{1,0:T(8,128)(2,1)S(1)}, u32[]{:S(2)}, u32[]{:S(2)}) collective-permute-start(bf16[384,128]{1,0:T(8,128)(2,1)S(1)} %get-tuple-element.27), channel_id=1, source_target_pairs={{0,384},{1,385},{2,386},{3,387},{4,388},{5,389},{6,390},{7,391},{8... | collective-permute-start | bytes 294920 | tf_op jit(solution)/shard_map/ppermute | solution.py:30
  34.7 3.0 %collective-permute-start.7 = (bf16[384,128]{1,0:T(8,128)(2,1)S(1)}, bf16[384,128]{1,0:T(8,128)(2,1)S(1)}, u32[]{:S(2)}, u32[]{:S(2)}) collective-permute-start(bf16[384,128]{1,0:T(8,128)(2,1)S(1)} %get-tuple-element.26), channel_id=1, source_target_pairs={{0,448},{1,449},{2,450},{3,451},{4,452},{5,453},{6,454},{7,455},{8... | collective-permute-start | bytes 294920 | tf_op jit(solution)/shard_map/ppermute | solution.py:30
  37.8 1.9 %collective-permute-start.3 = (bf16[128,1280]{1,0:T(8,128)(2,1)S(1)}, bf16[128,1280]{1,0:T(8,128)(2,1)S(1)}, u32[]{:S(2)}, u32[]{:S(2)}) collective-permute-start(bf16[128,1280]{1,0:T(8,128)(2,1)S(1)} %get-tuple-element.13), channel_id=1, source_target_pairs={{0,64},{1,65},{2,66},{3,67},{4,68},{5,69},{6,70},{7,71},{8,72},{9,... | collective-permute-start | bytes 983048 | tf_op jit(solution)/shard_map/ppermute | solution.py:30
  39.7 0.0 collective-permute-done.4
  39.8 0.0 collective-permute-done.5
  39.8 2.3 %collective-permute-done.6 = bf16[384,128]{1,0:T(8,128)(2,1)S(1)} collective-permute-done((bf16[384,128]{1,0:T(8,128)(2,1)S(1)}, bf16[384,128]{1,0:T(8,128)(2,1)S(1)}, u32[]{:S(2)}, u32[]{:S(2)}) %collective-permute-start.6) | collective-permute-done | bytes 98336 | tf_op jit(solution)/shard_map/ppermute | solution.py:30
  42.0 2.5 %collective-permute-done.7 = bf16[384,128]{1,0:T(8,128)(2,1)S(1)} collective-permute-done((bf16[384,128]{1,0:T(8,128)(2,1)S(1)}, bf16[384,128]{1,0:T(8,128)(2,1)S(1)}, u32[]{:S(2)}, u32[]{:S(2)}) %collective-permute-start.7) | collective-permute-done | bytes 98336 | tf_op jit(solution)/shard_map/ppermute | solution.py:30
  44.5 0.1 fusion
  44.6 7.6 %collective-permute-start.8 = (bf16[128,128]{1,0:T(8,128)(2,1)S(1)}, bf16[128,128]{1,0:T(8,128)(2,1)S(1)}, u32[]{:S(2)}, u32[]{:S(2)}) collective-permute-start(bf16[128,128]{1,0:T(8,128)(2,1)S(1)} %get-tuple-element.36), channel_id=1, source_target_pairs={{1,0},{2,1},{3,2},{4,387},{5,4},{6,5},{7,6},{8,391},{9,8},{10,9},{... | collective-permute-start | bytes 98312 | tf_op jit(solution)/shard_map/ppermute | solution.py:30
  52.3 2.1 %collective-permute-start.9 = (bf16[128,128]{1,0:T(8,128)(2,1)S(1)}, bf16[128,128]{1,0:T(8,128)(2,1)S(1)}, u32[]{:S(2)}, u32[]{:S(2)}) collective-permute-start(bf16[128,128]{1,0:T(8,128)(2,1)S(1)} %get-tuple-element.35), channel_id=1, source_target_pairs={{2,0},{3,1},{4,386},{5,387},{6,4},{7,5},{8,390},{9,391},{10,8},{11... | collective-permute-start | bytes 98312 | tf_op jit(solution)/shard_map/ppermute | solution.py:30
  54.4 0.6 slice.100.own_ref
  55.0 0.0 collective-permute-done.8.one_ref
  55.0 0.0 copy-start.5
  55.0 10.6 %collective-permute-done.9.two_ref = bf16[128,128]{1,0:T(8,128)(2,1)S(1)} collective-permute-done((bf16[128,128]{1,0:T(8,128)(2,1)S(1)}, bf16[128,128]{1,0:T(8,128)(2,1)S(1)}, u32[]{:S(2)}, u32[]{:S(2)}) %collective-permute-start.9) | collective-permute-done | bytes 32800 | tf_op jit(solution)/shard_map/ppermute | solution.py:30
  65.6 0.0 copy-done.5
  65.6 0.0 copy-start.6
  65.6 0.6 copy-done.6
  66.2 1.6 %finish.1 = (f32[64,128]{1,0:T(8,128)}, f32[64,128]{1,0:T(8,128)}) custom-call(f32[128,128]{1,0:T(8,128)} %slice.100.own_ref, bf16[128,128]{1,0:T(8,128)(2,1)} %copy-done.5, bf16[128,128]{1,0:T(8,128)(2,1)} %copy-done.6), custom_call_target="tpu_custom_call" | custom-call | tf_op jit(solution)/shard_map/finish/pallas_call | solution.py:191
  67.8 0.0 collective-permute-done.3
  67.8 1.0 %maximum_select_fusion = bf16[1,128,2560]{2,1,0:T(8,128)(2,1)} fusion(bf16[1,128,640]{2,1,0:T(8,128)(2,1)S(1)} %get-tuple-element.20, bf16[1,128,1280]{2,1,0:T(8,128)(2,1)S(1)} %bitcast.35, bf16[1,128,640]{2,1,0:T(8,128)(2,1)S(1)} %get-tuple-element.19, bf16[1,128,640]{2,1,0:T(8,128)(2,1)S(1)} %get-tuple-element.30, ...), kind=kLoop, calls=%fused_computation.1 | loop fusion | flops 4259840 | bytes 1966081 | tf_op jit(solution)/shard_map/jit(_where)/select_n | solution.py:190
  (11 shorter events, 0.2 us)
Async XLA Ops:
  0.6 3.3 %copy-start = (bf16[1,128,2560]{2,1,0:T(8,128)(2,1)S(1)}, bf16[1,128,2560]{2,1,0:T(8,128)(2,1)}, u32[]{:S(2)}) copy-start(bf16[1,128,2560]{2,1,0:T(8,128)(2,1)} %param.5) | copy-start | bytes 1966084
  2.9 1.1 %copy-start.1 = (bf16[1,128,2560]{2,1,0:T(8,128)(2,1)S(1)}, bf16[1,128,2560]{2,1,0:T(8,128)(2,1)}, u32[]{:S(2)}) copy-start(bf16[1,128,2560]{2,1,0:T(8,128)(2,1)} %param.8) | copy-start | bytes 1966084
  4.3 14.8 %copy-start.2 = (bf16[128,512]{1,0:T(8,128)(2,1)S(1)}, bf16[128,512]{1,0:T(8,128)(2,1)}, u32[]{:S(2)}) copy-start(bf16[128,512]{1,0:T(8,128)(2,1)} %k_ref.1) | copy-start | bytes 393220
  4.3 14.8 %copy-start.3 = (bf16[128,512]{1,0:T(8,128)(2,1)S(1)}, bf16[128,512]{1,0:T(8,128)(2,1)}, u32[]{:S(2)}) copy-start(bf16[128,512]{1,0:T(8,128)(2,1)} %v_ref.1) | copy-start | bytes 393220
  4.3 14.8 %copy-start.4 = (s32[128]{0:T(128)S(1)}, s32[128]{0:T(128)}, u32[]{:S(2)}) copy-start(s32[128]{0:T(128)} %param.9) | copy-start | bytes 1540
  4.4 14.8 %collective-permute-start = (bf16[256,1280]{1,0:T(8,128)(2,1)S(1)}, bf16[256,1280]{1,0:T(8,128)(2,1)S(1)}, u32[]{:S(2)}, u32[]{:S(2)}) collective-permute-start(bf16[256,1280]{1,0:T(8,128)(2,1)S(1)} %pad_maximum_fusion), channel_id=1, source_target_pairs={{0,64},{1,65},{2,66},{3,67},{4,68},{5,69},{6,70},{7,71},{8,72},{9,... | collective-permute-start | bytes 1966088 | tf_op jit(solution)/shard_map/ppermute | solution.py:30
  6.5 9.3 %collective-permute-start.1 = (bf16[144,512]{1,0:T(8,128)(2,1)S(1)}, bf16[144,512]{1,0:T(8,128)(2,1)S(1)}, u32[]{:S(2)}, u32[]{:S(2)}) collective-permute-start(bf16[144,512]{1,0:T(8,128)(2,1)S(1)} %pad_maximum_fusion.1), channel_id=1, source_target_pairs={{0,1},{1,2},{2,3},{3,388},{4,5},{5,6},{6,7},{7,392},{8,9},{9,10},{... | collective-permute-start | bytes 442376 | tf_op jit(solution)/shard_map/ppermute | solution.py:30
  9.6 9.6 %collective-permute-start.2 = (bf16[144,512]{1,0:T(8,128)(2,1)S(1)}, bf16[144,512]{1,0:T(8,128)(2,1)S(1)}, u32[]{:S(2)}, u32[]{:S(2)}) collective-permute-start(bf16[144,512]{1,0:T(8,128)(2,1)S(1)} %pad_maximum_fusion.1), channel_id=1, source_target_pairs={{0,2},{1,3},{2,388},{3,389},{4,6},{5,7},{6,392},{7,393},{8,10},{9,... | collective-permute-start | bytes 442376 | tf_op jit(solution)/shard_map/ppermute | solution.py:30
  24.8 15.0 %collective-permute-start.4 = (bf16[384,128]{1,0:T(8,128)(2,1)S(1)}, bf16[384,128]{1,0:T(8,128)(2,1)S(1)}, u32[]{:S(2)}, u32[]{:S(2)}) collective-permute-start(bf16[384,128]{1,0:T(8,128)(2,1)S(1)} %get-tuple-element.25), channel_id=1, source_target_pairs={{0,0},{1,1},{2,2},{3,3},{4,4},{5,5},{6,6},{7,7},{8,8},{9,9},{10,10... | collective-permute-start | bytes 294920 | tf_op jit(solution)/shard_map/ppermute | solution.py:30
  29.4 10.4 %collective-permute-start.5 = (bf16[384,128]{1,0:T(8,128)(2,1)S(1)}, bf16[384,128]{1,0:T(8,128)(2,1)S(1)}, u32[]{:S(2)}, u32[]{:S(2)}) collective-permute-start(bf16[384,128]{1,0:T(8,128)(2,1)S(1)} %get-tuple-element.28), channel_id=1, source_target_pairs={{0,64},{1,65},{2,66},{3,67},{4,68},{5,69},{6,70},{7,71},{8,72},{9,... | collective-permute-start | bytes 294920 | tf_op jit(solution)/shard_map/ppermute | solution.py:30
  31.3 10.7 %collective-permute-start.6 = (bf16[384,128]{1,0:T(8,128)(2,1)S(1)}, bf16[384,128]{1,0:T(8,128)(2,1)S(1)}, u32[]{:S(2)}, u32[]{:S(2)}) collective-permute-start(bf16[384,128]{1,0:T(8,128)(2,1)S(1)} %get-tuple-element.27), channel_id=1, source_target_pairs={{0,384},{1,385},{2,386},{3,387},{4,388},{5,389},{6,390},{7,391},{8... | collective-permute-start | bytes 294920 | tf_op jit(solution)/shard_map/ppermute | solution.py:30
  34.7 9.8 %collective-permute-start.7 = (bf16[384,128]{1,0:T(8,128)(2,1)S(1)}, bf16[384,128]{1,0:T(8,128)(2,1)S(1)}, u32[]{:S(2)}, u32[]{:S(2)}) collective-permute-start(bf16[384,128]{1,0:T(8,128)(2,1)S(1)} %get-tuple-element.26), channel_id=1, source_target_pairs={{0,448},{1,449},{2,450},{3,451},{4,452},{5,453},{6,454},{7,455},{8... | collective-permute-start | bytes 294920 | tf_op jit(solution)/shard_map/ppermute | solution.py:30
  37.8 30.0 %collective-permute-start.3 = (bf16[128,1280]{1,0:T(8,128)(2,1)S(1)}, bf16[128,1280]{1,0:T(8,128)(2,1)S(1)}, u32[]{:S(2)}, u32[]{:S(2)}) collective-permute-start(bf16[128,1280]{1,0:T(8,128)(2,1)S(1)} %get-tuple-element.13), channel_id=1, source_target_pairs={{0,64},{1,65},{2,66},{3,67},{4,68},{5,69},{6,70},{7,71},{8,72},{9,... | collective-permute-start | bytes 983048 | tf_op jit(solution)/shard_map/ppermute | solution.py:30
  44.6 10.4 %collective-permute-start.8 = (bf16[128,128]{1,0:T(8,128)(2,1)S(1)}, bf16[128,128]{1,0:T(8,128)(2,1)S(1)}, u32[]{:S(2)}, u32[]{:S(2)}) collective-permute-start(bf16[128,128]{1,0:T(8,128)(2,1)S(1)} %get-tuple-element.36), channel_id=1, source_target_pairs={{1,0},{2,1},{3,2},{4,387},{5,4},{6,5},{7,6},{8,391},{9,8},{10,9},{... | collective-permute-start | bytes 98312 | tf_op jit(solution)/shard_map/ppermute | solution.py:30
  52.3 13.3 %collective-permute-start.9 = (bf16[128,128]{1,0:T(8,128)(2,1)S(1)}, bf16[128,128]{1,0:T(8,128)(2,1)S(1)}, u32[]{:S(2)}, u32[]{:S(2)}) collective-permute-start(bf16[128,128]{1,0:T(8,128)(2,1)S(1)} %get-tuple-element.35), channel_id=1, source_target_pairs={{2,0},{3,1},{4,386},{5,387},{6,4},{7,5},{8,390},{9,391},{10,8},{11... | collective-permute-start | bytes 98312 | tf_op jit(solution)/shard_map/ppermute | solution.py:30
  55.0 10.6 %copy-start.5 = (bf16[128,128]{1,0:T(8,128)(2,1)}, bf16[128,128]{1,0:T(8,128)(2,1)S(1)}, u32[]{:S(2)}) copy-start(bf16[128,128]{1,0:T(8,128)(2,1)S(1)} %collective-permute-done.8.one_ref) | copy-start | bytes 98308
  65.6 0.6 copy-start.6

commit v3 on v2

--- a/solution.py
+++ b/solution.py
@@ -30,12 +30,24 @@
     return lax.ppermute(x, AXES, found)
 
 
-def shifted(x, by):
+def fetched(x):
     def target(s, c):
-        leaves = (c // ROW) != ((c + by) // ROW)
-        return ((3 - s // 2) * 2 + s % 2 if leaves else s, c + by)
+        to = c + 1 + s // 2 % 2
+        return (s ^ 4 if c // ROW != to // ROW else s, to)
 
     return permuted(x, target)
+
+
+def returned(x):
+    def target(s, c):
+        to = c - 1 - s % 2
+        return ((3 - s // 2) * 2 + s % 2 if c // ROW != to // ROW else s, to)
+
+    return permuted(x, target)
+
+
+def next_chip(x):
+    return permuted(x, lambda s, c: (s ^ 2, c))
 
 
 def other_core(x):
@@ -54,21 +66,36 @@
     return permuted(x, target)
 
 
+def pack_halo(place_ref, ids_ref, k_ref, v_ref, out_ref):
+    out_ref[:TOK, :DH] = k_ref[...]
+    out_ref[:TOK, DH:] = v_ref[...]
+    ids = jnp.broadcast_to((ids_ref[...] + 1).astype(jnp.float32), (ID_ROWS, TOK)).astype(jnp.bfloat16)
+    out_ref[TOK:, :DH] = ids
+    out_ref[TOK:, DH:] = ids
+
+
+def pack_rows(place_ref, q_ref, c_ref, q_out_ref, c_out_ref):
+    q_out_ref[...] = q_ref[...]
+    c_out_ref[...] = c_ref[...]
+
+
 def attend(
-    place_ref, ids_ref, q_ref, c_ref, oq_ref, oc_ref, k_ref, v_ref, k1_ref, v1_ref, k2_ref, v2_ref,
-    id1_ref, id2_ref, dq_ref, odq_ref, part_ref,
+    place_ref, ids_ref, q_ref, c_ref, oq_ref, oc_ref, k_ref, v_ref, fetched_ref, swapped_ref, dq_ref, odq_ref, part_ref
 ):
     slot = pl.program_id(0)
     ids = ids_ref[...].astype(jnp.float32)
     first = ids[:, 0:1]
-    keys = jnp.concatenate([k_ref[...], k1_ref[...], k2_ref[...]], 0)
-    values = jnp.concatenate([v_ref[...], v1_ref[...], v2_ref[...]], 0)
+    even = place_ref[1] % 2 == 0
+    one = jnp.where(even, fetched_ref[...], swapped_ref[...])
+    two = jnp.where(even, swapped_ref[...], fetched_ref[...])
+    keys = jnp.concatenate([k_ref[...], one[:TOK, :DH], two[:TOK, :DH]], 0)
+    values = jnp.concatenate([v_ref[...], one[:TOK, DH:], two[:TOK, DH:]], 0)
     row = lax.broadcasted_iota(jnp.int32, (TOK, TOK), 0)
     col = lax.broadcasted_iota(jnp.int32, (TOK, TOK), 1)
     wide = jnp.broadcast_to(ids, (TOK, TOK))
     biases = [jnp.where((wide.T == wide) & (row <= col), 0.0, NEG)]
-    for id_ref in (id1_ref, id2_ref):
-        before = id_ref[0:1, :].astype(jnp.float32)
+    for halo in (one, two):
+        before = halo[TOK:, :DH].astype(jnp.float32)[0:1]
         held = jnp.sum(jnp.where(before == first + 1.0, 1.0, 0.0), -1, keepdims=True)
         biases.append(jnp.where((wide == first) & (row.astype(jnp.float32) >= TOK - held), 0.0, NEG))
     bias = jnp.concatenate(biases, 0)
@@ -105,16 +132,17 @@
         jnp.concatenate([grad_k[:, :half], grad_v[:, :half]], 1),
         jnp.concatenate([grad_k[:, half:], grad_v[:, half:]], 1),
     )
-    for block in range(3):
-        mirror = place_ref[2 + block]
-        rows = slice(block * TOK, (block + 1) * TOK)
-        for side in range(2):
-            share = 2 * (slot ^ mirror) + side
-            part_ref[share ^ place_ref[1], rows, :] = shares[side][rows]
-
-
-def finish(own_ref, one_ref, two_ref, dk_ref, dv_ref):
-    total = own_ref[...] + one_ref[...].astype(jnp.float32) + two_ref[...].astype(jnp.float32)
+    for side in range(2):
+        part_ref[(2 * slot + side) ^ place_ref[1], :TOK, :] = shares[side][:TOK]
+        for block in (1, 2):
+            carrier = 2 * (slot ^ place_ref[1 + block]) + block - 1
+            rows = slice((1 + side) * TOK, (2 + side) * TOK)
+            part_ref[carrier ^ place_ref[1], rows, :] = shares[side][block * TOK : (block + 1) * TOK]
+
+
+def finish(place_ref, own_ref, back_ref, swapped_ref, dq_ref, dk_ref, dv_ref):
+    mine = back_ref[pl.ds(pl.multiple_of(place_ref[0] * TOK, TOK), TOK), :]
+    total = own_ref[...] + mine.astype(jnp.float32) + swapped_ref[...].astype(jnp.float32)
     total = total.T
     dk_ref[...] = total[: DH // 2]
     dv_ref[...] = total[DH // 2 :]
@@ -126,50 +154,67 @@
     tok = keys.shape[0]
     q, c = queries[0], cotangent[0]
 
-    def of_core(x, unit, which):
-        outer = jnp.concatenate([x[:, :unit], x[:, 3 * unit :]], 1)
-        return jnp.where(which == 0, outer, x[:, unit : 3 * unit])
-
-    ids = jnp.broadcast_to((segment_ids + 1).astype(jnp.bfloat16)[None], (ID_ROWS, tok))
-    ids = jnp.pad(ids, ((0, 0), (0, 4 * DH - tok)))
-    sent = jnp.concatenate([of_core(keys, DH, core), of_core(values, DH, core)], 1)
-    sent = jnp.concatenate([sent, ids], 0)
-    one, two = shifted(sent, 1), shifted(sent, 2)
-    q, c, _ = lax.optimization_barrier((q, c, sent))
-    swapped = other_core(jnp.concatenate([of_core(q, WIDE, 1 - core), of_core(c, WIDE, 1 - core)], 0))
-    place = jnp.stack(
-        [core, y_lo, jnp.zeros_like(core), (me % ROW < 1).astype(core.dtype), (me % ROW < 2).astype(core.dtype)]
-    ).astype(jnp.int32)
+    ids = segment_ids.reshape(1, tok)
+    place = jnp.stack([core, y_lo, (me % ROW < 1).astype(core.dtype), (me % ROW < 2).astype(core.dtype)])
+    place = place.astype(jnp.int32)
 
     def own(g, at):
         return (0, group_of(at[0], g))
 
-    def halo(row, lane):
-        return lambda g, at: (row, lane + g)
-
+    def others(g, at):
+        return (0, group_of(1 - at[0], g))
+
+    def column(g, at):
+        return (0, g)
+
+    def fixed(g, at):
+        return (0, 0)
+
+    sent = pl.pallas_call(
+        pack_halo,
+        grid_spec=pltpu.PrefetchScalarGridSpec(
+            num_scalar_prefetch=1,
+            grid=(2,),
+            in_specs=[pl.BlockSpec((1, tok), fixed), pl.BlockSpec((tok, DH), own), pl.BlockSpec((tok, DH), own)],
+            out_specs=pl.BlockSpec((tok + ID_ROWS, 2 * DH), column),
+        ),
+        out_shape=jax.ShapeDtypeStruct((tok + ID_ROWS, 4 * DH), jnp.bfloat16),
+        name="pack_halo",
+    )(place, ids, keys, values)
+    halo = fetched(sent)
+    halo_other = next_chip(halo)
+    q, c, _ = lax.optimization_barrier((q, c, sent))
+    other_rows = pl.pallas_call(
+        pack_rows,
+        grid_spec=pltpu.PrefetchScalarGridSpec(
+            num_scalar_prefetch=1,
+            grid=(2,),
+            in_specs=[pl.BlockSpec((tok, WIDE), others), pl.BlockSpec((tok, WIDE), others)],
+            out_specs=(pl.BlockSpec((tok, WIDE), column),) * 2,
+        ),
+        out_shape=(jax.ShapeDtypeStruct((tok, 2 * WIDE), jnp.bfloat16),) * 2,
+        name="pack_rows",
+    )(place, q, c)
+    other_rows = [other_core(x) for x in other_rows]
     grad_q, other_q, part = pl.pallas_call(
         attend,
         grid_spec=pltpu.PrefetchScalarGridSpec(
             num_scalar_prefetch=1,
             grid=(2,),
             in_specs=[
-                pl.BlockSpec((1, tok), lambda g, at: (0, 0)),
+                pl.BlockSpec((1, tok), fixed),
                 pl.BlockSpec((tok, WIDE), own),
                 pl.BlockSpec((tok, WIDE), own),
-                pl.BlockSpec((tok, WIDE), halo(0, 0)),
-                pl.BlockSpec((tok, WIDE), halo(1, 0)),
+                pl.BlockSpec((tok, WIDE), column),
+                pl.BlockSpec((tok, WIDE), column),
                 pl.BlockSpec((tok, DH), own),
                 pl.BlockSpec((tok, DH), own),
-                pl.BlockSpec((tok, DH), halo(0, 0)),
-                pl.BlockSpec((tok, DH), halo(0, 2)),
-                pl.BlockSpec((tok, DH), halo(0, 0)),
-                pl.BlockSpec((tok, DH), halo(0, 2)),
-                pl.BlockSpec((ID_ROWS, tok), lambda g, at: (tok // ID_ROWS, 0)),
-                pl.BlockSpec((ID_ROWS, tok), lambda g, at: (tok // ID_ROWS, 0)),
+                pl.BlockSpec((tok + ID_ROWS, 2 * DH), column),
+                pl.BlockSpec((tok + ID_ROWS, 2 * DH), column),
             ],
             out_specs=(
                 pl.BlockSpec((tok, WIDE), own),
-                pl.BlockSpec((tok, WIDE), halo(0, 0)),
+                pl.BlockSpec((tok, WIDE), column),
                 pl.BlockSpec((4, 3 * tok, DH), lambda g, at: (0, 0, 0)),
             ),
         ),
@@ -180,19 +225,23 @@
         ),
         compiler_params=pltpu.CompilerParams(vmem_limit_bytes=24 * 1024 * 1024),
         name="attend",
-    )(place, segment_ids.reshape(1, tok), q, c, swapped, swapped, keys, values, one, one, two, two, one, two)
-    total = sum(to_owner(part[step], step).astype(jnp.float32) for step in range(4))
-    back_one = shifted(total[tok : 2 * tok].astype(jnp.bfloat16), -1)
-    back_two = shifted(total[2 * tok :].astype(jnp.bfloat16), -2)
+    )(place, ids, q, c, *other_rows, keys, values, halo, halo_other)
+    shares = [to_owner(part[step], step) for step in range(4)]
+    total = sum(share[:tok].astype(jnp.float32) for share in shares)
+    back = sum(share[tok:].astype(jnp.float32) for share in shares).astype(jnp.bfloat16)
+    back = returned(back)
+    back_other = other_core(jnp.where(core == 0, back[tok:], back[:tok]))
     back_q = other_core(other_q)
     outer = jnp.concatenate([back_q[:, :WIDE], grad_q[:, WIDE : 3 * WIDE], back_q[:, WIDE:]], 1)
     inner = jnp.concatenate([grad_q[:, :WIDE], back_q, grad_q[:, 3 * WIDE :]], 1)
     grad_q = jnp.where(core == 0, inner, outer)
+    vmem = pl.BlockSpec(memory_space=pltpu.VMEM)
     grad_k, grad_v = pl.pallas_call(
         finish,
+        in_specs=[pl.BlockSpec(memory_space=pltpu.SMEM), vmem, vmem, vmem, pl.BlockSpec(memory_space=pl.ANY)],
         out_shape=(jax.ShapeDtypeStruct((DH // 2, tok), jnp.float32),) * 2,
         name="finish",
-    )(total[:tok], back_one, back_two)
+    )(place, total, back, back_other, grad_q)
     return (grad_q[None], grad_k.T, grad_v.T)
 
 

time: 69.3 us -> 72 us (1.039)
  the two profiles are of different devices: /device:TPU:244 before, /device:TPU:231 now
where the time goes in v3:
time: 72 us; the launch traced here: 71.3 us
  starting transfers between devices  42.8 us (59%)
  Pallas kernels  12.1 us (17%)
  waiting for transfers between devices  11.4 us (16%)
  other arithmetic  3.33 us (5%)
  between operations  0.89 us (1%)
  local copies, waits for them, and re-layouts  0.82 us (1%)
    ppermute x11, starting transfers between devices, permuted(): return lax.ppermute(x, AXES, found)  42.8 us
    ppermute x11, waiting for transfers between devices, permuted(): return lax.ppermute(x, AXES, found)  11.4 us
    pallas_call x1, Pallas kernels, on_device(): pl.pallas_call(attend, grid_spec=pltpu.PrefetchScalarGridSpec(num_scalar_...  5.45 us
    pallas_call x1, Pallas kernels, on_device(): pl.pallas_call(pack_rows, grid_spec=pltpu.PrefetchScalarGridSpec(num_scal...  2.73 us
    pallas_call x1, Pallas kernels, on_device(): pl.pallas_call(pack_halo, grid_spec=pltpu.PrefetchScalarGridSpec(num_scal...  2.31 us
    select_n x2, other arithmetic, on_device(): grad_q = jnp.where(core == 0, inner, outer)  2.05 us
    pallas_call x1, Pallas kernels, on_device(): pl.pallas_call(finish, in_specs=[pl.BlockSpec(memory_space=pltpu.SMEM), v...  1.6 us
  transfers between devices with their start and end apart: 11, of which 4 were waited for; matrix products, arithmetic and copies ran while one was open for 4% of the time, Pallas kernels for 0%

profile of v3, /device:TPU:231, one launch (start us, length us, event | category | flops | bytes accessed | tf_op | source)
XLA Modules:
  0.0 71.3 jit_solution(10037788260663956846)
XLA Ops:
  0.7 0.6 pad_add_fusion.place_ref
  1.2 0.0 copy-start.2
  1.2 0.0 copy-start.3
  1.2 2.3 %pack_halo.1 = bf16[144,512]{1,0:T(8,128)(2,1)} custom-call(s32[4]{0:T(128)} %pad_add_fusion.place_ref, s32[1,128]{1,0:T(1,128)} %bitcast.32, bf16[128,512]{1,0:T(8,128)(2,1)} %k_ref.3, bf16[128,512]{1,0:T(8,128)(2,1)} %v_ref.3), custom_call_target="tpu_custom_call" | custom-call | tf_op jit(solution)/shard_map/pack_halo/pallas_call | solution.py:173
  3.6 0.0 copy-start
  3.6 0.0 copy-start.1
  3.6 0.0 copy-start.4
  3.6 0.0 copy-start.5
  3.6 2.7 %pack_rows.1 = (bf16[128,1280]{1,0:T(8,128)(2,1)}, bf16[128,1280]{1,0:T(8,128)(2,1)}) custom-call(s32[4]{0:T(128)} %pad_add_fusion.place_ref, bf16[128,2560]{1,0:T(8,128)(2,1)} %bitcast.28, bf16[128,2560]{1,0:T(8,128)(2,1)} %bitcast.30), custom_call_target="tpu_custom_call" | custom-call | tf_op jit(solution)/shard_map/pack_rows/pallas_call | solution.py:187
  6.3 2.6 %collective-permute-start = (bf16[128,1280]{1,0:T(8,128)(2,1)}, bf16[128,1280]{1,0:T(8,128)(2,1)S(1)}, u32[]{:S(2)}, u32[]{:S(2)}) collective-permute-start(bf16[128,1280]{1,0:T(8,128)(2,1)} %get-tuple-element.14), channel_id=1, source_target_pairs={{0,64},{1,65},{2,66},{3,67},{4,68},{5,69},{6,70},{7,71},{8,72},{9,... | collective-permute-start | bytes 983048 | tf_op jit(solution)/shard_map/ppermute | solution.py:30
  8.9 1.9 %collective-permute-start.1 = (bf16[128,1280]{1,0:T(8,128)(2,1)}, bf16[128,1280]{1,0:T(8,128)(2,1)S(1)}, u32[]{:S(2)}, u32[]{:S(2)}) collective-permute-start(bf16[128,1280]{1,0:T(8,128)(2,1)} %get-tuple-element.15), channel_id=1, source_target_pairs={{0,64},{1,65},{2,66},{3,67},{4,68},{5,69},{6,70},{7,71},{8,72},{9,... | collective-permute-start | bytes 983048 | tf_op jit(solution)/shard_map/ppermute | solution.py:30
  10.8 4.9 %collective-permute-start.2 = (bf16[144,512]{1,0:T(8,128)(2,1)}, bf16[144,512]{1,0:T(8,128)(2,1)S(1)}, u32[]{:S(2)}, u32[]{:S(2)}) collective-permute-start(bf16[144,512]{1,0:T(8,128)(2,1)} %pack_halo.1), channel_id=1, source_target_pairs={{0,1},{1,2},{2,3},{3,260},{4,5},{5,6},{6,7},{7,264},{8,9},{9,10},{... | collective-permute-start | bytes 442376 | tf_op jit(solution)/shard_map/ppermute | solution.py:30
  15.7 3.0 %collective-permute-done.2.fetched_ref = bf16[144,512]{1,0:T(8,128)(2,1)S(1)} collective-permute-done((bf16[144,512]{1,0:T(8,128)(2,1)}, bf16[144,512]{1,0:T(8,128)(2,1)S(1)}, u32[]{:S(2)}, u32[]{:S(2)}) %collective-permute-start.2) | collective-permute-done | bytes 147488 | tf_op jit(solution)/shard_map/ppermute | solution.py:30
  18.7 4.2 %collective-permute-start.3 = (bf16[144,512]{1,0:T(8,128)(2,1)S(1)}, bf16[144,512]{1,0:T(8,128)(2,1)S(1)}, u32[]{:S(2)}, u32[]{:S(2)}) collective-permute-start(bf16[144,512]{1,0:T(8,128)(2,1)S(1)} %collective-permute-done.2.fetched_ref), channel_id=1, source_target_pairs={{0,128},{1,129},{2,130},{3,131},{4,132},{5,133},{6,134},{7,135},{8... | collective-permute-start | bytes 442376 | tf_op jit(solution)/shard_map/ppermute | solution.py:30
  22.9 2.5 %collective-permute-done.3.swapped_ref = bf16[144,512]{1,0:T(8,128)(2,1)S(1)} collective-permute-done((bf16[144,512]{1,0:T(8,128)(2,1)S(1)}, bf16[144,512]{1,0:T(8,128)(2,1)S(1)}, u32[]{:S(2)}, u32[]{:S(2)}) %collective-permute-start.3) | collective-permute-done | bytes 147488 | tf_op jit(solution)/shard_map/ppermute | solution.py:30
  25.4 0.0 collective-permute-done.oq_ref
  25.4 0.0 collective-permute-done.1.oc_ref
  25.4 0.0 copy-done.2
  25.4 0.0 copy-done.3
  25.4 0.0 copy-done
  25.5 0.0 copy-done.1
  25.5 0.0 copy-done.4
  25.5 0.0 copy-done.5
  25.5 5.4 %attend.1 = (bf16[128,2560]{1,0:T(8,128)(2,1)S(1)}, bf16[128,1280]{1,0:T(8,128)(2,1)S(1)}, bf16[4,384,128]{2,1,0:T(8,128)(2,1)S(1)}) custom-call(s32[4]{0:T(128)S(1)} %copy-done.4, s32[1,128]{1,0:T(1,128)S(1)} %bitcast.33, bf16[128,2560]{1,0:T(8,128)(2,1)S(1)} %bitcast.29, bf16[128,2560]{1,0:T(8,128)(2,1)S(1)} %bitcast.31, ...), custom_call_target="tpu_custom_call" | custom-call | tf_op jit(solution)/shard_map/attend/pallas_call | solution.py:199
  31.0 6.4 %collective-permute-start.5 = (bf16[384,128]{1,0:T(8,128)(2,1)S(1)}, bf16[384,128]{1,0:T(8,128)(2,1)S(1)}, u32[]{:S(2)}, u32[]{:S(2)}) collective-permute-start(bf16[384,128]{1,0:T(8,128)(2,1)S(1)} %get-tuple-element.27), channel_id=1, source_target_pairs={{0,0},{1,1},{2,2},{3,3},{4,4},{5,5},{6,6},{7,7},{8,8},{9,9},{10,10... | collective-permute-start | bytes 294920 | tf_op jit(solution)/shard_map/ppermute | solution.py:30
  37.4 2.7 %collective-permute-start.8 = (bf16[384,128]{1,0:T(8,128)(2,1)S(1)}, bf16[384,128]{1,0:T(8,128)(2,1)S(1)}, u32[]{:S(2)}, u32[]{:S(2)}) collective-permute-start(bf16[384,128]{1,0:T(8,128)(2,1)S(1)} %get-tuple-element.28), channel_id=1, source_target_pairs={{0,448},{1,449},{2,450},{3,451},{4,452},{5,453},{6,454},{7,455},{8... | collective-permute-start | bytes 294920 | tf_op jit(solution)/shard_map/ppermute | solution.py:30
  40.1 3.8 %collective-permute-start.7 = (bf16[384,128]{1,0:T(8,128)(2,1)S(1)}, bf16[384,128]{1,0:T(8,128)(2,1)S(1)}, u32[]{:S(2)}, u32[]{:S(2)}) collective-permute-start(bf16[384,128]{1,0:T(8,128)(2,1)S(1)} %get-tuple-element.29), channel_id=1, source_target_pairs={{0,384},{1,385},{2,386},{3,387},{4,388},{5,389},{6,390},{7,391},{8... | collective-permute-start | bytes 294920 | tf_op jit(solution)/shard_map/ppermute | solution.py:30
  43.9 1.9 %collective-permute-start.6 = (bf16[384,128]{1,0:T(8,128)(2,1)S(1)}, bf16[384,128]{1,0:T(8,128)(2,1)S(1)}, u32[]{:S(2)}, u32[]{:S(2)}) collective-permute-start(bf16[384,128]{1,0:T(8,128)(2,1)S(1)} %get-tuple-element.30), channel_id=1, source_target_pairs={{0,64},{1,65},{2,66},{3,67},{4,68},{5,69},{6,70},{7,71},{8,72},{9,... | collective-permute-start | bytes 294920 | tf_op jit(solution)/shard_map/ppermute | solution.py:30
  45.9 0.1 fusion.1
  45.9 2.4 %collective-permute-start.4 = (bf16[128,1280]{1,0:T(8,128)(2,1)S(1)}, bf16[128,1280]{1,0:T(8,128)(2,1)S(1)}, u32[]{:S(2)}, u32[]{:S(2)}) collective-permute-start(bf16[128,1280]{1,0:T(8,128)(2,1)S(1)} %get-tuple-element.17), channel_id=1, source_target_pairs={{0,64},{1,65},{2,66},{3,67},{4,68},{5,69},{6,70},{7,71},{8,72},{9,... | collective-permute-start | bytes 983048 | tf_op jit(solution)/shard_map/ppermute | solution.py:30
  48.3 0.0 collective-permute-done.5
  48.3 0.0 collective-permute-done.8
  48.4 0.5 collective-permute-done.7
  48.8 0.0 collective-permute-done.6
  48.9 7.3 %collective-permute-start.9 = (bf16[256,128]{1,0:T(8,128)(2,1)S(1)}, bf16[256,128]{1,0:T(8,128)(2,1)S(1)}, u32[]{:S(2)}, u32[]{:S(2)}) collective-permute-start(bf16[256,128]{1,0:T(8,128)(2,1)S(1)} %add_convert_fusion), channel_id=1, source_target_pairs={{1,0},{2,1},{3,2},{4,387},{5,4},{6,5},{7,6},{8,391},{9,8},{10,9},{... | collective-permute-start | bytes 196616 | tf_op jit(solution)/shard_map/ppermute | solution.py:30
  56.2 0.6 convert_add_fusion.own_ref
  56.8 5.4 %collective-permute-done.9.back_ref = bf16[256,128]{1,0:T(8,128)(2,1)S(1)} collective-permute-done((bf16[256,128]{1,0:T(8,128)(2,1)S(1)}, bf16[256,128]{1,0:T(8,128)(2,1)S(1)}, u32[]{:S(2)}, u32[]{:S(2)}) %collective-permute-start.9) | collective-permute-done | bytes 65568 | tf_op jit(solution)/shard_map/ppermute | solution.py:30
  62.3 0.0 copy-start.6
  62.3 4.7 %collective-permute-start.10 = (bf16[128,128]{1,0:T(8,128)(2,1)S(1)}, bf16[128,128]{1,0:T(8,128)(2,1)S(1)}, u32[]{:S(2)}, u32[]{:S(2)}) collective-permute-start(bf16[128,128]{1,0:T(8,128)(2,1)S(1)} %slice_select_fusion), channel_id=1, source_target_pairs={{0,64},{1,65},{2,66},{3,67},{4,68},{5,69},{6,70},{7,71},{8,72},{9,... | collective-permute-start | bytes 98312 | tf_op jit(solution)/shard_map/ppermute | solution.py:30
  67.0 0.0 collective-permute-done.4
  67.0 0.1 fusion.2
  67.1 1.0 %maximum_select_fusion = bf16[1,128,2560]{2,1,0:T(8,128)(2,1)} fusion(bf16[1,128,640]{2,1,0:T(8,128)(2,1)S(1)} %get-tuple-element.25, bf16[1,128,1280]{2,1,0:T(8,128)(2,1)S(1)} %bitcast.34, bf16[1,128,640]{2,1,0:T(8,128)(2,1)S(1)} %get-tuple-element.24, bf16[1,128,640]{2,1,0:T(8,128)(2,1)S(1)} %get-tuple-element.33, ...), kind=kLoop, calls=%fused_computation | loop fusion | flops 4259840 | bytes 1966081 | tf_op jit(solution)/shard_map/jit(_where)/select_n | solution.py:237
  68.1 0.0 copy-done.6
  68.1 1.0 %maximum_select_fusion.1.dq_ref = bf16[128,2560]{1,0:T(8,128)(2,1)} fusion(bf16[128,640]{1,0:T(8,128)(2,1)S(1)} %get-tuple-element.26, bf16[128,1280]{1,0:T(8,128)(2,1)S(1)} %collective-permute-done.4, bf16[128,640]{1,0:T(8,128)(2,1)S(1)} %get-tuple-element.23, bf16[128,640]{1,0:T(8,128)(2,1)S(1)} %get-tuple-element.34, ...), kind=kLoop, calls=%fused_computation.1 | loop fusion | flops 4259840 | bytes 1966081 | tf_op jit(solution)/shard_map/jit(_where)/select_n | solution.py:237
  69.1 0.0 collective-permute-done.10.swapped_ref
  69.1 0.0 copy-start.7
  69.1 0.6 copy-done.7
  69.7 1.6 %finish.1 = (f32[64,128]{1,0:T(8,128)}, f32[64,128]{1,0:T(8,128)}) custom-call(s32[4]{0:T(128)} %pad_add_fusion.place_ref, f32[128,128]{1,0:T(8,128)} %convert_add_fusion.own_ref, bf16[256,128]{1,0:T(8,128)(2,1)} %copy-done.6, bf16[128,128]{1,0:T(8,128)(2,1)} %copy-done.7, bf16[128,2560]{1,0:T(8,128)(2,1)} %maximum_select_fusion.1.dq_ref), custom_call_target="tpu_custom_call" | custom-call | tf_op jit(solution)/shard_map/finish/pallas_call | solution.py:239
  (4 shorter events, 0.1 us)
Async XLA Ops:
  1.2 24.2 %copy-start.2 = (bf16[128,512]{1,0:T(8,128)(2,1)S(1)}, bf16[128,512]{1,0:T(8,128)(2,1)}, u32[]{:S(2)}) copy-start(bf16[128,512]{1,0:T(8,128)(2,1)} %k_ref.3) | copy-start | bytes 393220
  1.2 24.2 %copy-start.3 = (bf16[128,512]{1,0:T(8,128)(2,1)S(1)}, bf16[128,512]{1,0:T(8,128)(2,1)}, u32[]{:S(2)}) copy-start(bf16[128,512]{1,0:T(8,128)(2,1)} %v_ref.3) | copy-start | bytes 393220
  3.6 21.9 %copy-start = (bf16[1,128,2560]{2,1,0:T(8,128)(2,1)S(1)}, bf16[1,128,2560]{2,1,0:T(8,128)(2,1)}, u32[]{:S(2)}) copy-start(bf16[1,128,2560]{2,1,0:T(8,128)(2,1)} %param.5) | copy-start | bytes 1966084
  3.6 21.9 %copy-start.1 = (bf16[1,128,2560]{2,1,0:T(8,128)(2,1)S(1)}, bf16[1,128,2560]{2,1,0:T(8,128)(2,1)}, u32[]{:S(2)}) copy-start(bf16[1,128,2560]{2,1,0:T(8,128)(2,1)} %param.8) | copy-start | bytes 1966084
  3.6 21.9 %copy-start.4 = (s32[4]{0:T(128)S(1)}, s32[4]{0:T(128)}, u32[]{:S(2)}) copy-start(s32[4]{0:T(128)} %pad_add_fusion.place_ref) | copy-start | bytes 52
  3.6 21.9 %copy-start.5 = (s32[128]{0:T(128)S(1)}, s32[128]{0:T(128)}, u32[]{:S(2)}) copy-start(s32[128]{0:T(128)} %param.9) | copy-start | bytes 1540
  6.3 19.1 %collective-permute-start = (bf16[128,1280]{1,0:T(8,128)(2,1)}, bf16[128,1280]{1,0:T(8,128)(2,1)S(1)}, u32[]{:S(2)}, u32[]{:S(2)}) collective-permute-start(bf16[128,1280]{1,0:T(8,128)(2,1)} %get-tuple-element.14), channel_id=1, source_target_pairs={{0,64},{1,65},{2,66},{3,67},{4,68},{5,69},{6,70},{7,71},{8,72},{9,... | collective-permute-start | bytes 983048 | tf_op jit(solution)/shard_map/ppermute | solution.py:30
  8.9 16.5 %collective-permute-start.1 = (bf16[128,1280]{1,0:T(8,128)(2,1)}, bf16[128,1280]{1,0:T(8,128)(2,1)S(1)}, u32[]{:S(2)}, u32[]{:S(2)}) collective-permute-start(bf16[128,1280]{1,0:T(8,128)(2,1)} %get-tuple-element.15), channel_id=1, source_target_pairs={{0,64},{1,65},{2,66},{3,67},{4,68},{5,69},{6,70},{7,71},{8,72},{9,... | collective-permute-start | bytes 983048 | tf_op jit(solution)/shard_map/ppermute | solution.py:30
  10.8 7.9 %collective-permute-start.2 = (bf16[144,512]{1,0:T(8,128)(2,1)}, bf16[144,512]{1,0:T(8,128)(2,1)S(1)}, u32[]{:S(2)}, u32[]{:S(2)}) collective-permute-start(bf16[144,512]{1,0:T(8,128)(2,1)} %pack_halo.1), channel_id=1, source_target_pairs={{0,1},{1,2},{2,3},{3,260},{4,5},{5,6},{6,7},{7,264},{8,9},{9,10},{... | collective-permute-start | bytes 442376 | tf_op jit(solution)/shard_map/ppermute | solution.py:30
  18.7 6.7 %collective-permute-start.3 = (bf16[144,512]{1,0:T(8,128)(2,1)S(1)}, bf16[144,512]{1,0:T(8,128)(2,1)S(1)}, u32[]{:S(2)}, u32[]{:S(2)}) collective-permute-start(bf16[144,512]{1,0:T(8,128)(2,1)S(1)} %collective-permute-done.2.fetched_ref), channel_id=1, source_target_pairs={{0,128},{1,129},{2,130},{3,131},{4,132},{5,133},{6,134},{7,135},{8... | collective-permute-start | bytes 442376 | tf_op jit(solution)/shard_map/ppermute | solution.py:30
  31.0 17.4 %collective-permute-start.5 = (bf16[384,128]{1,0:T(8,128)(2,1)S(1)}, bf16[384,128]{1,0:T(8,128)(2,1)S(1)}, u32[]{:S(2)}, u32[]{:S(2)}) collective-permute-start(bf16[384,128]{1,0:T(8,128)(2,1)S(1)} %get-tuple-element.27), channel_id=1, source_target_pairs={{0,0},{1,1},{2,2},{3,3},{4,4},{5,5},{6,6},{7,7},{8,8},{9,9},{10,10... | collective-permute-start | bytes 294920 | tf_op jit(solution)/shard_map/ppermute | solution.py:30
  37.4 10.9 %collective-permute-start.8 = (bf16[384,128]{1,0:T(8,128)(2,1)S(1)}, bf16[384,128]{1,0:T(8,128)(2,1)S(1)}, u32[]{:S(2)}, u32[]{:S(2)}) collective-permute-start(bf16[384,128]{1,0:T(8,128)(2,1)S(1)} %get-tuple-element.28), channel_id=1, source_target_pairs={{0,448},{1,449},{2,450},{3,451},{4,452},{5,453},{6,454},{7,455},{8... | collective-permute-start | bytes 294920 | tf_op jit(solution)/shard_map/ppermute | solution.py:30
  40.1 8.7 %collective-permute-start.7 = (bf16[384,128]{1,0:T(8,128)(2,1)S(1)}, bf16[384,128]{1,0:T(8,128)(2,1)S(1)}, u32[]{:S(2)}, u32[]{:S(2)}) collective-permute-start(bf16[384,128]{1,0:T(8,128)(2,1)S(1)} %get-tuple-element.29), channel_id=1, source_target_pairs={{0,384},{1,385},{2,386},{3,387},{4,388},{5,389},{6,390},{7,391},{8... | collective-permute-start | bytes 294920 | tf_op jit(solution)/shard_map/ppermute | solution.py:30
  43.9 4.9 %collective-permute-start.6 = (bf16[384,128]{1,0:T(8,128)(2,1)S(1)}, bf16[384,128]{1,0:T(8,128)(2,1)S(1)}, u32[]{:S(2)}, u32[]{:S(2)}) collective-permute-start(bf16[384,128]{1,0:T(8,128)(2,1)S(1)} %get-tuple-element.30), channel_id=1, source_target_pairs={{0,64},{1,65},{2,66},{3,67},{4,68},{5,69},{6,70},{7,71},{8,72},{9,... | collective-permute-start | bytes 294920 | tf_op jit(solution)/shard_map/ppermute | solution.py:30
  45.9 21.1 %collective-permute-start.4 = (bf16[128,1280]{1,0:T(8,128)(2,1)S(1)}, bf16[128,1280]{1,0:T(8,128)(2,1)S(1)}, u32[]{:S(2)}, u32[]{:S(2)}) collective-permute-start(bf16[128,1280]{1,0:T(8,128)(2,1)S(1)} %get-tuple-element.17), channel_id=1, source_target_pairs={{0,64},{1,65},{2,66},{3,67},{4,68},{5,69},{6,70},{7,71},{8,72},{9,... | collective-permute-start | bytes 983048 | tf_op jit(solution)/shard_map/ppermute | solution.py:30
  48.9 13.4 %collective-permute-start.9 = (bf16[256,128]{1,0:T(8,128)(2,1)S(1)}, bf16[256,128]{1,0:T(8,128)(2,1)S(1)}, u32[]{:S(2)}, u32[]{:S(2)}) collective-permute-start(bf16[256,128]{1,0:T(8,128)(2,1)S(1)} %add_convert_fusion), channel_id=1, source_target_pairs={{1,0},{2,1},{3,2},{4,387},{5,4},{6,5},{7,6},{8,391},{9,8},{10,9},{... | collective-permute-start | bytes 196616 | tf_op jit(solution)/shard_map/ppermute | solution.py:30
  62.3 5.8 %copy-start.6 = (bf16[256,128]{1,0:T(8,128)(2,1)}, bf16[256,128]{1,0:T(8,128)(2,1)S(1)}, u32[]{:S(2)}) copy-start(bf16[256,128]{1,0:T(8,128)(2,1)S(1)} %collective-permute-done.9.back_ref) | copy-start | bytes 196612
  62.3 6.8 %collective-permute-start.10 = (bf16[128,128]{1,0:T(8,128)(2,1)S(1)}, bf16[128,128]{1,0:T(8,128)(2,1)S(1)}, u32[]{:S(2)}, u32[]{:S(2)}) collective-permute-start(bf16[128,128]{1,0:T(8,128)(2,1)S(1)} %slice_select_fusion), channel_id=1, source_target_pairs={{0,64},{1,65},{2,66},{3,67},{4,68},{5,69},{6,70},{7,71},{8,72},{9,... | collective-permute-start | bytes 98312 | tf_op jit(solution)/shard_map/ppermute | solution.py:30
  69.1 0.6 copy-start.7

commit v4 on v3

v4 whole, which is shorter than its diff:
```python
import jax
import jax.numpy as jnp
from jax import lax
from jax.experimental import pallas as pl
from jax.experimental.pallas import tpu as pltpu
from jax.sharding import PartitionSpec as P

DH = 128
TOK = 128
RATIO = 5
WIDE = RATIO * DH
ROW = 4
ID_ROWS = 16
SCALE = DH ** (-0.5)
LOG2E = 1.4426950408889634
NEG = -1e30
OWN_FLOPS = 1 << 34
AXES = ("section", "ctx")
NT = (((1,), (1,)), ((), ()))
TN = (((0,), (0,)), ((), ()))


def permuted(x, target):
    sections, cycle = lax.axis_size("section"), lax.axis_size("ctx")
    found = []
    for s in range(sections):
        for c in range(cycle):
            to = target(s, c)
            if 0 <= to[1] < cycle:
                found.append((s * cycle + c, to[0] * cycle + to[1]))
    return lax.ppermute(x, AXES, found)


def shifted(x, by):
    def target(s, c):
        leaves = c // ROW != (c + by) // ROW
        return ((3 - s // 2) * 2 + s % 2 if leaves else s, c + by)

    return permuted(x, target)


def returned(x):
    def target(s, c):
        to = c - 1 - s % 2
        return ((3 - s // 2) * 2 + s % 2 if c // ROW != to // ROW else s, to)

    return permuted(x, target)


def other_core(x):
    return permuted(x, lambda s, c: (s ^ 1, c))


def group_of(core, slot):
    return core + slot * (3 - 2 * core)


def to_owner(x, step):
    def target(s, c):
        share = (s // 2) ^ step
        return (group_of(s % 2, share // 2) * 2 + share % 2, c)

    return permuted(x, target)


def core_groups(core):
    return [group_of(core, slot) for slot in range(2)]


def columns(group, width):
    return pl.ds(pl.multiple_of(group * width, width), width)


def run(copies):
    for copy in copies:
        copy.start()
    for copy in copies:
        copy.wait()


def pack_halo(ids_ref, k_ref, v_ref, out_ref, ids_vmem, sems):
    copies = [pltpu.make_async_copy(ids_ref, ids_vmem, sems.at[4])]
    for slot, group in enumerate(core_groups(lax.axis_index("section") % 2)):
        for i, ref in enumerate((k_ref, v_ref)):
            to = out_ref.at[pl.ds(0, TOK), pl.ds((2 * slot + i) * DH, DH)]
            copies.append(pltpu.make_async_copy(ref.at[:, columns(group, DH)], to, sems.at[2 * slot + i]))
    run(copies)
    ids = jnp.broadcast_to((ids_vmem[...] + 1).astype(jnp.float32), (ID_ROWS, TOK)).astype(jnp.bfloat16)
    for column in range(4):
        out_ref[TOK:, column * DH : (column + 1) * DH] = ids


def pack_rows(q_ref, c_ref, out_ref, sems):
    copies = []
    for slot, group in enumerate(core_groups(1 - lax.axis_index("section") % 2)):
        for i, ref in enumerate((q_ref, c_ref)):
            to = out_ref.at[pl.ds(i * TOK, TOK), pl.ds(slot * WIDE, WIDE)]
            copies.append(pltpu.make_async_copy(ref.at[:, columns(group, WIDE)], to, sems.at[2 * slot + i]))
    run(copies)


def one_layer(ids_ref, q_ref, c_ref, k_ref, v_ref, one_ref, two_ref, dq_ref):
    ids = ids_ref[...].astype(jnp.float32)
    first = ids[:, 0:1]
    keys = jnp.concatenate([k_ref[...], one_ref[:TOK, :DH], two_ref[:TOK, :DH]], 0)
    values = jnp.concatenate([v_ref[...], one_ref[:TOK, DH:], two_ref[:TOK, DH:]], 0)
    row = lax.broadcasted_iota(jnp.int32, (TOK, TOK), 0)
    col = lax.broadcasted_iota(jnp.int32, (TOK, TOK), 1)
    wide = jnp.broadcast_to(ids, (TOK, TOK))
    biases = [jnp.where((wide.T == wide) & (row <= col), 0.0, NEG)]
    for halo in (one_ref, two_ref):
        before = halo[TOK:, :DH].astype(jnp.float32)[0:1]
        held = jnp.sum(jnp.where(before == first + 1.0, 1.0, 0.0), -1, keepdims=True)
        biases.append(jnp.where((wide == first) & (row.astype(jnp.float32) >= TOK - held), 0.0, NEG))
    bias = jnp.concatenate(biases, 0)
    queries = jnp.concatenate([q_ref[:, h * DH : (h + 1) * DH] for h in range(RATIO)], 0)
    cots = jnp.concatenate([c_ref[:, h * DH : (h + 1) * DH] for h in range(RATIO)], 0)
    scores = lax.dot_general(keys, queries, NT, preferred_element_type=jnp.float32)
    grad_probs = lax.dot_general(values, cots, NT, preferred_element_type=jnp.float32)
    probs_low, scaled_low = [], []
    for h in range(RATIO):
        at = slice(h * TOK, (h + 1) * TOK)
        s = scores[:, at] * (SCALE * LOG2E) + bias
        e = jnp.exp2(s - jnp.max(s, 0, keepdims=True))
        p = e * (1.0 / jnp.sum(e, 0, keepdims=True))
        low = p.astype(jnp.bfloat16)
        g = grad_probs[:, at]
        dot = jnp.sum(low.astype(jnp.float32) * g, 0, keepdims=True)
        probs_low.append(low)
        scaled_low.append((p * (g - dot) * SCALE).astype(jnp.bfloat16))
    probs_low = jnp.concatenate(probs_low, 1)
    scaled_low = jnp.concatenate(scaled_low, 1)
    grad_v = jnp.dot(probs_low, cots, preferred_element_type=jnp.float32)
    grad_k = jnp.dot(scaled_low, queries, preferred_element_type=jnp.float32)
    grad_q = lax.dot_general(keys, scaled_low, TN, preferred_element_type=jnp.float32)
    for h in range(RATIO):
        at = slice(h * TOK, (h + 1) * TOK)
        dq_ref[:, at] = grad_q[:, at].T.astype(jnp.bfloat16)
    return grad_k, grad_v


def attend_own(place_ref, ids_ref, q_ref, c_ref, k_ref, v_ref, one_ref, two_ref, dq_ref, dk_ref, dv_ref):
    grad_k, grad_v = one_layer(ids_ref, q_ref, c_ref, k_ref, v_ref, one_ref, two_ref, dq_ref)
    dk_ref[...] = grad_k
    dv_ref[...] = grad_v


def attend_other(
    place_ref, ids_ref, q_ref, c_ref, k_ref, v_ref, one_ref, two_ref, dk_ref, dv_ref, dq_ref, part_ref
):
    slot = pl.program_id(0)
    grad_k, grad_v = one_layer(ids_ref, q_ref, c_ref, k_ref, v_ref, one_ref, two_ref, dq_ref)
    half = DH // 2
    grad_k = (grad_k + dk_ref[...]).astype(jnp.bfloat16)
    grad_v = (grad_v + dv_ref[...]).astype(jnp.bfloat16)
    shares = (
        jnp.concatenate([grad_k[:, :half], grad_v[:, :half]], 1),
        jnp.concatenate([grad_k[:, half:], grad_v[:, half:]], 1),
    )
    for side in range(2):
        part_ref[(2 * slot + side) ^ place_ref[1], :TOK, :] = shares[side][:TOK]
        for block in (1, 2):
            carrier = 2 * (slot ^ place_ref[1 + block]) + block - 1
            rows = slice((1 + side) * TOK, (2 + side) * TOK)
            part_ref[carrier ^ place_ref[1], rows, :] = shares[side][block * TOK : (block + 1) * TOK]


def finish(own_ref, back_ref, swapped_ref, dq_in_ref, dq_ref, dk_ref, dv_ref, total_ref, sems):
    core = lax.axis_index("section") % 2
    half = DH // 2
    copies = []
    for slot, group in enumerate(core_groups(1 - core)):
        src = swapped_ref.at[:, pl.ds(slot * WIDE, WIDE)]
        copies.append(pltpu.make_async_copy(src, dq_ref.at[:, columns(group, WIDE)], sems.at[slot]))
    for copy in copies:
        copy.start()
    mine = back_ref[pl.ds(pl.multiple_of(core * TOK, TOK), TOK), :]
    total = own_ref[...] + mine.astype(jnp.float32) + swapped_ref[:, 2 * WIDE :].astype(jnp.float32)
    total_ref[...] = total.T
    for i, ref in enumerate((dk_ref, dv_ref)):
        copies.append(pltpu.make_async_copy(total_ref.at[pl.ds(i * half, half)], ref, sems.at[2 + i]))
        copies[-1].start()
    for copy in copies:
        copy.wait()


def on_device(queries, keys, values, cotangent, segment_ids):
    section, me = lax.axis_index("section"), lax.axis_index("ctx")
    core, y_lo = section % 2, section // 2
    tok = keys.shape[0]
    q, c = queries[0], cotangent[0]
    ids = segment_ids.reshape(1, tok)
    hbm = pl.BlockSpec(memory_space=pltpu.HBM)
    vmem = pl.BlockSpec(memory_space=pltpu.VMEM)

    def own(g, at):
        return (0, group_of(at[0], g))

    def column(g, at):
        return (0, g)

    def fixed(g, at):
        return (0, 0)

    sent = pl.pallas_call(
        pack_halo,
        in_specs=[hbm] * 3,
        out_specs=vmem,
        out_shape=jax.ShapeDtypeStruct((tok + ID_ROWS, 4 * DH), jnp.bfloat16),
        scratch_shapes=[pltpu.VMEM((1, tok), jnp.int32), pltpu.SemaphoreType.DMA((5,))],
        compiler_params=pltpu.CompilerParams(vmem_limit_bytes=8 * 1024 * 1024),
        name="pack_halo",
    )(*(pltpu.with_memory_space_constraint(x, pltpu.HBM) for x in (ids, keys, values)))
    one, two = shifted(sent, 1), shifted(sent, 2)
    q, c, _ = lax.optimization_barrier((q, c, sent))
    rows = pl.pallas_call(
        pack_rows,
        in_specs=[hbm] * 2,
        out_specs=vmem,
        out_shape=jax.ShapeDtypeStruct((2 * tok, 2 * WIDE), jnp.bfloat16),
        scratch_shapes=[pltpu.SemaphoreType.DMA((4,))],
        compiler_params=pltpu.CompilerParams(vmem_limit_bytes=8 * 1024 * 1024),
        name="pack_rows",
    )(*(pltpu.with_memory_space_constraint(x, pltpu.HBM) for x in (q, c)))
    rows = other_core(rows)
    place = jnp.stack([core, y_lo, (me % ROW < 1).astype(core.dtype), (me % ROW < 2).astype(core.dtype)])
    place = place.astype(jnp.int32)
    shared = [
        pl.BlockSpec((tok, DH), own),
        pl.BlockSpec((tok, DH), own),
        pl.BlockSpec((tok + ID_ROWS, 2 * DH), column),
        pl.BlockSpec((tok + ID_ROWS, 2 * DH), column),
    ]
    grads = (pl.BlockSpec((3 * tok, DH), column),) * 2
    params = pltpu.CompilerParams(vmem_limit_bytes=24 * 1024 * 1024)
    grad_q, grad_k, grad_v = pl.pallas_call(
        attend_own,
        grid_spec=pltpu.PrefetchScalarGridSpec(
            num_scalar_prefetch=1,
            grid=(2,),
            in_specs=[
                pl.BlockSpec((1, tok), fixed),
                pl.BlockSpec((tok, WIDE), own),
                pl.BlockSpec((tok, WIDE), own),
                *shared,
            ],
            out_specs=(pl.BlockSpec((tok, WIDE), own), *grads),
        ),
        out_shape=(
            jax.ShapeDtypeStruct(q.shape, jnp.bfloat16),
            jax.ShapeDtypeStruct((3 * tok, 2 * DH), jnp.float32),
            jax.ShapeDtypeStruct((3 * tok, 2 * DH), jnp.float32),
        ),
        compiler_params=params,
        cost_estimate=pl.CostEstimate(flops=OWN_FLOPS, bytes_accessed=0, transcendentals=0),
        name="attend_own",
    )(place, ids, q, c, keys, values, one, two)
    other_q, part = pl.pallas_call(
        attend_other,
        grid_spec=pltpu.PrefetchScalarGridSpec(
            num_scalar_prefetch=1,
            grid=(2,),
            in_specs=[
                pl.BlockSpec((1, tok), fixed),
                pl.BlockSpec((tok, WIDE), column),
                pl.BlockSpec((tok, WIDE), lambda g, at: (1, g)),
                *shared,
                *grads,
            ],
            out_specs=(pl.BlockSpec((tok, WIDE), column), pl.BlockSpec((4, 3 * tok, DH), lambda g, at: (0, 0, 0))),
        ),
        out_shape=(
            jax.ShapeDtypeStruct((tok, 2 * WIDE), jnp.bfloat16),
            jax.ShapeDtypeStruct((4, 3 * tok, DH), jnp.bfloat16),
        ),
        compiler_params=params,
        name="attend_other",
    )(place, ids, rows, rows, keys, values, one, two, grad_k, grad_v)
    shares = [to_owner(part[step], step) for step in range(4)]
    total = sum(share[:tok].astype(jnp.float32) for share in shares)
    back = sum(share[tok:].astype(jnp.float32) for share in shares).astype(jnp.bfloat16)
    back = returned(back)
    swapped = other_core(jnp.concatenate([other_q, jnp.where(core == 0, back[tok:], back[:tok])], 1))
    grad_q, grad_k, grad_v = pl.pallas_call(
        finish,
        in_specs=[vmem, vmem, vmem, hbm],
        out_specs=(hbm, hbm, hbm),
        out_shape=(
            jax.ShapeDtypeStruct(q.shape, jnp.bfloat16),
            jax.ShapeDtypeStruct((DH // 2, tok), jnp.float32),
            jax.ShapeDtypeStruct((DH // 2, tok), jnp.float32),
        ),
        scratch_shapes=[pltpu.VMEM((DH, tok), jnp.float32), pltpu.SemaphoreType.DMA((4,))],
        input_output_aliases={3: 0},
        name="finish",
    )(total, back, swapped, grad_q)
    return (grad_q[None], grad_k.T, grad_v.T)


def solution(mesh):
    placed = (
        P("section", "ctx", None),
        P("ctx", None),
        P("ctx", None),
        P("section", "ctx", None),
        P("ctx"),
    )
    return jax.shard_map(
        on_device,
        mesh=mesh,
        in_specs=placed,
        out_specs=(P("section", "ctx", None), P("ctx", "section"), P("ctx", "section")),
        check_vma=False,
    )
```

time: 72 us -> 64 us (0.89)
  starting transfers between devices: 42.8 us -> 31.8 us
  waiting for transfers between devices: 11.4 us -> 17.2 us
  other arithmetic: 3.33 us -> 0.8 us
    ppermute x11 -> x9, starting transfers between devices: 42.8 us -> 31.8 us  [permuted(): return lax.ppermute(x, AXES, found)]
    ppermute x11 -> x9, waiting for transfers between devices: 11.4 us -> 17.2 us  [permuted(): return lax.ppermute(x, AXES, found)]
    select_n x3 -> x1, other arithmetic: 2.06 us -> 0.01 us  [on_device(): jnp.where(core == 0, back[tok:], back[:tok])]
    pallas_call x4 -> x5, Pallas kernels: 12.1 us -> 11.4 us  [the longest x1 3.95 us: on_device(): pl.pallas_call(attend_own, grid_spec=pltpu.PrefetchScalarGridSpec(num_sca...]
  transfers between devices with their start and end apart: 11 -> 9, of which waited for: 4 -> 5; matrix products, arithmetic and copies ran while one was open for 4% -> 1% of each run, Pallas kernels for 0% -> 8%
where the time goes in v4:
time: 64 us; the launch traced here: 63.5 us
  starting transfers between devices  31.8 us (50%)
  waiting for transfers between devices  17.2 us (27%)
  Pallas kernels  11.4 us (18%)
  local copies, waits for them, and re-layouts  1.37 us (2%)
  between operations  0.85 us (1%)
  other arithmetic  0.8 us (1%)
    ppermute x9, starting transfers between devices, permuted(): return lax.ppermute(x, AXES, found)  31.8 us
    ppermute x9, waiting for transfers between devices, permuted(): return lax.ppermute(x, AXES, found)  17.2 us
    pallas_call x1, Pallas kernels, on_device(): pl.pallas_call(attend_own, grid_spec=pltpu.PrefetchScalarGridSpec(num_sca...  3.95 us
    pallas_call x1, Pallas kernels, on_device(): pl.pallas_call(attend_other, grid_spec=pltpu.PrefetchScalarGridSpec(num_s...  3.46 us
    pallas_call x1, Pallas kernels, on_device(): pl.pallas_call(finish, in_specs=[vmem, vmem, vmem, hbm], out_specs=(hbm,...  1.83 us
    unnamed x14, local copies, waits for them, and re-layouts  1.34 us
    pallas_call x1, Pallas kernels, on_device(): pl.pallas_call(pack_rows, in_specs=[hbm] * 2, out_specs=vmem, out_shape=j...  1.31 us
  transfers between devices with their start and end apart: 9, of which 5 were waited for; matrix products, arithmetic and copies ran while one was open for 1% of the time, Pallas kernels for 8%

profile of v4, /device:TPU:231, one launch (start us, length us, event | category | flops | bytes accessed | tf_op | source)
XLA Modules:
  0.0 63.5 jit_solution(12209117089333554519)
XLA Ops:
  0.6 0.9 %pack_halo.1 = bf16[144,512]{1,0:T(8,128)(2,1)S(1)} custom-call(s32[1,128]{1,0:T(1,128)} %bitcast.22, bf16[128,512]{1,0:T(8,128)(2,1)} %k_ref.5, bf16[128,512]{1,0:T(8,128)(2,1)} %v_ref.5), custom_call_target="tpu_custom_call" | custom-call | tf_op jit(solution)/shard_map/pack_halo/pallas_call | solution.py:205
  1.5 5.9 %collective-permute-start.2 = (bf16[144,512]{1,0:T(8,128)(2,1)S(1)}, bf16[144,512]{1,0:T(8,128)(2,1)S(1)}, u32[]{:S(2)}, u32[]{:S(2)}) collective-permute-start(bf16[144,512]{1,0:T(8,128)(2,1)S(1)} %pack_halo.1), channel_id=1, source_target_pairs={{0,2},{1,3},{2,388},{3,389},{4,6},{5,7},{6,392},{7,393},{8,10},{9,... | collective-permute-start | bytes 442376 | tf_op jit(solution)/shard_map/ppermute | solution.py:31
  7.5 3.7 %collective-permute-start.1 = (bf16[144,512]{1,0:T(8,128)(2,1)S(1)}, bf16[144,512]{1,0:T(8,128)(2,1)S(1)}, u32[]{:S(2)}, u32[]{:S(2)}) collective-permute-start(bf16[144,512]{1,0:T(8,128)(2,1)S(1)} %pack_halo.1), channel_id=1, source_target_pairs={{0,1},{1,2},{2,3},{3,388},{4,5},{5,6},{6,7},{7,392},{8,9},{9,10},{... | collective-permute-start | bytes 442376 | tf_op jit(solution)/shard_map/ppermute | solution.py:31
  11.2 0.0 copy-start
  11.2 0.0 copy-start.1
  11.2 0.0 copy-start.2
  11.2 0.0 copy-start.3
  11.2 1.3 %pack_rows.1 = bf16[256,1280]{1,0:T(8,128)(2,1)S(1)} custom-call(bf16[128,2560]{1,0:T(8,128)(2,1)} %bitcast.18, bf16[128,2560]{1,0:T(8,128)(2,1)} %bitcast.20), custom_call_target="tpu_custom_call" | custom-call | tf_op jit(solution)/shard_map/pack_rows/pallas_call | solution.py:216
  12.6 3.1 %collective-permute-start = (bf16[256,1280]{1,0:T(8,128)(2,1)S(1)}, bf16[256,1280]{1,0:T(8,128)(2,1)S(1)}, u32[]{:S(2)}, u32[]{:S(2)}) collective-permute-start(bf16[256,1280]{1,0:T(8,128)(2,1)S(1)} %pack_rows.1), channel_id=1, source_target_pairs={{0,64},{1,65},{2,66},{3,67},{4,68},{5,69},{6,70},{7,71},{8,72},{9,... | collective-permute-start | bytes 1966088 | tf_op jit(solution)/shard_map/ppermute | solution.py:31
  15.7 0.0 copy-start.4
  15.8 0.1 pad_add_fusion.place_ref
  15.8 0.5 collective-permute-done.2.two_ref
  16.4 3.3 %collective-permute-done.1.one_ref = bf16[144,512]{1,0:T(8,128)(2,1)S(1)} collective-permute-done((bf16[144,512]{1,0:T(8,128)(2,1)S(1)}, bf16[144,512]{1,0:T(8,128)(2,1)S(1)}, u32[]{:S(2)}, u32[]{:S(2)}) %collective-permute-start.1) | collective-permute-done | bytes 147488 | tf_op jit(solution)/shard_map/ppermute | solution.py:31
  19.7 0.0 copy-done
  19.7 0.0 copy-done.1
  19.7 0.0 copy-done.2
  19.7 0.0 copy-done.3
  19.7 0.0 copy-done.4
  19.7 4.0 %attend_own.1 = (bf16[128,2560]{1,0:T(8,128)(2,1)}, f32[384,256]{1,0:T(8,128)S(1)}, f32[384,256]{1,0:T(8,128)S(1)}) custom-call(s32[4]{0:T(128)S(1)} %pad_add_fusion.place_ref, s32[1,128]{1,0:T(1,128)S(1)} %bitcast.23, bf16[128,2560]{1,0:T(8,128)(2,1)S(1)} %bitcast.19, bf16[128,2560]{1,0:T(8,128)(2,1)S(1)} %bitcast.21, bf16[128,512]{1,0:T(8,128)(2,1)S(1)} %copy-done.2, ...), custom_call_target="tpu_custom_call" | custom-call | flops 17179869184 | tf_op jit(solution)/shard_map/attend_own/pallas_call | solution.py:236
  23.7 0.0 collective-permute-done.q_ref.c_ref
  23.7 3.5 %attend_other.1 = (bf16[128,1280]{1,0:T(8,128)(2,1)S(1)}, bf16[4,384,128]{2,1,0:T(8,128)(2,1)S(1)}) custom-call(s32[4]{0:T(128)S(1)} %pad_add_fusion.place_ref, s32[1,128]{1,0:T(1,128)S(1)} %bitcast.24, bf16[256,1280]{1,0:T(8,128)(2,1)S(1)} %collective-permute-done.q_ref.c_ref, bf16[256,1280]{1,0:T(8,128)(2,1)S(1)} %collective-permute-done.q_ref.c_ref, ...), custom_call_target="tpu_custom_call" | custom-call | tf_op jit(solution)/shard_map/attend_other/pallas_call | solution.py:258
  27.2 1.9 %collective-permute-start.3 = (bf16[384,128]{1,0:T(8,128)(2,1)S(1)}, bf16[384,128]{1,0:T(8,128)(2,1)S(1)}, u32[]{:S(2)}, u32[]{:S(2)}) collective-permute-start(bf16[384,128]{1,0:T(8,128)(2,1)S(1)} %get-tuple-element.23), channel_id=1, source_target_pairs={{0,0},{1,1},{2,2},{3,3},{4,4},{5,5},{6,6},{7,7},{8,8},{9,9},{10,10... | collective-permute-start | bytes 294920 | tf_op jit(solution)/shard_map/ppermute | solution.py:31
  29.1 1.9 %collective-permute-start.6 = (bf16[384,128]{1,0:T(8,128)(2,1)S(1)}, bf16[384,128]{1,0:T(8,128)(2,1)S(1)}, u32[]{:S(2)}, u32[]{:S(2)}) collective-permute-start(bf16[384,128]{1,0:T(8,128)(2,1)S(1)} %get-tuple-element.24), channel_id=1, source_target_pairs={{0,448},{1,449},{2,450},{3,451},{4,452},{5,453},{6,454},{7,455},{8... | collective-permute-start | bytes 294920 | tf_op jit(solution)/shard_map/ppermute | solution.py:31
  31.0 4.5 %collective-permute-start.5 = (bf16[384,128]{1,0:T(8,128)(2,1)S(1)}, bf16[384,128]{1,0:T(8,128)(2,1)S(1)}, u32[]{:S(2)}, u32[]{:S(2)}) collective-permute-start(bf16[384,128]{1,0:T(8,128)(2,1)S(1)} %get-tuple-element.25), channel_id=1, source_target_pairs={{0,384},{1,385},{2,386},{3,387},{4,388},{5,389},{6,390},{7,391},{8... | collective-permute-start | bytes 294920 | tf_op jit(solution)/shard_map/ppermute | solution.py:31
  35.6 1.9 %collective-permute-start.4 = (bf16[384,128]{1,0:T(8,128)(2,1)S(1)}, bf16[384,128]{1,0:T(8,128)(2,1)S(1)}, u32[]{:S(2)}, u32[]{:S(2)}) collective-permute-start(bf16[384,128]{1,0:T(8,128)(2,1)S(1)} %get-tuple-element.26), channel_id=1, source_target_pairs={{0,64},{1,65},{2,66},{3,67},{4,68},{5,69},{6,70},{7,71},{8,72},{9,... | collective-permute-start | bytes 294920 | tf_op jit(solution)/shard_map/ppermute | solution.py:31
  37.5 0.0 collective-permute-done.3
  37.5 2.7 %collective-permute-done.6 = bf16[384,128]{1,0:T(8,128)(2,1)S(1)} collective-permute-done((bf16[384,128]{1,0:T(8,128)(2,1)S(1)}, bf16[384,128]{1,0:T(8,128)(2,1)S(1)}, u32[]{:S(2)}, u32[]{:S(2)}) %collective-permute-start.6) | collective-permute-done | bytes 98336 | tf_op jit(solution)/shard_map/ppermute | solution.py:31
  40.2 0.0 collective-permute-done.5
  40.2 0.0 collective-permute-done.4
  40.3 2.2 %collective-permute-start.7 = (bf16[256,128]{1,0:T(8,128)(2,1)S(1)}, bf16[256,128]{1,0:T(8,128)(2,1)S(1)}, u32[]{:S(2)}, u32[]{:S(2)}) collective-permute-start(bf16[256,128]{1,0:T(8,128)(2,1)S(1)} %add_convert_fusion), channel_id=1, source_target_pairs={{1,0},{2,1},{3,2},{4,387},{5,4},{6,5},{7,6},{8,391},{9,8},{10,9},{... | collective-permute-start | bytes 196616 | tf_op jit(solution)/shard_map/ppermute | solution.py:31
  42.4 10.1 %collective-permute-done.7.back_ref = bf16[256,128]{1,0:T(8,128)(2,1)S(1)} collective-permute-done((bf16[256,128]{1,0:T(8,128)(2,1)S(1)}, bf16[256,128]{1,0:T(8,128)(2,1)S(1)}, u32[]{:S(2)}, u32[]{:S(2)}) %collective-permute-start.7) | collective-permute-done | bytes 65568 | tf_op jit(solution)/shard_map/ppermute | solution.py:31
  52.5 0.0 copy-start.6
  52.5 0.6 copy-done.6
  53.1 6.6 %collective-permute-start.8 = (bf16[128,1408]{1,0:T(8,128)(2,1)S(1)}, bf16[128,1408]{1,0:T(8,128)(2,1)S(1)}, u32[]{:S(2)}, u32[]{:S(2)}) collective-permute-start(bf16[128,1408]{1,0:T(8,128)(2,1)S(1)} %pad_maximum_fusion), channel_id=1, source_target_pairs={{0,64},{1,65},{2,66},{3,67},{4,68},{5,69},{6,70},{7,71},{8,72},{9,... | collective-permute-start | bytes 1081352 | tf_op jit(solution)/shard_map/ppermute | solution.py:31
  59.7 0.6 %convert_add_fusion.own_ref = f32[128,128]{1,0:T(8,128)} fusion(bf16[384,128]{1,0:T(8,128)(2,1)S(1)} %collective-permute-done.6, bf16[384,128]{1,0:T(8,128)(2,1)S(1)} %collective-permute-done.5, bf16[384,128]{1,0:T(8,128)(2,1)S(1)} %collective-permute-done.4, bf16[384,128]{1,0:T(8,128)(2,1)S(1)} %collective-permute-done.3), kind=kLoop, calls=%fused_computation.6 | loop fusion | flops 114688 | bytes 196608 | tf_op jit(solution)/shard_map/add | solution.py:280
  60.3 0.6 collective-permute-done.8.swapped_ref
  61.0 0.0 copy-start.5
  61.0 0.7 %copy-done.5 = bf16[128,1408]{1,0:T(8,128)(2,1)} copy-done((bf16[128,1408]{1,0:T(8,128)(2,1)}, bf16[128,1408]{1,0:T(8,128)(2,1)S(1)}, u32[]{:S(2)}) %copy-start.5) | copy-done | bytes 360472
  61.7 1.8 %finish.1 = (bf16[128,2560]{1,0:T(8,128)(2,1)}, f32[64,128]{1,0:T(8,128)}, f32[64,128]{1,0:T(8,128)}) custom-call(f32[128,128]{1,0:T(8,128)} %convert_add_fusion.own_ref, bf16[256,128]{1,0:T(8,128)(2,1)} %copy-done.6, bf16[128,1408]{1,0:T(8,128)(2,1)} %copy-done.5, bf16[128,2560]{1,0:T(8,128)(2,1)} %get-tuple-element.19.dq_in_ref), custom_call_target="tpu_custom_call", output_to_operand_aliasing={{0}: (3, {})} | custom-call | tf_op jit(solution)/shard_map/finish/pallas_call | solution.py:284
  (4 shorter events, 0.1 us)
Async XLA Ops:
  1.5 14.9 %collective-permute-start.2 = (bf16[144,512]{1,0:T(8,128)(2,1)S(1)}, bf16[144,512]{1,0:T(8,128)(2,1)S(1)}, u32[]{:S(2)}, u32[]{:S(2)}) collective-permute-start(bf16[144,512]{1,0:T(8,128)(2,1)S(1)} %pack_halo.1), channel_id=1, source_target_pairs={{0,2},{1,3},{2,388},{3,389},{4,6},{5,7},{6,392},{7,393},{8,10},{9,... | collective-permute-start | bytes 442376 | tf_op jit(solution)/shard_map/ppermute | solution.py:31
  7.5 12.2 %collective-permute-start.1 = (bf16[144,512]{1,0:T(8,128)(2,1)S(1)}, bf16[144,512]{1,0:T(8,128)(2,1)S(1)}, u32[]{:S(2)}, u32[]{:S(2)}) collective-permute-start(bf16[144,512]{1,0:T(8,128)(2,1)S(1)} %pack_halo.1), channel_id=1, source_target_pairs={{0,1},{1,2},{2,3},{3,388},{4,5},{5,6},{6,7},{7,392},{8,9},{9,10},{... | collective-permute-start | bytes 442376 | tf_op jit(solution)/shard_map/ppermute | solution.py:31
  11.2 8.5 %copy-start = (bf16[1,128,2560]{2,1,0:T(8,128)(2,1)S(1)}, bf16[1,128,2560]{2,1,0:T(8,128)(2,1)}, u32[]{:S(2)}) copy-start(bf16[1,128,2560]{2,1,0:T(8,128)(2,1)} %param.5) | copy-start | bytes 1966084
  11.2 8.5 %copy-start.1 = (bf16[1,128,2560]{2,1,0:T(8,128)(2,1)S(1)}, bf16[1,128,2560]{2,1,0:T(8,128)(2,1)}, u32[]{:S(2)}) copy-start(bf16[1,128,2560]{2,1,0:T(8,128)(2,1)} %param.8) | copy-start | bytes 1966084
  11.2 8.5 %copy-start.2 = (bf16[128,512]{1,0:T(8,128)(2,1)S(1)}, bf16[128,512]{1,0:T(8,128)(2,1)}, u32[]{:S(2)}) copy-start(bf16[128,512]{1,0:T(8,128)(2,1)} %k_ref.5) | copy-start | bytes 393220
  11.2 8.5 %copy-start.3 = (bf16[128,512]{1,0:T(8,128)(2,1)S(1)}, bf16[128,512]{1,0:T(8,128)(2,1)}, u32[]{:S(2)}) copy-start(bf16[128,512]{1,0:T(8,128)(2,1)} %v_ref.5) | copy-start | bytes 393220
  12.6 11.1 %collective-permute-start = (bf16[256,1280]{1,0:T(8,128)(2,1)S(1)}, bf16[256,1280]{1,0:T(8,128)(2,1)S(1)}, u32[]{:S(2)}, u32[]{:S(2)}) collective-permute-start(bf16[256,1280]{1,0:T(8,128)(2,1)S(1)} %pack_rows.1), channel_id=1, source_target_pairs={{0,64},{1,65},{2,66},{3,67},{4,68},{5,69},{6,70},{7,71},{8,72},{9,... | collective-permute-start | bytes 1966088 | tf_op jit(solution)/shard_map/ppermute | solution.py:31
  15.7 4.0 %copy-start.4 = (s32[128]{0:T(128)S(1)}, s32[128]{0:T(128)}, u32[]{:S(2)}) copy-start(s32[128]{0:T(128)} %param.9) | copy-start | bytes 1540
  27.2 10.3 %collective-permute-start.3 = (bf16[384,128]{1,0:T(8,128)(2,1)S(1)}, bf16[384,128]{1,0:T(8,128)(2,1)S(1)}, u32[]{:S(2)}, u32[]{:S(2)}) collective-permute-start(bf16[384,128]{1,0:T(8,128)(2,1)S(1)} %get-tuple-element.23), channel_id=1, source_target_pairs={{0,0},{1,1},{2,2},{3,3},{4,4},{5,5},{6,6},{7,7},{8,8},{9,9},{10,10... | collective-permute-start | bytes 294920 | tf_op jit(solution)/shard_map/ppermute | solution.py:31
  29.1 11.1 %collective-permute-start.6 = (bf16[384,128]{1,0:T(8,128)(2,1)S(1)}, bf16[384,128]{1,0:T(8,128)(2,1)S(1)}, u32[]{:S(2)}, u32[]{:S(2)}) collective-permute-start(bf16[384,128]{1,0:T(8,128)(2,1)S(1)} %get-tuple-element.24), channel_id=1, source_target_pairs={{0,448},{1,449},{2,450},{3,451},{4,452},{5,453},{6,454},{7,455},{8... | collective-permute-start | bytes 294920 | tf_op jit(solution)/shard_map/ppermute | solution.py:31
  31.0 9.2 %collective-permute-start.5 = (bf16[384,128]{1,0:T(8,128)(2,1)S(1)}, bf16[384,128]{1,0:T(8,128)(2,1)S(1)}, u32[]{:S(2)}, u32[]{:S(2)}) collective-permute-start(bf16[384,128]{1,0:T(8,128)(2,1)S(1)} %get-tuple-element.25), channel_id=1, source_target_pairs={{0,384},{1,385},{2,386},{3,387},{4,388},{5,389},{6,390},{7,391},{8... | collective-permute-start | bytes 294920 | tf_op jit(solution)/shard_map/ppermute | solution.py:31
  35.6 4.6 %collective-permute-start.4 = (bf16[384,128]{1,0:T(8,128)(2,1)S(1)}, bf16[384,128]{1,0:T(8,128)(2,1)S(1)}, u32[]{:S(2)}, u32[]{:S(2)}) collective-permute-start(bf16[384,128]{1,0:T(8,128)(2,1)S(1)} %get-tuple-element.26), channel_id=1, source_target_pairs={{0,64},{1,65},{2,66},{3,67},{4,68},{5,69},{6,70},{7,71},{8,72},{9,... | collective-permute-start | bytes 294920 | tf_op jit(solution)/shard_map/ppermute | solution.py:31
  40.3 12.2 %collective-permute-start.7 = (bf16[256,128]{1,0:T(8,128)(2,1)S(1)}, bf16[256,128]{1,0:T(8,128)(2,1)S(1)}, u32[]{:S(2)}, u32[]{:S(2)}) collective-permute-start(bf16[256,128]{1,0:T(8,128)(2,1)S(1)} %add_convert_fusion), channel_id=1, source_target_pairs={{1,0},{2,1},{3,2},{4,387},{5,4},{6,5},{7,6},{8,391},{9,8},{10,9},{... | collective-permute-start | bytes 196616 | tf_op jit(solution)/shard_map/ppermute | solution.py:31
  52.5 0.6 copy-start.6
  53.1 7.9 %collective-permute-start.8 = (bf16[128,1408]{1,0:T(8,128)(2,1)S(1)}, bf16[128,1408]{1,0:T(8,128)(2,1)S(1)}, u32[]{:S(2)}, u32[]{:S(2)}) collective-permute-start(bf16[128,1408]{1,0:T(8,128)(2,1)S(1)} %pad_maximum_fusion), channel_id=1, source_target_pairs={{0,64},{1,65},{2,66},{3,67},{4,68},{5,69},{6,70},{7,71},{8,72},{9,... | collective-permute-start | bytes 1081352 | tf_op jit(solution)/shard_map/ppermute | solution.py:31
  61.0 0.7 %copy-start.5 = (bf16[128,1408]{1,0:T(8,128)(2,1)}, bf16[128,1408]{1,0:T(8,128)(2,1)S(1)}, u32[]{:S(2)}) copy-start(bf16[128,1408]{1,0:T(8,128)(2,1)S(1)} %collective-permute-done.8.swapped_ref) | copy-start | bytes 1081348

commit v5 on v4

v5 whole, which is shorter than its diff:
```python
import jax
import jax.numpy as jnp
from jax import lax
from jax.experimental import pallas as pl
from jax.experimental.pallas import tpu as pltpu
from jax.sharding import PartitionSpec as P

DH = 128
TOK = 128
RATIO = 5
WIDE = RATIO * DH
ROW = 4
ID_ROWS = 16
SCALE = DH ** (-0.5)
LOG2E = 1.4426950408889634
NEG = -1e30
MASK_FLOPS = 1 << 34
AXES = ("section", "ctx")
NT = (((1,), (1,)), ((), ()))
TN = (((0,), (0,)), ((), ()))


def permuted(x, target):
    sections, cycle = lax.axis_size("section"), lax.axis_size("ctx")
    found = []
    for s in range(sections):
        for c in range(cycle):
            to = target(s, c)
            if 0 <= to[1] < cycle:
                found.append((s * cycle + c, to[0] * cycle + to[1]))
    return lax.ppermute(x, AXES, found)


def shifted(x, by):
    def target(s, c):
        leaves = c // ROW != (c + by) // ROW
        return ((3 - s // 2) * 2 + s % 2 if leaves else s, c + by)

    return permuted(x, target)


def returned(x):
    def target(s, c):
        to = c - 1 - s % 2
        return ((3 - s // 2) * 2 + s % 2 if c // ROW != to // ROW else s, to)

    return permuted(x, target)


def other_core(x):
    return permuted(x, lambda s, c: (s ^ 1, c))


def group_of(core, slot):
    return core + slot * (3 - 2 * core)


def to_owner(x, step):
    def target(s, c):
        share = (s // 2) ^ step
        return (group_of(s % 2, share // 2) * 2 + share % 2, c)

    return permuted(x, target)


def core_groups(core):
    return [group_of(core, slot) for slot in range(2)]


def columns(group, width):
    return pl.ds(pl.multiple_of(group * width, width), width)


def run(copies):
    for copy in copies:
        copy.start()
    for copy in copies:
        copy.wait()


def pack_halo(ids_ref, k_ref, v_ref, out_ref, ids_vmem, sems):
    copies = [pltpu.make_async_copy(ids_ref, ids_vmem, sems.at[4])]
    for slot, group in enumerate(core_groups(lax.axis_index("section") % 2)):
        for i, ref in enumerate((k_ref, v_ref)):
            to = out_ref.at[pl.ds(0, TOK), pl.ds((2 * slot + i) * DH, DH)]
            copies.append(pltpu.make_async_copy(ref.at[:, columns(group, DH)], to, sems.at[2 * slot + i]))
    run(copies)
    ids = jnp.broadcast_to((ids_vmem[...] + 1).astype(jnp.float32), (ID_ROWS, TOK)).astype(jnp.bfloat16)
    for column in range(4):
        out_ref[TOK:, column * DH : (column + 1) * DH] = ids


def pack_rows(q_ref, c_ref, out_ref, sems):
    copies = []
    for slot, group in enumerate(core_groups(1 - lax.axis_index("section") % 2)):
        for i, ref in enumerate((q_ref, c_ref)):
            to = out_ref.at[pl.ds(i * TOK, TOK), pl.ds(slot * WIDE, WIDE)]
            copies.append(pltpu.make_async_copy(ref.at[:, columns(group, WIDE)], to, sems.at[2 * slot + i]))
    run(copies)


def mask(ids_ref, one_ref, two_ref, out_ref):
    ids = ids_ref[...].astype(jnp.float32)
    first = ids[:, 0:1]
    row = lax.broadcasted_iota(jnp.int32, (TOK, TOK), 0)
    col = lax.broadcasted_iota(jnp.int32, (TOK, TOK), 1)
    wide = jnp.broadcast_to(ids, (TOK, TOK))
    out_ref[:TOK] = jnp.where((wide.T == wide) & (row <= col), 0.0, NEG)
    for block, halo in enumerate((one_ref, two_ref)):
        before = halo[TOK:, :DH].astype(jnp.float32)[0:1]
        held = jnp.sum(jnp.where(before == first + 1.0, 1.0, 0.0), -1, keepdims=True)
        out_ref[(block + 1) * TOK : (block + 2) * TOK] = jnp.where(
            (wide == first) & (row.astype(jnp.float32) >= TOK - held), 0.0, NEG
        )


def attend(place_ref, bias_ref, q_ref, c_ref, oqc_ref, k_ref, v_ref, one_ref, two_ref, dq_ref, odq_ref, part_ref):
    slot = pl.program_id(0)
    group = group_of(place_ref[0], slot)

    def lanes(start, size=DH):
        return pl.ds(pl.multiple_of(start, DH), size)

    keys = jnp.concatenate(
        [k_ref[:, lanes(group * DH)], one_ref[:TOK, lanes(slot * 2 * DH)], two_ref[:TOK, lanes(slot * 2 * DH)]], 0
    )
    values = jnp.concatenate(
        [v_ref[:, lanes(group * DH)], one_ref[:TOK, lanes((slot * 2 + 1) * DH)], two_ref[:TOK, lanes((slot * 2 + 1) * DH)]],
        0,
    )
    bias = bias_ref[...]
    grad_k = jnp.zeros((3 * TOK, DH), jnp.float32)
    grad_v = jnp.zeros((3 * TOK, DH), jnp.float32)
    for mine in (True, False):
        start = (group if mine else slot) * WIDE
        queries, cots = [], []
        for h in range(RATIO):
            at = lanes(start + h * DH)
            queries.append(q_ref[:, at] if mine else oqc_ref[:TOK, at])
            cots.append(c_ref[:, at] if mine else oqc_ref[TOK:, at])
        queries, cots = jnp.concatenate(queries, 0), jnp.concatenate(cots, 0)
        scores = lax.dot_general(keys, queries, NT, preferred_element_type=jnp.float32)
        grad_probs = lax.dot_general(values, cots, NT, preferred_element_type=jnp.float32)
        probs_low, scaled_low = [], []
        for h in range(RATIO):
            at = slice(h * TOK, (h + 1) * TOK)
            s = scores[:, at] * (SCALE * LOG2E) + bias
            e = jnp.exp2(s - jnp.max(s, 0, keepdims=True))
            p = e * (1.0 / jnp.sum(e, 0, keepdims=True))
            low = p.astype(jnp.bfloat16)
            g = grad_probs[:, at]
            dot = jnp.sum(low.astype(jnp.float32) * g, 0, keepdims=True)
            probs_low.append(low)
            scaled_low.append((p * (g - dot) * SCALE).astype(jnp.bfloat16))
        probs_low = jnp.concatenate(probs_low, 1)
        scaled_low = jnp.concatenate(scaled_low, 1)
        grad_v += jnp.dot(probs_low, cots, preferred_element_type=jnp.float32)
        grad_k += jnp.dot(scaled_low, queries, preferred_element_type=jnp.float32)
        grad_q = lax.dot_general(keys, scaled_low, TN, preferred_element_type=jnp.float32)
        out = dq_ref if mine else odq_ref
        for h in range(RATIO):
            out[:, lanes(slot * WIDE + h * DH)] = grad_q[:, h * TOK : (h + 1) * TOK].T.astype(jnp.bfloat16)
    half = DH // 2
    grad_k = grad_k.astype(jnp.bfloat16)
    grad_v = grad_v.astype(jnp.bfloat16)
    shares = (
        jnp.concatenate([grad_k[:, :half], grad_v[:, :half]], 1),
        jnp.concatenate([grad_k[:, half:], grad_v[:, half:]], 1),
    )
    for side in range(2):
        part_ref[(2 * slot + side) ^ place_ref[1], :TOK, :] = shares[side][:TOK]
        for block in (1, 2):
            carrier = 2 * (slot ^ place_ref[1 + block]) + block - 1
            rows = slice((1 + side) * TOK, (2 + side) * TOK)
            part_ref[carrier ^ place_ref[1], rows, :] = shares[side][block * TOK : (block + 1) * TOK]


def finish(own_ref, back_ref, swapped_ref, own_q_ref, dq_ref, dk_ref, dv_ref, total_ref, sems):
    core = lax.axis_index("section") % 2
    half = DH // 2
    copies = []
    for i, ref in enumerate((own_q_ref, swapped_ref)):
        for slot, group in enumerate(core_groups(core if i == 0 else 1 - core)):
            src = ref.at[:, pl.ds(slot * WIDE, WIDE)]
            copies.append(pltpu.make_async_copy(src, dq_ref.at[:, columns(group, WIDE)], sems.at[2 * i + slot]))
    for copy in copies:
        copy.start()
    mine = back_ref[pl.ds(pl.multiple_of(core * TOK, TOK), TOK), :]
    total = own_ref[...] + mine.astype(jnp.float32) + swapped_ref[:, 2 * WIDE :].astype(jnp.float32)
    total_ref[...] = total.T
    for i, ref in enumerate((dk_ref, dv_ref)):
        copies.append(pltpu.make_async_copy(total_ref.at[pl.ds(i * half, half)], ref, sems.at[4 + i]))
        copies[-1].start()
    for copy in copies:
        copy.wait()


def on_device(queries, keys, values, cotangent, segment_ids):
    section, me = lax.axis_index("section"), lax.axis_index("ctx")
    core, y_lo = section % 2, section // 2
    tok = keys.shape[0]
    q, c = queries[0], cotangent[0]
    ids = segment_ids.reshape(1, tok)
    hbm = pl.BlockSpec(memory_space=pltpu.HBM)
    vmem = pl.BlockSpec(memory_space=pltpu.VMEM)

    small = pltpu.CompilerParams(vmem_limit_bytes=4 * 1024 * 1024)

    sent = pl.pallas_call(
        pack_halo,
        in_specs=[hbm] * 3,
        out_specs=vmem,
        out_shape=jax.ShapeDtypeStruct((tok + ID_ROWS, 4 * DH), jnp.bfloat16),
        scratch_shapes=[pltpu.VMEM((1, tok), jnp.int32), pltpu.SemaphoreType.DMA((5,))],
        compiler_params=small,
        name="pack_halo",
    )(*(pltpu.with_memory_space_constraint(x, pltpu.HBM) for x in (ids, keys, values)))
    one, two = shifted(sent, 1), shifted(sent, 2)
    q, c, _ = lax.optimization_barrier((q, c, sent))
    rows = pl.pallas_call(
        pack_rows,
        in_specs=[hbm] * 2,
        out_specs=vmem,
        out_shape=jax.ShapeDtypeStruct((2 * tok, 2 * WIDE), jnp.bfloat16),
        scratch_shapes=[pltpu.SemaphoreType.DMA((4,))],
        compiler_params=small,
        name="pack_rows",
    )(*(pltpu.with_memory_space_constraint(x, pltpu.HBM) for x in (q, c)))
    rows = other_core(rows)
    place = jnp.stack([core, y_lo, (me % ROW < 1).astype(core.dtype), (me % ROW < 2).astype(core.dtype)])
    place = place.astype(jnp.int32)
    bias = pl.pallas_call(
        mask,
        in_specs=[vmem] * 3,
        out_specs=vmem,
        out_shape=jax.ShapeDtypeStruct((3 * tok, tok), jnp.float32),
        compiler_params=small,
        cost_estimate=pl.CostEstimate(flops=MASK_FLOPS, bytes_accessed=0, transcendentals=0),
        name="mask",
    )(ids, one, two)
    own_q, other_q, part = pl.pallas_call(
        attend,
        grid=(2,),
        in_specs=[pl.BlockSpec(memory_space=pltpu.SMEM)] + [vmem] * 8,
        out_specs=(vmem,) * 3,
        out_shape=(
            jax.ShapeDtypeStruct((tok, 2 * WIDE), jnp.bfloat16),
            jax.ShapeDtypeStruct((tok, 2 * WIDE), jnp.bfloat16),
            jax.ShapeDtypeStruct((4, 3 * tok, DH), jnp.bfloat16),
        ),
        compiler_params=pltpu.CompilerParams(vmem_limit_bytes=24 * 1024 * 1024),
        name="attend",
    )(place, bias, q, c, rows, keys, values, one, two)
    shares = [to_owner(part[step], step) for step in range(4)]
    total = sum(share[:tok].astype(jnp.float32) for share in shares)
    back = sum(share[tok:].astype(jnp.float32) for share in shares).astype(jnp.bfloat16)
    back = returned(back)
    swapped = other_core(jnp.concatenate([other_q, jnp.where(core == 0, back[tok:], back[:tok])], 1))
    grad_q, grad_k, grad_v = pl.pallas_call(
        finish,
        in_specs=[vmem] * 4,
        out_specs=(hbm, hbm, hbm),
        out_shape=(
            jax.ShapeDtypeStruct(q.shape, jnp.bfloat16),
            jax.ShapeDtypeStruct((DH // 2, tok), jnp.float32),
            jax.ShapeDtypeStruct((DH // 2, tok), jnp.float32),
        ),
        scratch_shapes=[pltpu.VMEM((DH, tok), jnp.float32), pltpu.SemaphoreType.DMA((6,))],
        compiler_params=small,
        name="finish",
    )(total, back, swapped, own_q)
    return (grad_q[None], grad_k.T, grad_v.T)


def solution(mesh):
    placed = (
        P("section", "ctx", None),
        P("ctx", None),
        P("ctx", None),
        P("section", "ctx", None),
        P("ctx"),
    )
    return jax.shard_map(
        on_device,
        mesh=mesh,
        in_specs=placed,
        out_specs=(P("section", "ctx", None), P("ctx", "section"), P("ctx", "section")),
        check_vma=False,
    )
```

time: 64 us -> 59.7 us (0.933)
  Pallas kernels: 11.4 us -> 8.29 us
  local copies, waits for them, and re-layouts: 1.37 us -> 0.05 us
  waiting for transfers between devices: 17.2 us -> 18 us
    pallas_call x3, Pallas kernels: 9.25 us -> 6.21 us  [the longest x1 5.15 us: on_device(): pl.pallas_call(attend, grid=(2,), in_specs=[pl.BlockSpec(memory_space=plt...]
    unnamed x14 -> x10, local copies, waits for them, and re-layouts: 1.34 us -> 0.02 us
    ppermute x9, waiting for transfers between devices: 17.2 us -> 18 us  [permuted(): return lax.ppermute(x, AXES, found)]
  transfers between devices with their start and end apart: 9 -> 9, of which waited for: 5 -> 5; matrix products, arithmetic and copies ran while one was open for 1% -> 0% of each run, Pallas kernels for 8% -> 2%
where the time goes in v5:
time: 59.7 us; the launch traced here: 59.2 us
  starting transfers between devices  31.8 us (53%)
  waiting for transfers between devices  18 us (30%)
  Pallas kernels  8.29 us (14%)
  between operations  0.86 us (1%)
    ppermute x9, starting transfers between devices, permuted(): return lax.ppermute(x, AXES, found)  31.8 us
    ppermute x9, waiting for transfers between devices, permuted(): return lax.ppermute(x, AXES, found)  18 us
    pallas_call x1, Pallas kernels, on_device(): pl.pallas_call(attend, grid=(2,), in_specs=[pl.BlockSpec(memory_space=plt...  5.15 us
    pallas_call x1, Pallas kernels, on_device(): pl.pallas_call(pack_rows, in_specs=[hbm] * 2, out_specs=vmem, out_shape=j...  1.21 us
  transfers between devices with their start and end apart: 9, of which 5 were waited for; matrix products, arithmetic and copies ran while one was open for 0% of the time, Pallas kernels for 2%

profile of v5, /device:TPU:231, one launch (start us, length us, event | category | flops | bytes accessed | tf_op | source)
XLA Modules:
  0.0 59.2 jit_solution(1351638185750157482)
XLA Ops:
  0.6 0.9 %pack_halo.1 = bf16[144,512]{1,0:T(8,128)(2,1)S(1)} custom-call(s32[1,128]{1,0:T(1,128)} %bitcast.22, bf16[128,512]{1,0:T(8,128)(2,1)} %k_ref.3, bf16[128,512]{1,0:T(8,128)(2,1)} %v_ref.3), custom_call_target="tpu_custom_call" | custom-call | tf_op jit(solution)/shard_map/pack_halo/pallas_call | solution.py:209
  1.5 5.9 %collective-permute-start.1 = (bf16[144,512]{1,0:T(8,128)(2,1)S(1)}, bf16[144,512]{1,0:T(8,128)(2,1)S(1)}, u32[]{:S(2)}, u32[]{:S(2)}) collective-permute-start(bf16[144,512]{1,0:T(8,128)(2,1)S(1)} %pack_halo.1), channel_id=1, source_target_pairs={{0,2},{1,3},{2,388},{3,389},{4,6},{5,7},{6,392},{7,393},{8,10},{9,... | collective-permute-start | bytes 442376 | tf_op jit(solution)/shard_map/ppermute | solution.py:31
  7.5 3.7 %collective-permute-start = (bf16[144,512]{1,0:T(8,128)(2,1)S(1)}, bf16[144,512]{1,0:T(8,128)(2,1)S(1)}, u32[]{:S(2)}, u32[]{:S(2)}) collective-permute-start(bf16[144,512]{1,0:T(8,128)(2,1)S(1)} %pack_halo.1), channel_id=1, source_target_pairs={{0,1},{1,2},{2,3},{3,388},{4,5},{5,6},{6,7},{7,392},{8,9},{9,10},{... | collective-permute-start | bytes 442376 | tf_op jit(solution)/shard_map/ppermute | solution.py:31
  11.2 1.2 %pack_rows.1 = bf16[256,1280]{1,0:T(8,128)(2,1)S(1)} custom-call(bf16[128,2560]{1,0:T(8,128)(2,1)} %bitcast.18, bf16[128,2560]{1,0:T(8,128)(2,1)} %bitcast.20), custom_call_target="tpu_custom_call" | custom-call | tf_op jit(solution)/shard_map/pack_rows/pallas_call | solution.py:220
  12.4 3.1 %collective-permute-start.2 = (bf16[256,1280]{1,0:T(8,128)(2,1)S(1)}, bf16[256,1280]{1,0:T(8,128)(2,1)S(1)}, u32[]{:S(2)}, u32[]{:S(2)}) collective-permute-start(bf16[256,1280]{1,0:T(8,128)(2,1)S(1)} %pack_rows.1), channel_id=1, source_target_pairs={{0,64},{1,65},{2,66},{3,67},{4,68},{5,69},{6,70},{7,71},{8,72},{9,... | collective-permute-start | bytes 1966088 | tf_op jit(solution)/shard_map/ppermute | solution.py:31
  15.6 0.0 copy-start.4
  15.6 0.1 pad_add_fusion.place_ref
  15.7 0.0 copy-start
  15.7 0.0 copy-start.1
  15.7 0.0 copy-start.2
  15.7 0.0 copy-start.3
  15.7 0.7 %collective-permute-done.1.two_ref = bf16[144,512]{1,0:T(8,128)(2,1)S(1)} collective-permute-done((bf16[144,512]{1,0:T(8,128)(2,1)S(1)}, bf16[144,512]{1,0:T(8,128)(2,1)S(1)}, u32[]{:S(2)}, u32[]{:S(2)}) %collective-permute-start.1) | collective-permute-done | bytes 147488 | tf_op jit(solution)/shard_map/ppermute | solution.py:31
  16.4 3.3 %collective-permute-done.one_ref = bf16[144,512]{1,0:T(8,128)(2,1)S(1)} collective-permute-done((bf16[144,512]{1,0:T(8,128)(2,1)S(1)}, bf16[144,512]{1,0:T(8,128)(2,1)S(1)}, u32[]{:S(2)}, u32[]{:S(2)}) %collective-permute-start) | collective-permute-done | bytes 147488 | tf_op jit(solution)/shard_map/ppermute | solution.py:31
  19.7 0.0 copy-done.4
  19.7 0.2 mask.1.bias_ref
  19.9 0.0 collective-permute-done.2.oqc_ref
  19.9 0.0 copy-done
  19.9 0.0 copy-done.1
  19.9 0.0 copy-done.2
  19.9 0.0 copy-done.3
  19.9 5.1 %attend.1 = (bf16[128,1280]{1,0:T(8,128)(2,1)S(1)}, bf16[128,1280]{1,0:T(8,128)(2,1)S(1)}, bf16[4,384,128]{2,1,0:T(8,128)(2,1)S(1)}) custom-call(s32[4]{0:T(128)S(1)} %pad_add_fusion.place_ref, f32[384,128]{1,0:T(8,128)S(1)} %mask.1.bias_ref, bf16[128,2560]{1,0:T(8,128)(2,1)S(1)} %bitcast.19, bf16[128,2560]{1,0:T(8,128)(2,1)S(1)} %bitcast.21, ...), custom_call_target="tpu_custom_call" | custom-call | tf_op jit(solution)/shard_map/attend/pallas_call | solution.py:241
  25.1 1.9 %collective-permute-start.3 = (bf16[384,128]{1,0:T(8,128)(2,1)S(1)}, bf16[384,128]{1,0:T(8,128)(2,1)S(1)}, u32[]{:S(2)}, u32[]{:S(2)}) collective-permute-start(bf16[384,128]{1,0:T(8,128)(2,1)S(1)} %get-tuple-element.19), channel_id=1, source_target_pairs={{0,0},{1,1},{2,2},{3,3},{4,4},{5,5},{6,6},{7,7},{8,8},{9,9},{10,10... | collective-permute-start | bytes 294920 | tf_op jit(solution)/shard_map/ppermute | solution.py:31
  27.0 1.9 %collective-permute-start.6 = (bf16[384,128]{1,0:T(8,128)(2,1)S(1)}, bf16[384,128]{1,0:T(8,128)(2,1)S(1)}, u32[]{:S(2)}, u32[]{:S(2)}) collective-permute-start(bf16[384,128]{1,0:T(8,128)(2,1)S(1)} %get-tuple-element.20), channel_id=1, source_target_pairs={{0,448},{1,449},{2,450},{3,451},{4,452},{5,453},{6,454},{7,455},{8... | collective-permute-start | bytes 294920 | tf_op jit(solution)/shard_map/ppermute | solution.py:31
  29.0 4.5 %collective-permute-start.5 = (bf16[384,128]{1,0:T(8,128)(2,1)S(1)}, bf16[384,128]{1,0:T(8,128)(2,1)S(1)}, u32[]{:S(2)}, u32[]{:S(2)}) collective-permute-start(bf16[384,128]{1,0:T(8,128)(2,1)S(1)} %get-tuple-element.21), channel_id=1, source_target_pairs={{0,384},{1,385},{2,386},{3,387},{4,388},{5,389},{6,390},{7,391},{8... | collective-permute-start | bytes 294920 | tf_op jit(solution)/shard_map/ppermute | solution.py:31
  33.5 1.9 %collective-permute-start.4 = (bf16[384,128]{1,0:T(8,128)(2,1)S(1)}, bf16[384,128]{1,0:T(8,128)(2,1)S(1)}, u32[]{:S(2)}, u32[]{:S(2)}) collective-permute-start(bf16[384,128]{1,0:T(8,128)(2,1)S(1)} %get-tuple-element.22), channel_id=1, source_target_pairs={{0,64},{1,65},{2,66},{3,67},{4,68},{5,69},{6,70},{7,71},{8,72},{9,... | collective-permute-start | bytes 294920 | tf_op jit(solution)/shard_map/ppermute | solution.py:31
  35.4 0.0 collective-permute-done.3
  35.4 2.7 %collective-permute-done.6 = bf16[384,128]{1,0:T(8,128)(2,1)S(1)} collective-permute-done((bf16[384,128]{1,0:T(8,128)(2,1)S(1)}, bf16[384,128]{1,0:T(8,128)(2,1)S(1)}, u32[]{:S(2)}, u32[]{:S(2)}) %collective-permute-start.6) | collective-permute-done | bytes 98336 | tf_op jit(solution)/shard_map/ppermute | solution.py:31
  38.1 0.0 collective-permute-done.5
  38.1 0.0 collective-permute-done.4
  38.2 2.1 %collective-permute-start.7 = (bf16[256,128]{1,0:T(8,128)(2,1)S(1)}, bf16[256,128]{1,0:T(8,128)(2,1)S(1)}, u32[]{:S(2)}, u32[]{:S(2)}) collective-permute-start(bf16[256,128]{1,0:T(8,128)(2,1)S(1)} %add_convert_fusion), channel_id=1, source_target_pairs={{1,0},{2,1},{3,2},{4,387},{5,4},{6,5},{7,6},{8,391},{9,8},{10,9},{... | collective-permute-start | bytes 196616 | tf_op jit(solution)/shard_map/ppermute | solution.py:31
  40.3 10.1 %collective-permute-done.7.back_ref = bf16[256,128]{1,0:T(8,128)(2,1)S(1)} collective-permute-done((bf16[256,128]{1,0:T(8,128)(2,1)S(1)}, bf16[256,128]{1,0:T(8,128)(2,1)S(1)}, u32[]{:S(2)}, u32[]{:S(2)}) %collective-permute-start.7) | collective-permute-done | bytes 65568 | tf_op jit(solution)/shard_map/ppermute | solution.py:31
  50.4 6.6 %collective-permute-start.8 = (bf16[128,1408]{1,0:T(8,128)(2,1)S(1)}, bf16[128,1408]{1,0:T(8,128)(2,1)S(1)}, u32[]{:S(2)}, u32[]{:S(2)}) collective-permute-start(bf16[128,1408]{1,0:T(8,128)(2,1)S(1)} %pad_maximum_fusion), channel_id=1, source_target_pairs={{0,64},{1,65},{2,66},{3,67},{4,68},{5,69},{6,70},{7,71},{8,72},{9,... | collective-permute-start | bytes 1081352 | tf_op jit(solution)/shard_map/ppermute | solution.py:31
  57.1 1.3 %collective-permute-done.8.swapped_ref = bf16[128,1408]{1,0:T(8,128)(2,1)S(1)} collective-permute-done((bf16[128,1408]{1,0:T(8,128)(2,1)S(1)}, bf16[128,1408]{1,0:T(8,128)(2,1)S(1)}, u32[]{:S(2)}, u32[]{:S(2)}) %collective-permute-start.8) | collective-permute-done | bytes 360480 | tf_op jit(solution)/shard_map/ppermute | solution.py:31
  58.3 0.9 %finish.1 = (bf16[128,2560]{1,0:T(8,128)(2,1)}, f32[64,128]{1,0:T(8,128)}, f32[64,128]{1,0:T(8,128)}) custom-call(f32[128,128]{1,0:T(8,128)S(1)} %convert_add_fusion.own_ref, bf16[256,128]{1,0:T(8,128)(2,1)S(1)} %collective-permute-done.7.back_ref, bf16[128,1408]{1,0:T(8,128)(2,1)S(1)} %collective-permute-done.8.swapped_ref, ...), custom_call_target="tpu_custom_call" | custom-call | tf_op jit(solution)/shard_map/finish/pallas_call | solution.py:259
  (5 shorter events, 0.1 us)
Async XLA Ops:
  1.5 14.9 %collective-permute-start.1 = (bf16[144,512]{1,0:T(8,128)(2,1)S(1)}, bf16[144,512]{1,0:T(8,128)(2,1)S(1)}, u32[]{:S(2)}, u32[]{:S(2)}) collective-permute-start(bf16[144,512]{1,0:T(8,128)(2,1)S(1)} %pack_halo.1), channel_id=1, source_target_pairs={{0,2},{1,3},{2,388},{3,389},{4,6},{5,7},{6,392},{7,393},{8,10},{9,... | collective-permute-start | bytes 442376 | tf_op jit(solution)/shard_map/ppermute | solution.py:31
  7.5 12.2 %collective-permute-start = (bf16[144,512]{1,0:T(8,128)(2,1)S(1)}, bf16[144,512]{1,0:T(8,128)(2,1)S(1)}, u32[]{:S(2)}, u32[]{:S(2)}) collective-permute-start(bf16[144,512]{1,0:T(8,128)(2,1)S(1)} %pack_halo.1), channel_id=1, source_target_pairs={{0,1},{1,2},{2,3},{3,388},{4,5},{5,6},{6,7},{7,392},{8,9},{9,10},{... | collective-permute-start | bytes 442376 | tf_op jit(solution)/shard_map/ppermute | solution.py:31
  12.4 7.5 %collective-permute-start.2 = (bf16[256,1280]{1,0:T(8,128)(2,1)S(1)}, bf16[256,1280]{1,0:T(8,128)(2,1)S(1)}, u32[]{:S(2)}, u32[]{:S(2)}) collective-permute-start(bf16[256,1280]{1,0:T(8,128)(2,1)S(1)} %pack_rows.1), channel_id=1, source_target_pairs={{0,64},{1,65},{2,66},{3,67},{4,68},{5,69},{6,70},{7,71},{8,72},{9,... | collective-permute-start | bytes 1966088 | tf_op jit(solution)/shard_map/ppermute | solution.py:31
  15.6 4.1 %copy-start.4 = (s32[128]{0:T(128)S(1)}, s32[128]{0:T(128)}, u32[]{:S(2)}) copy-start(s32[128]{0:T(128)} %param.9) | copy-start | bytes 1540
  15.7 4.2 %copy-start = (bf16[1,128,2560]{2,1,0:T(8,128)(2,1)S(1)}, bf16[1,128,2560]{2,1,0:T(8,128)(2,1)}, u32[]{:S(2)}) copy-start(bf16[1,128,2560]{2,1,0:T(8,128)(2,1)} %param.5) | copy-start | bytes 1966084
  15.7 4.2 %copy-start.1 = (bf16[1,128,2560]{2,1,0:T(8,128)(2,1)S(1)}, bf16[1,128,2560]{2,1,0:T(8,128)(2,1)}, u32[]{:S(2)}) copy-start(bf16[1,128,2560]{2,1,0:T(8,128)(2,1)} %param.8) | copy-start | bytes 1966084
  15.7 4.2 %copy-start.2 = (bf16[128,512]{1,0:T(8,128)(2,1)S(1)}, bf16[128,512]{1,0:T(8,128)(2,1)}, u32[]{:S(2)}) copy-start(bf16[128,512]{1,0:T(8,128)(2,1)} %k_ref.3) | copy-start | bytes 393220
  15.7 4.2 %copy-start.3 = (bf16[128,512]{1,0:T(8,128)(2,1)S(1)}, bf16[128,512]{1,0:T(8,128)(2,1)}, u32[]{:S(2)}) copy-start(bf16[128,512]{1,0:T(8,128)(2,1)} %v_ref.3) | copy-start | bytes 393220
  25.1 10.3 %collective-permute-start.3 = (bf16[384,128]{1,0:T(8,128)(2,1)S(1)}, bf16[384,128]{1,0:T(8,128)(2,1)S(1)}, u32[]{:S(2)}, u32[]{:S(2)}) collective-permute-start(bf16[384,128]{1,0:T(8,128)(2,1)S(1)} %get-tuple-element.19), channel_id=1, source_target_pairs={{0,0},{1,1},{2,2},{3,3},{4,4},{5,5},{6,6},{7,7},{8,8},{9,9},{10,10... | collective-permute-start | bytes 294920 | tf_op jit(solution)/shard_map/ppermute | solution.py:31
  27.0 11.1 %collective-permute-start.6 = (bf16[384,128]{1,0:T(8,128)(2,1)S(1)}, bf16[384,128]{1,0:T(8,128)(2,1)S(1)}, u32[]{:S(2)}, u32[]{:S(2)}) collective-permute-start(bf16[384,128]{1,0:T(8,128)(2,1)S(1)} %get-tuple-element.20), channel_id=1, source_target_pairs={{0,448},{1,449},{2,450},{3,451},{4,452},{5,453},{6,454},{7,455},{8... | collective-permute-start | bytes 294920 | tf_op jit(solution)/shard_map/ppermute | solution.py:31
  29.0 9.2 %collective-permute-start.5 = (bf16[384,128]{1,0:T(8,128)(2,1)S(1)}, bf16[384,128]{1,0:T(8,128)(2,1)S(1)}, u32[]{:S(2)}, u32[]{:S(2)}) collective-permute-start(bf16[384,128]{1,0:T(8,128)(2,1)S(1)} %get-tuple-element.21), channel_id=1, source_target_pairs={{0,384},{1,385},{2,386},{3,387},{4,388},{5,389},{6,390},{7,391},{8... | collective-permute-start | bytes 294920 | tf_op jit(solution)/shard_map/ppermute | solution.py:31
  33.5 4.6 %collective-permute-start.4 = (bf16[384,128]{1,0:T(8,128)(2,1)S(1)}, bf16[384,128]{1,0:T(8,128)(2,1)S(1)}, u32[]{:S(2)}, u32[]{:S(2)}) collective-permute-start(bf16[384,128]{1,0:T(8,128)(2,1)S(1)} %get-tuple-element.22), channel_id=1, source_target_pairs={{0,64},{1,65},{2,66},{3,67},{4,68},{5,69},{6,70},{7,71},{8,72},{9,... | collective-permute-start | bytes 294920 | tf_op jit(solution)/shard_map/ppermute | solution.py:31
  38.2 12.2 %collective-permute-start.7 = (bf16[256,128]{1,0:T(8,128)(2,1)S(1)}, bf16[256,128]{1,0:T(8,128)(2,1)S(1)}, u32[]{:S(2)}, u32[]{:S(2)}) collective-permute-start(bf16[256,128]{1,0:T(8,128)(2,1)S(1)} %add_convert_fusion), channel_id=1, source_target_pairs={{1,0},{2,1},{3,2},{4,387},{5,4},{6,5},{7,6},{8,391},{9,8},{10,9},{... | collective-permute-start | bytes 196616 | tf_op jit(solution)/shard_map/ppermute | solution.py:31
  50.4 7.9 %collective-permute-start.8 = (bf16[128,1408]{1,0:T(8,128)(2,1)S(1)}, bf16[128,1408]{1,0:T(8,128)(2,1)S(1)}, u32[]{:S(2)}, u32[]{:S(2)}) collective-permute-start(bf16[128,1408]{1,0:T(8,128)(2,1)S(1)} %pad_maximum_fusion), channel_id=1, source_target_pairs={{0,64},{1,65},{2,66},{3,67},{4,68},{5,69},{6,70},{7,71},{8,72},{9,... | collective-permute-start | bytes 1081352 | tf_op jit(solution)/shard_map/ppermute | solution.py:31

commit v6 on v5

--- a/solution.py
+++ b/solution.py
@@ -14,7 +14,7 @@
 SCALE = DH ** (-0.5)
 LOG2E = 1.4426950408889634
 NEG = -1e30
-MASK_FLOPS = 1 << 34
+MASK_FLOPS = 9 << 29
 AXES = ("section", "ctx")
 NT = (((1,), (1,)), ((), ()))
 TN = (((0,), (0,)), ((), ()))
@@ -31,8 +31,10 @@
     return lax.ppermute(x, AXES, found)
 
 
-def shifted(x, by):
+def shifted(x, by, places=range(ROW)):
     def target(s, c):
+        if (c + by) % ROW not in places:
+            return (s, -1)
         leaves = c // ROW != (c + by) // ROW
         return ((3 - s // 2) * 2 + s % 2 if leaves else s, c + by)
 
@@ -82,12 +84,11 @@
     copies = [pltpu.make_async_copy(ids_ref, ids_vmem, sems.at[4])]
     for slot, group in enumerate(core_groups(lax.axis_index("section") % 2)):
         for i, ref in enumerate((k_ref, v_ref)):
-            to = out_ref.at[pl.ds(0, TOK), pl.ds((2 * slot + i) * DH, DH)]
+            to = out_ref.at[pl.ds((2 * slot + i) * TOK, TOK)]
             copies.append(pltpu.make_async_copy(ref.at[:, columns(group, DH)], to, sems.at[2 * slot + i]))
     run(copies)
-    ids = jnp.broadcast_to((ids_vmem[...] + 1).astype(jnp.float32), (ID_ROWS, TOK)).astype(jnp.bfloat16)
-    for column in range(4):
-        out_ref[TOK:, column * DH : (column + 1) * DH] = ids
+    ids = jnp.broadcast_to((ids_vmem[...] + 1).astype(jnp.float32), (ID_ROWS, TOK))
+    out_ref[4 * TOK :] = ids.astype(jnp.bfloat16)
 
 
 def pack_rows(q_ref, c_ref, out_ref, sems):
@@ -99,35 +100,37 @@
     run(copies)
 
 
-def mask(ids_ref, one_ref, two_ref, out_ref):
+def mask(ids_ref, one_ref, two_ref, relay_ref, out_ref):
     ids = ids_ref[...].astype(jnp.float32)
     first = ids[:, 0:1]
     row = lax.broadcasted_iota(jnp.int32, (TOK, TOK), 0)
     col = lax.broadcasted_iota(jnp.int32, (TOK, TOK), 1)
     wide = jnp.broadcast_to(ids, (TOK, TOK))
     out_ref[:TOK] = jnp.where((wide.T == wide) & (row <= col), 0.0, NEG)
-    for block, halo in enumerate((one_ref, two_ref)):
-        before = halo[TOK:, :DH].astype(jnp.float32)[0:1]
+    for block, halos in enumerate(((one_ref,), (two_ref, relay_ref))):
+        before = sum(halo[4 * TOK :].astype(jnp.float32)[0:1] for halo in halos)
         held = jnp.sum(jnp.where(before == first + 1.0, 1.0, 0.0), -1, keepdims=True)
         out_ref[(block + 1) * TOK : (block + 2) * TOK] = jnp.where(
             (wide == first) & (row.astype(jnp.float32) >= TOK - held), 0.0, NEG
         )
 
 
-def attend(place_ref, bias_ref, q_ref, c_ref, oqc_ref, k_ref, v_ref, one_ref, two_ref, dq_ref, odq_ref, part_ref):
+def attend(
+    place_ref, bias_ref, q_ref, c_ref, oqc_ref, k_ref, v_ref, one_ref, two_ref, relay_ref, dq_ref, odq_ref, part_ref
+):
     slot = pl.program_id(0)
     group = group_of(place_ref[0], slot)
 
     def lanes(start, size=DH):
         return pl.ds(pl.multiple_of(start, DH), size)
 
-    keys = jnp.concatenate(
-        [k_ref[:, lanes(group * DH)], one_ref[:TOK, lanes(slot * 2 * DH)], two_ref[:TOK, lanes(slot * 2 * DH)]], 0
-    )
-    values = jnp.concatenate(
-        [v_ref[:, lanes(group * DH)], one_ref[:TOK, lanes((slot * 2 + 1) * DH)], two_ref[:TOK, lanes((slot * 2 + 1) * DH)]],
-        0,
-    )
+    def rows(i):
+        return pl.ds(pl.multiple_of((2 * slot + i) * TOK, TOK), TOK)
+
+    keys, values = [
+        jnp.concatenate([ref[:, lanes(group * DH)], one_ref[rows(i)], two_ref[rows(i)] + relay_ref[rows(i)]], 0)
+        for i, ref in enumerate((k_ref, v_ref))
+    ]
     bias = bias_ref[...]
     grad_k = jnp.zeros((3 * TOK, DH), jnp.float32)
     grad_v = jnp.zeros((3 * TOK, DH), jnp.float32)
@@ -171,8 +174,8 @@
         part_ref[(2 * slot + side) ^ place_ref[1], :TOK, :] = shares[side][:TOK]
         for block in (1, 2):
             carrier = 2 * (slot ^ place_ref[1 + block]) + block - 1
-            rows = slice((1 + side) * TOK, (2 + side) * TOK)
-            part_ref[carrier ^ place_ref[1], rows, :] = shares[side][block * TOK : (block + 1) * TOK]
+            at = slice((1 + side) * TOK, (2 + side) * TOK)
+            part_ref[carrier ^ place_ref[1], at, :] = shares[side][block * TOK : (block + 1) * TOK]
 
 
 def finish(own_ref, back_ref, swapped_ref, own_q_ref, dq_ref, dk_ref, dv_ref, total_ref, sems):
@@ -210,12 +213,13 @@
         pack_halo,
         in_specs=[hbm] * 3,
         out_specs=vmem,
-        out_shape=jax.ShapeDtypeStruct((tok + ID_ROWS, 4 * DH), jnp.bfloat16),
+        out_shape=jax.ShapeDtypeStruct((4 * tok + ID_ROWS, DH), jnp.bfloat16),
         scratch_shapes=[pltpu.VMEM((1, tok), jnp.int32), pltpu.SemaphoreType.DMA((5,))],
         compiler_params=small,
         name="pack_halo",
     )(*(pltpu.with_memory_space_constraint(x, pltpu.HBM) for x in (ids, keys, values)))
-    one, two = shifted(sent, 1), shifted(sent, 2)
+    one, two = shifted(sent, 1), shifted(sent, 2, (0, 2, 3))
+    relay = shifted(one, 1, (1,))
     q, c, _ = lax.optimization_barrier((q, c, sent))
     rows = pl.pallas_call(
         pack_rows,
@@ -231,17 +235,17 @@
     place = place.astype(jnp.int32)
     bias = pl.pallas_call(
         mask,
-        in_specs=[vmem] * 3,
+        in_specs=[vmem] * 4,
         out_specs=vmem,
         out_shape=jax.ShapeDtypeStruct((3 * tok, tok), jnp.float32),
         compiler_params=small,
         cost_estimate=pl.CostEstimate(flops=MASK_FLOPS, bytes_accessed=0, transcendentals=0),
         name="mask",
-    )(ids, one, two)
+    )(ids, one, two, relay)
     own_q, other_q, part = pl.pallas_call(
         attend,
         grid=(2,),
-        in_specs=[pl.BlockSpec(memory_space=pltpu.SMEM)] + [vmem] * 8,
+        in_specs=[pl.BlockSpec(memory_space=pltpu.SMEM)] + [vmem] * 9,
         out_specs=(vmem,) * 3,
         out_shape=(
             jax.ShapeDtypeStruct((tok, 2 * WIDE), jnp.bfloat16),
@@ -250,7 +254,7 @@
         ),
         compiler_params=pltpu.CompilerParams(vmem_limit_bytes=24 * 1024 * 1024),
         name="attend",
-    )(place, bias, q, c, rows, keys, values, one, two)
+    )(place, bias, q, c, rows, keys, values, one, two, relay)
     shares = [to_owner(part[step], step) for step in range(4)]
     total = sum(share[:tok].astype(jnp.float32) for share in shares)
     back = sum(share[tok:].astype(jnp.float32) for share in shares).astype(jnp.bfloat16)

time: 59.7 us -> 59.7 us (level)
    ppermute x9 -> x10, waiting for transfers between devices: 18 us -> 17.6 us  [permuted(): return lax.ppermute(x, AXES, found)]
    ppermute x9 -> x10, starting transfers between devices: 31.8 us -> 32.2 us  [permuted(): return lax.ppermute(x, AXES, found)]
  transfers between devices with their start and end apart: 9 -> 10, of which waited for: 5 -> 4; matrix products, arithmetic and copies ran while one was open for 0% -> 0% of each run, Pallas kernels for 2% -> 2%
where the time goes in v6:
time: 59.7 us; the launch traced here: 59.2 us
  starting transfers between devices  32.2 us (54%)
  waiting for transfers between devices  17.6 us (29%)
  Pallas kernels  8.32 us (14%)
  between operations  0.88 us (1%)
    ppermute x10, starting transfers between devices, permuted(): return lax.ppermute(x, AXES, found)  32.2 us
    ppermute x10, waiting for transfers between devices, permuted(): return lax.ppermute(x, AXES, found)  17.6 us
    pallas_call x1, Pallas kernels, on_device(): pl.pallas_call(attend, grid=(2,), in_specs=[pl.BlockSpec(memory_space=plt...  5.17 us
    pallas_call x1, Pallas kernels, on_device(): pl.pallas_call(pack_rows, in_specs=[hbm] * 2, out_specs=vmem, out_shape=j...  1.21 us
  transfers between devices with their start and end apart: 10, of which 4 were waited for; matrix products, arithmetic and copies ran while one was open for 0% of the time, Pallas kernels for 2%

profile of v6, /device:TPU:231, one launch (start us, length us, event | category | flops | bytes accessed | tf_op | source)
XLA Modules:
  0.0 59.2 jit_solution(11250394769239436034)
XLA Ops:
  0.6 0.9 %pack_halo.1 = bf16[528,128]{1,0:T(8,128)(2,1)S(1)} custom-call(s32[1,128]{1,0:T(1,128)} %bitcast.22, bf16[128,512]{1,0:T(8,128)(2,1)} %k_ref.3, bf16[128,512]{1,0:T(8,128)(2,1)} %v_ref.3), custom_call_target="tpu_custom_call" | custom-call | tf_op jit(solution)/shard_map/pack_halo/pallas_call | solution.py:212
  1.5 5.0 %collective-permute-start = (bf16[528,128]{1,0:T(8,128)(2,1)S(1)}, bf16[528,128]{1,0:T(8,128)(2,1)S(1)}, u32[]{:S(2)}, u32[]{:S(2)}) collective-permute-start(bf16[528,128]{1,0:T(8,128)(2,1)S(1)} %pack_halo.1), channel_id=1, source_target_pairs={{0,1},{1,2},{2,3},{3,388},{4,5},{5,6},{6,7},{7,392},{8,9},{9,10},{... | collective-permute-start | bytes 405512 | tf_op jit(solution)/shard_map/ppermute | solution.py:31
  6.5 1.2 %pack_rows.1 = bf16[256,1280]{1,0:T(8,128)(2,1)S(1)} custom-call(bf16[128,2560]{1,0:T(8,128)(2,1)} %bitcast.18, bf16[128,2560]{1,0:T(8,128)(2,1)} %bitcast.20), custom_call_target="tpu_custom_call" | custom-call | tf_op jit(solution)/shard_map/pack_rows/pallas_call | solution.py:224
  7.7 2.9 %collective-permute-start.3 = (bf16[256,1280]{1,0:T(8,128)(2,1)S(1)}, bf16[256,1280]{1,0:T(8,128)(2,1)S(1)}, u32[]{:S(2)}, u32[]{:S(2)}) collective-permute-start(bf16[256,1280]{1,0:T(8,128)(2,1)S(1)} %pack_rows.1), channel_id=1, source_target_pairs={{0,64},{1,65},{2,66},{3,67},{4,68},{5,69},{6,70},{7,71},{8,72},{9,... | collective-permute-start | bytes 1966088 | tf_op jit(solution)/shard_map/ppermute | solution.py:31
  10.6 1.3 %collective-permute-start.1 = (bf16[528,128]{1,0:T(8,128)(2,1)S(1)}, bf16[528,128]{1,0:T(8,128)(2,1)S(1)}, u32[]{:S(2)}, u32[]{:S(2)}) collective-permute-start(bf16[528,128]{1,0:T(8,128)(2,1)S(1)} %pack_halo.1), channel_id=1, source_target_pairs={{0,2},{1,3},{2,388},{4,6},{5,7},{6,392},{8,10},{9,11},{10,396},{12... | collective-permute-start | bytes 405512 | tf_op jit(solution)/shard_map/ppermute | solution.py:31
  11.9 0.0 collective-permute-done.one_ref
  11.9 0.7 %collective-permute-start.2 = (bf16[528,128]{1,0:T(8,128)(2,1)S(1)}, bf16[528,128]{1,0:T(8,128)(2,1)S(1)}, u32[]{:S(2)}, u32[]{:S(2)}) collective-permute-start(bf16[528,128]{1,0:T(8,128)(2,1)S(1)} %collective-permute-done.one_ref), channel_id=1, source_target_pairs={{0,1},{4,5},{8,9},{12,13},{16,17},{20,21},{24,25},{28,29},{32,33},... | collective-permute-start | bytes 405512 | tf_op jit(solution)/shard_map/ppermute | solution.py:31
  12.6 0.0 copy-start.4
  12.6 0.1 pad_add_fusion.place_ref
  12.7 0.0 copy-start
  12.7 0.0 copy-start.1
  12.7 0.0 copy-start.2
  12.7 0.0 copy-start.3
  12.7 6.5 %collective-permute-done.1.two_ref = bf16[528,128]{1,0:T(8,128)(2,1)S(1)} collective-permute-done((bf16[528,128]{1,0:T(8,128)(2,1)S(1)}, bf16[528,128]{1,0:T(8,128)(2,1)S(1)}, u32[]{:S(2)}, u32[]{:S(2)}) %collective-permute-start.1) | collective-permute-done | bytes 135200 | tf_op jit(solution)/shard_map/ppermute | solution.py:31
  19.2 0.0 collective-permute-done.2.relay_ref
  19.2 0.0 copy-done.4
  19.2 0.2 mask.1.bias_ref
  19.4 0.0 collective-permute-done.3.oqc_ref
  19.4 0.0 copy-done
  19.4 0.0 copy-done.1
  19.4 0.0 copy-done.2
  19.4 0.0 copy-done.3
  19.4 5.2 %attend.1 = (bf16[128,1280]{1,0:T(8,128)(2,1)S(1)}, bf16[128,1280]{1,0:T(8,128)(2,1)S(1)}, bf16[4,384,128]{2,1,0:T(8,128)(2,1)S(1)}) custom-call(s32[4]{0:T(128)S(1)} %pad_add_fusion.place_ref, f32[384,128]{1,0:T(8,128)S(1)} %mask.1.bias_ref, bf16[128,2560]{1,0:T(8,128)(2,1)S(1)} %bitcast.19, bf16[128,2560]{1,0:T(8,128)(2,1)S(1)} %bitcast.21, ...), custom_call_target="tpu_custom_call" | custom-call | tf_op jit(solution)/shard_map/attend/pallas_call | solution.py:245
  24.7 3.7 %collective-permute-start.4 = (bf16[384,128]{1,0:T(8,128)(2,1)S(1)}, bf16[384,128]{1,0:T(8,128)(2,1)S(1)}, u32[]{:S(2)}, u32[]{:S(2)}) collective-permute-start(bf16[384,128]{1,0:T(8,128)(2,1)S(1)} %get-tuple-element.19), channel_id=1, source_target_pairs={{0,0},{1,1},{2,2},{3,3},{4,4},{5,5},{6,6},{7,7},{8,8},{9,9},{10,10... | collective-permute-start | bytes 294920 | tf_op jit(solution)/shard_map/ppermute | solution.py:31
  28.3 1.9 %collective-permute-start.7 = (bf16[384,128]{1,0:T(8,128)(2,1)S(1)}, bf16[384,128]{1,0:T(8,128)(2,1)S(1)}, u32[]{:S(2)}, u32[]{:S(2)}) collective-permute-start(bf16[384,128]{1,0:T(8,128)(2,1)S(1)} %get-tuple-element.20), channel_id=1, source_target_pairs={{0,448},{1,449},{2,450},{3,451},{4,452},{5,453},{6,454},{7,455},{8... | collective-permute-start | bytes 294920 | tf_op jit(solution)/shard_map/ppermute | solution.py:31
  30.3 4.5 %collective-permute-start.6 = (bf16[384,128]{1,0:T(8,128)(2,1)S(1)}, bf16[384,128]{1,0:T(8,128)(2,1)S(1)}, u32[]{:S(2)}, u32[]{:S(2)}) collective-permute-start(bf16[384,128]{1,0:T(8,128)(2,1)S(1)} %get-tuple-element.21), channel_id=1, source_target_pairs={{0,384},{1,385},{2,386},{3,387},{4,388},{5,389},{6,390},{7,391},{8... | collective-permute-start | bytes 294920 | tf_op jit(solution)/shard_map/ppermute | solution.py:31
  34.8 1.9 %collective-permute-start.5 = (bf16[384,128]{1,0:T(8,128)(2,1)S(1)}, bf16[384,128]{1,0:T(8,128)(2,1)S(1)}, u32[]{:S(2)}, u32[]{:S(2)}) collective-permute-start(bf16[384,128]{1,0:T(8,128)(2,1)S(1)} %get-tuple-element.22), channel_id=1, source_target_pairs={{0,64},{1,65},{2,66},{3,67},{4,68},{5,69},{6,70},{7,71},{8,72},{9,... | collective-permute-start | bytes 294920 | tf_op jit(solution)/shard_map/ppermute | solution.py:31
  36.7 0.0 collective-permute-done.4
  36.8 2.3 %collective-permute-done.7 = bf16[384,128]{1,0:T(8,128)(2,1)S(1)} collective-permute-done((bf16[384,128]{1,0:T(8,128)(2,1)S(1)}, bf16[384,128]{1,0:T(8,128)(2,1)S(1)}, u32[]{:S(2)}, u32[]{:S(2)}) %collective-permute-start.7) | collective-permute-done | bytes 98336 | tf_op jit(solution)/shard_map/ppermute | solution.py:31
  39.0 0.0 collective-permute-done.6
  39.0 0.0 collective-permute-done.5
  39.1 5.3 %collective-permute-start.8 = (bf16[256,128]{1,0:T(8,128)(2,1)S(1)}, bf16[256,128]{1,0:T(8,128)(2,1)S(1)}, u32[]{:S(2)}, u32[]{:S(2)}) collective-permute-start(bf16[256,128]{1,0:T(8,128)(2,1)S(1)} %add_convert_fusion), channel_id=1, source_target_pairs={{1,0},{2,1},{3,2},{4,387},{5,4},{6,5},{7,6},{8,391},{9,8},{10,9},{... | collective-permute-start | bytes 196616 | tf_op jit(solution)/shard_map/ppermute | solution.py:31
  44.4 7.6 %collective-permute-done.8.back_ref = bf16[256,128]{1,0:T(8,128)(2,1)S(1)} collective-permute-done((bf16[256,128]{1,0:T(8,128)(2,1)S(1)}, bf16[256,128]{1,0:T(8,128)(2,1)S(1)}, u32[]{:S(2)}, u32[]{:S(2)}) %collective-permute-start.8) | collective-permute-done | bytes 65568 | tf_op jit(solution)/shard_map/ppermute | solution.py:31
  52.0 5.0 %collective-permute-start.9 = (bf16[128,1408]{1,0:T(8,128)(2,1)S(1)}, bf16[128,1408]{1,0:T(8,128)(2,1)S(1)}, u32[]{:S(2)}, u32[]{:S(2)}) collective-permute-start(bf16[128,1408]{1,0:T(8,128)(2,1)S(1)} %pad_maximum_fusion), channel_id=1, source_target_pairs={{0,64},{1,65},{2,66},{3,67},{4,68},{5,69},{6,70},{7,71},{8,72},{9,... | collective-permute-start | bytes 1081352 | tf_op jit(solution)/shard_map/ppermute | solution.py:31
  57.1 1.3 %collective-permute-done.9.swapped_ref = bf16[128,1408]{1,0:T(8,128)(2,1)S(1)} collective-permute-done((bf16[128,1408]{1,0:T(8,128)(2,1)S(1)}, bf16[128,1408]{1,0:T(8,128)(2,1)S(1)}, u32[]{:S(2)}, u32[]{:S(2)}) %collective-permute-start.9) | collective-permute-done | bytes 360480 | tf_op jit(solution)/shard_map/ppermute | solution.py:31
  58.3 0.9 %finish.1 = (bf16[128,2560]{1,0:T(8,128)(2,1)}, f32[64,128]{1,0:T(8,128)}, f32[64,128]{1,0:T(8,128)}) custom-call(f32[128,128]{1,0:T(8,128)S(1)} %convert_add_fusion.own_ref, bf16[256,128]{1,0:T(8,128)(2,1)S(1)} %collective-permute-done.8.back_ref, bf16[128,1408]{1,0:T(8,128)(2,1)S(1)} %collective-permute-done.9.swapped_ref, ...), custom_call_target="tpu_custom_call" | custom-call | tf_op jit(solution)/shard_map/finish/pallas_call | solution.py:263
  (5 shorter events, 0.1 us)
Async XLA Ops:
  1.5 10.4 %collective-permute-start = (bf16[528,128]{1,0:T(8,128)(2,1)S(1)}, bf16[528,128]{1,0:T(8,128)(2,1)S(1)}, u32[]{:S(2)}, u32[]{:S(2)}) collective-permute-start(bf16[528,128]{1,0:T(8,128)(2,1)S(1)} %pack_halo.1), channel_id=1, source_target_pairs={{0,1},{1,2},{2,3},{3,388},{4,5},{5,6},{6,7},{7,392},{8,9},{9,10},{... | collective-permute-start | bytes 405512 | tf_op jit(solution)/shard_map/ppermute | solution.py:31
  7.7 11.7 %collective-permute-start.3 = (bf16[256,1280]{1,0:T(8,128)(2,1)S(1)}, bf16[256,1280]{1,0:T(8,128)(2,1)S(1)}, u32[]{:S(2)}, u32[]{:S(2)}) collective-permute-start(bf16[256,1280]{1,0:T(8,128)(2,1)S(1)} %pack_rows.1), channel_id=1, source_target_pairs={{0,64},{1,65},{2,66},{3,67},{4,68},{5,69},{6,70},{7,71},{8,72},{9,... | collective-permute-start | bytes 1966088 | tf_op jit(solution)/shard_map/ppermute | solution.py:31
  10.6 8.6 %collective-permute-start.1 = (bf16[528,128]{1,0:T(8,128)(2,1)S(1)}, bf16[528,128]{1,0:T(8,128)(2,1)S(1)}, u32[]{:S(2)}, u32[]{:S(2)}) collective-permute-start(bf16[528,128]{1,0:T(8,128)(2,1)S(1)} %pack_halo.1), channel_id=1, source_target_pairs={{0,2},{1,3},{2,388},{4,6},{5,7},{6,392},{8,10},{9,11},{10,396},{12... | collective-permute-start | bytes 405512 | tf_op jit(solution)/shard_map/ppermute | solution.py:31
  11.9 7.3 %collective-permute-start.2 = (bf16[528,128]{1,0:T(8,128)(2,1)S(1)}, bf16[528,128]{1,0:T(8,128)(2,1)S(1)}, u32[]{:S(2)}, u32[]{:S(2)}) collective-permute-start(bf16[528,128]{1,0:T(8,128)(2,1)S(1)} %collective-permute-done.one_ref), channel_id=1, source_target_pairs={{0,1},{4,5},{8,9},{12,13},{16,17},{20,21},{24,25},{28,29},{32,33},... | collective-permute-start | bytes 405512 | tf_op jit(solution)/shard_map/ppermute | solution.py:31
  12.6 6.6 %copy-start.4 = (s32[128]{0:T(128)S(1)}, s32[128]{0:T(128)}, u32[]{:S(2)}) copy-start(s32[128]{0:T(128)} %param.9) | copy-start | bytes 1540
  12.7 6.7 %copy-start = (bf16[1,128,2560]{2,1,0:T(8,128)(2,1)S(1)}, bf16[1,128,2560]{2,1,0:T(8,128)(2,1)}, u32[]{:S(2)}) copy-start(bf16[1,128,2560]{2,1,0:T(8,128)(2,1)} %param.5) | copy-start | bytes 1966084
  12.7 6.7 %copy-start.1 = (bf16[1,128,2560]{2,1,0:T(8,128)(2,1)S(1)}, bf16[1,128,2560]{2,1,0:T(8,128)(2,1)}, u32[]{:S(2)}) copy-start(bf16[1,128,2560]{2,1,0:T(8,128)(2,1)} %param.8) | copy-start | bytes 1966084
  12.7 6.7 %copy-start.2 = (bf16[128,512]{1,0:T(8,128)(2,1)S(1)}, bf16[128,512]{1,0:T(8,128)(2,1)}, u32[]{:S(2)}) copy-start(bf16[128,512]{1,0:T(8,128)(2,1)} %k_ref.3) | copy-start | bytes 393220
  12.7 6.7 %copy-start.3 = (bf16[128,512]{1,0:T(8,128)(2,1)S(1)}, bf16[128,512]{1,0:T(8,128)(2,1)}, u32[]{:S(2)}) copy-start(bf16[128,512]{1,0:T(8,128)(2,1)} %v_ref.3) | copy-start | bytes 393220
  24.7 12.1 %collective-permute-start.4 = (bf16[384,128]{1,0:T(8,128)(2,1)S(1)}, bf16[384,128]{1,0:T(8,128)(2,1)S(1)}, u32[]{:S(2)}, u32[]{:S(2)}) collective-permute-start(bf16[384,128]{1,0:T(8,128)(2,1)S(1)} %get-tuple-element.19), channel_id=1, source_target_pairs={{0,0},{1,1},{2,2},{3,3},{4,4},{5,5},{6,6},{7,7},{8,8},{9,9},{10,10... | collective-permute-start | bytes 294920 | tf_op jit(solution)/shard_map/ppermute | solution.py:31
  28.3 10.7 %collective-permute-start.7 = (bf16[384,128]{1,0:T(8,128)(2,1)S(1)}, bf16[384,128]{1,0:T(8,128)(2,1)S(1)}, u32[]{:S(2)}, u32[]{:S(2)}) collective-permute-start(bf16[384,128]{1,0:T(8,128)(2,1)S(1)} %get-tuple-element.20), channel_id=1, source_target_pairs={{0,448},{1,449},{2,450},{3,451},{4,452},{5,453},{6,454},{7,455},{8... | collective-permute-start | bytes 294920 | tf_op jit(solution)/shard_map/ppermute | solution.py:31
  30.3 8.8 %collective-permute-start.6 = (bf16[384,128]{1,0:T(8,128)(2,1)S(1)}, bf16[384,128]{1,0:T(8,128)(2,1)S(1)}, u32[]{:S(2)}, u32[]{:S(2)}) collective-permute-start(bf16[384,128]{1,0:T(8,128)(2,1)S(1)} %get-tuple-element.21), channel_id=1, source_target_pairs={{0,384},{1,385},{2,386},{3,387},{4,388},{5,389},{6,390},{7,391},{8... | collective-permute-start | bytes 294920 | tf_op jit(solution)/shard_map/ppermute | solution.py:31
  34.8 4.2 %collective-permute-start.5 = (bf16[384,128]{1,0:T(8,128)(2,1)S(1)}, bf16[384,128]{1,0:T(8,128)(2,1)S(1)}, u32[]{:S(2)}, u32[]{:S(2)}) collective-permute-start(bf16[384,128]{1,0:T(8,128)(2,1)S(1)} %get-tuple-element.22), channel_id=1, source_target_pairs={{0,64},{1,65},{2,66},{3,67},{4,68},{5,69},{6,70},{7,71},{8,72},{9,... | collective-permute-start | bytes 294920 | tf_op jit(solution)/shard_map/ppermute | solution.py:31
  39.1 12.9 %collective-permute-start.8 = (bf16[256,128]{1,0:T(8,128)(2,1)S(1)}, bf16[256,128]{1,0:T(8,128)(2,1)S(1)}, u32[]{:S(2)}, u32[]{:S(2)}) collective-permute-start(bf16[256,128]{1,0:T(8,128)(2,1)S(1)} %add_convert_fusion), channel_id=1, source_target_pairs={{1,0},{2,1},{3,2},{4,387},{5,4},{6,5},{7,6},{8,391},{9,8},{10,9},{... | collective-permute-start | bytes 196616 | tf_op jit(solution)/shard_map/ppermute | solution.py:31
  52.0 6.3 %collective-permute-start.9 = (bf16[128,1408]{1,0:T(8,128)(2,1)S(1)}, bf16[128,1408]{1,0:T(8,128)(2,1)S(1)}, u32[]{:S(2)}, u32[]{:S(2)}) collective-permute-start(bf16[128,1408]{1,0:T(8,128)(2,1)S(1)} %pad_maximum_fusion), channel_id=1, source_target_pairs={{0,64},{1,65},{2,66},{3,67},{4,68},{5,69},{6,70},{7,71},{8,72},{9,... | collective-permute-start | bytes 1081352 | tf_op jit(solution)/shard_map/ppermute | solution.py:31

commit v7 on v6

--- a/solution.py
+++ b/solution.py
@@ -14,7 +14,7 @@
 SCALE = DH ** (-0.5)
 LOG2E = 1.4426950408889634
 NEG = -1e30
-MASK_FLOPS = 9 << 29
+MASK_FLOPS = 1 << 34
 AXES = ("section", "ctx")
 NT = (((1,), (1,)), ((), ()))
 TN = (((0,), (0,)), ((), ()))
@@ -100,23 +100,30 @@
     run(copies)
 
 
-def mask(ids_ref, one_ref, two_ref, relay_ref, out_ref):
+def halo_mask(ids, *halos):
+    first = ids[:, 0:1]
+    before = sum(halo[4 * TOK :].astype(jnp.float32)[0:1] for halo in halos)
+    held = jnp.sum(jnp.where(before == first + 1.0, 1.0, 0.0), -1, keepdims=True)
+    row = lax.broadcasted_iota(jnp.int32, (TOK, TOK), 0).astype(jnp.float32)
+    wide = jnp.broadcast_to(ids, (TOK, TOK))
+    return jnp.where((wide == first) & (row >= TOK - held), 0.0, NEG)
+
+
+def mask_near(ids_ref, one_ref, out_ref):
     ids = ids_ref[...].astype(jnp.float32)
-    first = ids[:, 0:1]
     row = lax.broadcasted_iota(jnp.int32, (TOK, TOK), 0)
     col = lax.broadcasted_iota(jnp.int32, (TOK, TOK), 1)
     wide = jnp.broadcast_to(ids, (TOK, TOK))
     out_ref[:TOK] = jnp.where((wide.T == wide) & (row <= col), 0.0, NEG)
-    for block, halos in enumerate(((one_ref,), (two_ref, relay_ref))):
-        before = sum(halo[4 * TOK :].astype(jnp.float32)[0:1] for halo in halos)
-        held = jnp.sum(jnp.where(before == first + 1.0, 1.0, 0.0), -1, keepdims=True)
-        out_ref[(block + 1) * TOK : (block + 2) * TOK] = jnp.where(
-            (wide == first) & (row.astype(jnp.float32) >= TOK - held), 0.0, NEG
-        )
+    out_ref[TOK:] = halo_mask(ids, one_ref)
+
+
+def mask_far(ids_ref, two_ref, relay_ref, out_ref):
+    out_ref[...] = halo_mask(ids_ref[...].astype(jnp.float32), two_ref, relay_ref)
 
 
 def attend(
-    place_ref, bias_ref, q_ref, c_ref, oqc_ref, k_ref, v_ref, one_ref, two_ref, relay_ref, dq_ref, odq_ref, part_ref
+    place_ref, near_ref, far_ref, q_ref, c_ref, oqc_ref, k_ref, v_ref, one_ref, two_ref, relay_ref, dq_ref, odq_ref, part_ref
 ):
     slot = pl.program_id(0)
     group = group_of(place_ref[0], slot)
@@ -131,7 +138,7 @@
         jnp.concatenate([ref[:, lanes(group * DH)], one_ref[rows(i)], two_ref[rows(i)] + relay_ref[rows(i)]], 0)
         for i, ref in enumerate((k_ref, v_ref))
     ]
-    bias = bias_ref[...]
+    bias = jnp.concatenate([near_ref[...], far_ref[...]], 0)
     grad_k = jnp.zeros((3 * TOK, DH), jnp.float32)
     grad_v = jnp.zeros((3 * TOK, DH), jnp.float32)
     for mine in (True, False):
@@ -219,7 +226,6 @@
         name="pack_halo",
     )(*(pltpu.with_memory_space_constraint(x, pltpu.HBM) for x in (ids, keys, values)))
     one, two = shifted(sent, 1), shifted(sent, 2, (0, 2, 3))
-    relay = shifted(one, 1, (1,))
     q, c, _ = lax.optimization_barrier((q, c, sent))
     rows = pl.pallas_call(
         pack_rows,
@@ -231,21 +237,31 @@
         name="pack_rows",
     )(*(pltpu.with_memory_space_constraint(x, pltpu.HBM) for x in (q, c)))
     rows = other_core(rows)
+    near = pl.pallas_call(
+        mask_near,
+        in_specs=[vmem] * 2,
+        out_specs=vmem,
+        out_shape=jax.ShapeDtypeStruct((2 * tok, tok), jnp.float32),
+        compiler_params=small,
+        cost_estimate=pl.CostEstimate(flops=MASK_FLOPS, bytes_accessed=0, transcendentals=0),
+        name="mask_near",
+    )(ids, one)
+    one, rows, near = lax.optimization_barrier((one, rows, near))
+    relay = shifted(one, 1, (1,))
     place = jnp.stack([core, y_lo, (me % ROW < 1).astype(core.dtype), (me % ROW < 2).astype(core.dtype)])
     place = place.astype(jnp.int32)
-    bias = pl.pallas_call(
-        mask,
-        in_specs=[vmem] * 4,
+    far = pl.pallas_call(
+        mask_far,
+        in_specs=[vmem] * 3,
         out_specs=vmem,
-        out_shape=jax.ShapeDtypeStruct((3 * tok, tok), jnp.float32),
-        compiler_params=small,
-        cost_estimate=pl.CostEstimate(flops=MASK_FLOPS, bytes_accessed=0, transcendentals=0),
-        name="mask",
-    )(ids, one, two, relay)
+        out_shape=jax.ShapeDtypeStruct((tok, tok), jnp.float32),
+        compiler_params=small,
+        name="mask_far",
+    )(ids, two, relay)
     own_q, other_q, part = pl.pallas_call(
         attend,
         grid=(2,),
-        in_specs=[pl.BlockSpec(memory_space=pltpu.SMEM)] + [vmem] * 9,
+        in_specs=[pl.BlockSpec(memory_space=pltpu.SMEM)] + [vmem] * 10,
         out_specs=(vmem,) * 3,
         out_shape=(
             jax.ShapeDtypeStruct((tok, 2 * WIDE), jnp.bfloat16),
@@ -254,7 +270,7 @@
         ),
         compiler_params=pltpu.CompilerParams(vmem_limit_bytes=24 * 1024 * 1024),
         name="attend",
-    )(place, bias, q, c, rows, keys, values, one, two, relay)
+    )(place, near, far, q, c, rows, keys, values, one, two, relay)
     shares = [to_owner(part[step], step) for step in range(4)]
     total = sum(share[:tok].astype(jnp.float32) for share in shares)
     back = sum(share[tok:].astype(jnp.float32) for share in shares).astype(jnp.bfloat16)

time: 59.7 us -> 58.5 us (0.980)
  the two profiles are of different devices: /device:TPU:231 before, /device:TPU:199 now
where the time goes in v7:
time: 58.5 us; the launch traced here: 58 us
  starting transfers between devices  36.1 us (62%)
  waiting for transfers between devices  11.7 us (20%)
  Pallas kernels  8.43 us (14%)
  between operations  0.88 us (2%)
  local copies, waits for them, and re-layouts  0.82 us (1%)
    ppermute x10, starting transfers between devices, permuted(): return lax.ppermute(x, AXES, found)  36.1 us
    ppermute x10, waiting for transfers between devices, permuted(): return lax.ppermute(x, AXES, found)  11.7 us
    pallas_call x1, Pallas kernels, on_device(): pl.pallas_call(attend, grid=(2,), in_specs=[pl.BlockSpec(memory_space=plt...  5.14 us
    pallas_call x1, Pallas kernels, on_device(): pl.pallas_call(pack_rows, in_specs=[hbm] * 2, out_specs=vmem, out_shape=j...  1.21 us
  transfers between devices with their start and end apart: 10, of which 4 were waited for; matrix products, arithmetic and copies ran while one was open for 0% of the time, Pallas kernels for 2%

profile of v7, /device:TPU:199, one launch (start us, length us, event | category | flops | bytes accessed | tf_op | source)
XLA Modules:
  0.0 58.0 jit_solution(17598163988348586348)
XLA Ops:
  0.6 0.9 %pack_halo.1 = bf16[528,128]{1,0:T(8,128)(2,1)S(1)} custom-call(s32[1,128]{1,0:T(1,128)} %bitcast.22, bf16[128,512]{1,0:T(8,128)(2,1)} %k_ref.3, bf16[128,512]{1,0:T(8,128)(2,1)} %v_ref.3), custom_call_target="tpu_custom_call" | custom-call | tf_op jit(solution)/shard_map/pack_halo/pallas_call | solution.py:219
  1.5 5.0 %collective-permute-start = (bf16[528,128]{1,0:T(8,128)(2,1)S(1)}, bf16[528,128]{1,0:T(8,128)(2,1)S(1)}, u32[]{:S(2)}, u32[]{:S(2)}) collective-permute-start(bf16[528,128]{1,0:T(8,128)(2,1)S(1)} %pack_halo.1), channel_id=1, source_target_pairs={{0,1},{1,2},{2,3},{3,388},{4,5},{5,6},{6,7},{7,392},{8,9},{9,10},{... | collective-permute-start | bytes 405512 | tf_op jit(solution)/shard_map/ppermute | solution.py:31
  6.5 1.3 %collective-permute-start.2 = (bf16[528,128]{1,0:T(8,128)(2,1)S(1)}, bf16[528,128]{1,0:T(8,128)(2,1)S(1)}, u32[]{:S(2)}, u32[]{:S(2)}) collective-permute-start(bf16[528,128]{1,0:T(8,128)(2,1)S(1)} %pack_halo.1), channel_id=1, source_target_pairs={{0,2},{1,3},{2,388},{4,6},{5,7},{6,392},{8,10},{9,11},{10,396},{12... | collective-permute-start | bytes 405512 | tf_op jit(solution)/shard_map/ppermute | solution.py:31
  7.8 0.0 copy-start.4
  7.8 1.2 %pack_rows.1 = bf16[256,1280]{1,0:T(8,128)(2,1)S(1)} custom-call(bf16[128,2560]{1,0:T(8,128)(2,1)} %bitcast.18, bf16[128,2560]{1,0:T(8,128)(2,1)} %bitcast.20), custom_call_target="tpu_custom_call" | custom-call | tf_op jit(solution)/shard_map/pack_rows/pallas_call | solution.py:230
  9.1 2.9 %collective-permute-start.1 = (bf16[256,1280]{1,0:T(8,128)(2,1)S(1)}, bf16[256,1280]{1,0:T(8,128)(2,1)S(1)}, u32[]{:S(2)}, u32[]{:S(2)}) collective-permute-start(bf16[256,1280]{1,0:T(8,128)(2,1)S(1)} %pack_rows.1), channel_id=1, source_target_pairs={{0,64},{1,65},{2,66},{3,67},{4,68},{5,69},{6,70},{7,71},{8,72},{9,... | collective-permute-start | bytes 1966088 | tf_op jit(solution)/shard_map/ppermute | solution.py:31
  11.9 0.0 collective-permute-done.one_ref
  11.9 0.0 copy-done.4
  11.9 0.0 copy-start
  12.0 0.0 copy-start.1
  12.0 0.2 mask_near.1.near_ref
  12.1 1.5 %collective-permute-done.1.oqc_ref = bf16[256,1280]{1,0:T(8,128)(2,1)S(1)} collective-permute-done((bf16[256,1280]{1,0:T(8,128)(2,1)S(1)}, bf16[256,1280]{1,0:T(8,128)(2,1)S(1)}, u32[]{:S(2)}, u32[]{:S(2)}) %collective-permute-start.1) | collective-permute-done | bytes 655392 | tf_op jit(solution)/shard_map/ppermute | solution.py:31
  13.6 0.7 %collective-permute-start.3 = (bf16[528,128]{1,0:T(8,128)(2,1)S(1)}, bf16[528,128]{1,0:T(8,128)(2,1)S(1)}, u32[]{:S(2)}, u32[]{:S(2)}) collective-permute-start(bf16[528,128]{1,0:T(8,128)(2,1)S(1)} %collective-permute-done.one_ref), channel_id=1, source_target_pairs={{0,1},{4,5},{8,9},{12,13},{16,17},{20,21},{24,25},{28,29},{32,33},... | collective-permute-start | bytes 405512 | tf_op jit(solution)/shard_map/ppermute | solution.py:31
  14.3 0.1 pad_add_fusion.place_ref
  14.4 0.0 copy-start.2
  14.4 0.0 copy-start.3
  14.4 0.0 collective-permute-done.2.two_ref
  14.4 0.0 collective-permute-done.3.relay_ref
  14.4 0.2 mask_far.1.far_ref
  14.6 0.0 copy-done
  14.6 0.0 copy-done.1
  14.6 0.7 %copy-done.2 = bf16[128,512]{1,0:T(8,128)(2,1)S(1)} copy-done((bf16[128,512]{1,0:T(8,128)(2,1)S(1)}, bf16[128,512]{1,0:T(8,128)(2,1)}, u32[]{:S(2)}) %copy-start.2) | copy-done | bytes 131096
  15.3 0.1 copy-done.3
  15.4 5.1 %attend.1 = (bf16[128,1280]{1,0:T(8,128)(2,1)S(1)}, bf16[128,1280]{1,0:T(8,128)(2,1)S(1)}, bf16[4,384,128]{2,1,0:T(8,128)(2,1)S(1)}) custom-call(s32[4]{0:T(128)S(1)} %pad_add_fusion.place_ref, f32[256,128]{1,0:T(8,128)S(1)} %mask_near.1.near_ref, f32[128,128]{1,0:T(8,128)S(1)} %mask_far.1.far_ref, bf16[128,2560]{1,0:T(8,128)(2,1)S(1)} %bitcast.19, ...), custom_call_target="tpu_custom_call" | custom-call | tf_op jit(solution)/shard_map/attend/pallas_call | solution.py:261
  20.6 4.5 %collective-permute-start.4 = (bf16[384,128]{1,0:T(8,128)(2,1)S(1)}, bf16[384,128]{1,0:T(8,128)(2,1)S(1)}, u32[]{:S(2)}, u32[]{:S(2)}) collective-permute-start(bf16[384,128]{1,0:T(8,128)(2,1)S(1)} %get-tuple-element.25), channel_id=1, source_target_pairs={{0,0},{1,1},{2,2},{3,3},{4,4},{5,5},{6,6},{7,7},{8,8},{9,9},{10,10... | collective-permute-start | bytes 294920 | tf_op jit(solution)/shard_map/ppermute | solution.py:31
  25.1 2.8 %collective-permute-start.7 = (bf16[384,128]{1,0:T(8,128)(2,1)S(1)}, bf16[384,128]{1,0:T(8,128)(2,1)S(1)}, u32[]{:S(2)}, u32[]{:S(2)}) collective-permute-start(bf16[384,128]{1,0:T(8,128)(2,1)S(1)} %get-tuple-element.26), channel_id=1, source_target_pairs={{0,448},{1,449},{2,450},{3,451},{4,452},{5,453},{6,454},{7,455},{8... | collective-permute-start | bytes 294920 | tf_op jit(solution)/shard_map/ppermute | solution.py:31
  27.9 3.7 %collective-permute-start.6 = (bf16[384,128]{1,0:T(8,128)(2,1)S(1)}, bf16[384,128]{1,0:T(8,128)(2,1)S(1)}, u32[]{:S(2)}, u32[]{:S(2)}) collective-permute-start(bf16[384,128]{1,0:T(8,128)(2,1)S(1)} %get-tuple-element.27), channel_id=1, source_target_pairs={{0,384},{1,385},{2,386},{3,387},{4,388},{5,389},{6,390},{7,391},{8... | collective-permute-start | bytes 294920 | tf_op jit(solution)/shard_map/ppermute | solution.py:31
  31.6 1.9 %collective-permute-start.5 = (bf16[384,128]{1,0:T(8,128)(2,1)S(1)}, bf16[384,128]{1,0:T(8,128)(2,1)S(1)}, u32[]{:S(2)}, u32[]{:S(2)}) collective-permute-start(bf16[384,128]{1,0:T(8,128)(2,1)S(1)} %get-tuple-element.28), channel_id=1, source_target_pairs={{0,64},{1,65},{2,66},{3,67},{4,68},{5,69},{6,70},{7,71},{8,72},{9,... | collective-permute-start | bytes 294920 | tf_op jit(solution)/shard_map/ppermute | solution.py:31
  33.5 0.0 collective-permute-done.4
  33.5 0.0 collective-permute-done.7
  33.5 2.2 %collective-permute-done.6 = bf16[384,128]{1,0:T(8,128)(2,1)S(1)} collective-permute-done((bf16[384,128]{1,0:T(8,128)(2,1)S(1)}, bf16[384,128]{1,0:T(8,128)(2,1)S(1)}, u32[]{:S(2)}, u32[]{:S(2)}) %collective-permute-start.6) | collective-permute-done | bytes 98336 | tf_op jit(solution)/shard_map/ppermute | solution.py:31
  35.7 0.0 collective-permute-done.5
  35.8 11.4 %collective-permute-start.8 = (bf16[256,128]{1,0:T(8,128)(2,1)S(1)}, bf16[256,128]{1,0:T(8,128)(2,1)S(1)}, u32[]{:S(2)}, u32[]{:S(2)}) collective-permute-start(bf16[256,128]{1,0:T(8,128)(2,1)S(1)} %add_convert_fusion), channel_id=1, source_target_pairs={{1,0},{2,1},{3,2},{4,387},{5,4},{6,5},{7,6},{8,391},{9,8},{10,9},{... | collective-permute-start | bytes 196616 | tf_op jit(solution)/shard_map/ppermute | solution.py:31
  47.2 6.4 %collective-permute-done.8.back_ref = bf16[256,128]{1,0:T(8,128)(2,1)S(1)} collective-permute-done((bf16[256,128]{1,0:T(8,128)(2,1)S(1)}, bf16[256,128]{1,0:T(8,128)(2,1)S(1)}, u32[]{:S(2)}, u32[]{:S(2)}) %collective-permute-start.8) | collective-permute-done | bytes 65568 | tf_op jit(solution)/shard_map/ppermute | solution.py:31
  53.6 1.9 %collective-permute-start.9 = (bf16[128,1408]{1,0:T(8,128)(2,1)S(1)}, bf16[128,1408]{1,0:T(8,128)(2,1)S(1)}, u32[]{:S(2)}, u32[]{:S(2)}) collective-permute-start(bf16[128,1408]{1,0:T(8,128)(2,1)S(1)} %pad_maximum_fusion), channel_id=1, source_target_pairs={{0,64},{1,65},{2,66},{3,67},{4,68},{5,69},{6,70},{7,71},{8,72},{9,... | collective-permute-start | bytes 1081352 | tf_op jit(solution)/shard_map/ppermute | solution.py:31
  55.5 1.6 %collective-permute-done.9.swapped_ref = bf16[128,1408]{1,0:T(8,128)(2,1)S(1)} collective-permute-done((bf16[128,1408]{1,0:T(8,128)(2,1)S(1)}, bf16[128,1408]{1,0:T(8,128)(2,1)S(1)}, u32[]{:S(2)}, u32[]{:S(2)}) %collective-permute-start.9) | collective-permute-done | bytes 360480 | tf_op jit(solution)/shard_map/ppermute | solution.py:31
  57.1 0.9 %finish.1 = (bf16[128,2560]{1,0:T(8,128)(2,1)}, f32[64,128]{1,0:T(8,128)}, f32[64,128]{1,0:T(8,128)}) custom-call(f32[128,128]{1,0:T(8,128)S(1)} %convert_add_fusion.own_ref, bf16[256,128]{1,0:T(8,128)(2,1)S(1)} %collective-permute-done.8.back_ref, bf16[128,1408]{1,0:T(8,128)(2,1)S(1)} %collective-permute-done.9.swapped_ref, ...), custom_call_target="tpu_custom_call" | custom-call | tf_op jit(solution)/shard_map/finish/pallas_call | solution.py:279
  (5 shorter events, 0.1 us)
Async XLA Ops:
  1.5 10.4 %collective-permute-start = (bf16[528,128]{1,0:T(8,128)(2,1)S(1)}, bf16[528,128]{1,0:T(8,128)(2,1)S(1)}, u32[]{:S(2)}, u32[]{:S(2)}) collective-permute-start(bf16[528,128]{1,0:T(8,128)(2,1)S(1)} %pack_halo.1), channel_id=1, source_target_pairs={{0,1},{1,2},{2,3},{3,388},{4,5},{5,6},{6,7},{7,392},{8,9},{9,10},{... | collective-permute-start | bytes 405512 | tf_op jit(solution)/shard_map/ppermute | solution.py:31
  6.5 7.9 %collective-permute-start.2 = (bf16[528,128]{1,0:T(8,128)(2,1)S(1)}, bf16[528,128]{1,0:T(8,128)(2,1)S(1)}, u32[]{:S(2)}, u32[]{:S(2)}) collective-permute-start(bf16[528,128]{1,0:T(8,128)(2,1)S(1)} %pack_halo.1), channel_id=1, source_target_pairs={{0,2},{1,3},{2,388},{4,6},{5,7},{6,392},{8,10},{9,11},{10,396},{12... | collective-permute-start | bytes 405512 | tf_op jit(solution)/shard_map/ppermute | solution.py:31
  7.8 4.1 %copy-start.4 = (s32[128]{0:T(128)S(1)}, s32[128]{0:T(128)}, u32[]{:S(2)}) copy-start(s32[128]{0:T(128)} %param.9) | copy-start | bytes 1540
  9.1 4.6 %collective-permute-start.1 = (bf16[256,1280]{1,0:T(8,128)(2,1)S(1)}, bf16[256,1280]{1,0:T(8,128)(2,1)S(1)}, u32[]{:S(2)}, u32[]{:S(2)}) collective-permute-start(bf16[256,1280]{1,0:T(8,128)(2,1)S(1)} %pack_rows.1), channel_id=1, source_target_pairs={{0,64},{1,65},{2,66},{3,67},{4,68},{5,69},{6,70},{7,71},{8,72},{9,... | collective-permute-start | bytes 1966088 | tf_op jit(solution)/shard_map/ppermute | solution.py:31
  11.9 2.6 %copy-start = (bf16[1,128,2560]{2,1,0:T(8,128)(2,1)S(1)}, bf16[1,128,2560]{2,1,0:T(8,128)(2,1)}, u32[]{:S(2)}) copy-start(bf16[1,128,2560]{2,1,0:T(8,128)(2,1)} %param.5) | copy-start | bytes 1966084
  12.0 2.6 %copy-start.1 = (bf16[1,128,2560]{2,1,0:T(8,128)(2,1)S(1)}, bf16[1,128,2560]{2,1,0:T(8,128)(2,1)}, u32[]{:S(2)}) copy-start(bf16[1,128,2560]{2,1,0:T(8,128)(2,1)} %param.8) | copy-start | bytes 1966084
  13.6 0.8 %collective-permute-start.3 = (bf16[528,128]{1,0:T(8,128)(2,1)S(1)}, bf16[528,128]{1,0:T(8,128)(2,1)S(1)}, u32[]{:S(2)}, u32[]{:S(2)}) collective-permute-start(bf16[528,128]{1,0:T(8,128)(2,1)S(1)} %collective-permute-done.one_ref), channel_id=1, source_target_pairs={{0,1},{4,5},{8,9},{12,13},{16,17},{20,21},{24,25},{28,29},{32,33},... | collective-permute-start | bytes 405512 | tf_op jit(solution)/shard_map/ppermute | solution.py:31
  14.4 0.9 %copy-start.2 = (bf16[128,512]{1,0:T(8,128)(2,1)S(1)}, bf16[128,512]{1,0:T(8,128)(2,1)}, u32[]{:S(2)}) copy-start(bf16[128,512]{1,0:T(8,128)(2,1)} %k_ref.3) | copy-start | bytes 393220
  14.4 1.0 %copy-start.3 = (bf16[128,512]{1,0:T(8,128)(2,1)S(1)}, bf16[128,512]{1,0:T(8,128)(2,1)}, u32[]{:S(2)}) copy-start(bf16[128,512]{1,0:T(8,128)(2,1)} %v_ref.3) | copy-start | bytes 393220
  20.6 13.0 %collective-permute-start.4 = (bf16[384,128]{1,0:T(8,128)(2,1)S(1)}, bf16[384,128]{1,0:T(8,128)(2,1)S(1)}, u32[]{:S(2)}, u32[]{:S(2)}) collective-permute-start(bf16[384,128]{1,0:T(8,128)(2,1)S(1)} %get-tuple-element.25), channel_id=1, source_target_pairs={{0,0},{1,1},{2,2},{3,3},{4,4},{5,5},{6,6},{7,7},{8,8},{9,9},{10,10... | collective-permute-start | bytes 294920 | tf_op jit(solution)/shard_map/ppermute | solution.py:31
  25.1 8.4 %collective-permute-start.7 = (bf16[384,128]{1,0:T(8,128)(2,1)S(1)}, bf16[384,128]{1,0:T(8,128)(2,1)S(1)}, u32[]{:S(2)}, u32[]{:S(2)}) collective-permute-start(bf16[384,128]{1,0:T(8,128)(2,1)S(1)} %get-tuple-element.26), channel_id=1, source_target_pairs={{0,448},{1,449},{2,450},{3,451},{4,452},{5,453},{6,454},{7,455},{8... | collective-permute-start | bytes 294920 | tf_op jit(solution)/shard_map/ppermute | solution.py:31
  27.9 7.8 %collective-permute-start.6 = (bf16[384,128]{1,0:T(8,128)(2,1)S(1)}, bf16[384,128]{1,0:T(8,128)(2,1)S(1)}, u32[]{:S(2)}, u32[]{:S(2)}) collective-permute-start(bf16[384,128]{1,0:T(8,128)(2,1)S(1)} %get-tuple-element.27), channel_id=1, source_target_pairs={{0,384},{1,385},{2,386},{3,387},{4,388},{5,389},{6,390},{7,391},{8... | collective-permute-start | bytes 294920 | tf_op jit(solution)/shard_map/ppermute | solution.py:31
  31.6 4.1 %collective-permute-start.5 = (bf16[384,128]{1,0:T(8,128)(2,1)S(1)}, bf16[384,128]{1,0:T(8,128)(2,1)S(1)}, u32[]{:S(2)}, u32[]{:S(2)}) collective-permute-start(bf16[384,128]{1,0:T(8,128)(2,1)S(1)} %get-tuple-element.28), channel_id=1, source_target_pairs={{0,64},{1,65},{2,66},{3,67},{4,68},{5,69},{6,70},{7,71},{8,72},{9,... | collective-permute-start | bytes 294920 | tf_op jit(solution)/shard_map/ppermute | solution.py:31
  35.8 17.8 %collective-permute-start.8 = (bf16[256,128]{1,0:T(8,128)(2,1)S(1)}, bf16[256,128]{1,0:T(8,128)(2,1)S(1)}, u32[]{:S(2)}, u32[]{:S(2)}) collective-permute-start(bf16[256,128]{1,0:T(8,128)(2,1)S(1)} %add_convert_fusion), channel_id=1, source_target_pairs={{1,0},{2,1},{3,2},{4,387},{5,4},{6,5},{7,6},{8,391},{9,8},{10,9},{... | collective-permute-start | bytes 196616 | tf_op jit(solution)/shard_map/ppermute | solution.py:31
  53.6 3.6 %collective-permute-start.9 = (bf16[128,1408]{1,0:T(8,128)(2,1)S(1)}, bf16[128,1408]{1,0:T(8,128)(2,1)S(1)}, u32[]{:S(2)}, u32[]{:S(2)}) collective-permute-start(bf16[128,1408]{1,0:T(8,128)(2,1)S(1)} %pad_maximum_fusion), channel_id=1, source_target_pairs={{0,64},{1,65},{2,66},{3,67},{4,68},{5,69},{6,70},{7,71},{8,72},{9,... | collective-permute-start | bytes 1081352 | tf_op jit(solution)/shard_map/ppermute | solution.py:31

commit v8 on v7

--- a/solution.py
+++ b/solution.py
@@ -14,7 +14,8 @@
 SCALE = DH ** (-0.5)
 LOG2E = 1.4426950408889634
 NEG = -1e30
-MASK_FLOPS = 1 << 34
+FAR_FLOPS = 1 << 31
+NEAR_FLOPS = 1 << 33
 AXES = ("section", "ctx")
 NT = (((1,), (1,)), ((), ()))
 TN = (((0,), (0,)), ((), ()))
@@ -43,8 +44,9 @@
 
 def returned(x):
     def target(s, c):
-        to = c - 1 - s % 2
-        return ((3 - s // 2) * 2 + s % 2 if c // ROW != to // ROW else s, to)
+        share = s // 2
+        chip, to = group_of(s % 2, share // 2), c - 1 - share % 2
+        return ((3 - chip if c // ROW != to // ROW else chip) * 2 + share % 2, to)
 
     return permuted(x, target)
 
@@ -57,12 +59,8 @@
     return core + slot * (3 - 2 * core)
 
 
-def to_owner(x, step):
-    def target(s, c):
-        share = (s // 2) ^ step
-        return (group_of(s % 2, share // 2) * 2 + share % 2, c)
-
-    return permuted(x, target)
+def to_owner(x):
+    return permuted(x, lambda s, c: (group_of(s % 2, s // 2 // 2) * 2 + s // 2 % 2, c))
 
 
 def core_groups(core):
@@ -178,11 +176,11 @@
         jnp.concatenate([grad_k[:, half:], grad_v[:, half:]], 1),
     )
     for side in range(2):
-        part_ref[(2 * slot + side) ^ place_ref[1], :TOK, :] = shares[side][:TOK]
+        part_ref[2 * slot + side, :TOK, :] = shares[side][:TOK]
         for block in (1, 2):
             carrier = 2 * (slot ^ place_ref[1 + block]) + block - 1
             at = slice((1 + side) * TOK, (2 + side) * TOK)
-            part_ref[carrier ^ place_ref[1], at, :] = shares[side][block * TOK : (block + 1) * TOK]
+            part_ref[carrier, at, :] = shares[side][block * TOK : (block + 1) * TOK]
 
 
 def finish(own_ref, back_ref, swapped_ref, own_q_ref, dq_ref, dk_ref, dv_ref, total_ref, sems):
@@ -196,7 +194,7 @@
     for copy in copies:
         copy.start()
     mine = back_ref[pl.ds(pl.multiple_of(core * TOK, TOK), TOK), :]
-    total = own_ref[...] + mine.astype(jnp.float32) + swapped_ref[:, 2 * WIDE :].astype(jnp.float32)
+    total = own_ref[...].astype(jnp.float32) + mine.astype(jnp.float32) + swapped_ref[:, 2 * WIDE :].astype(jnp.float32)
     total_ref[...] = total.T
     for i, ref in enumerate((dk_ref, dv_ref)):
         copies.append(pltpu.make_async_copy(total_ref.at[pl.ds(i * half, half)], ref, sems.at[4 + i]))
@@ -236,19 +234,19 @@
         compiler_params=small,
         name="pack_rows",
     )(*(pltpu.with_memory_space_constraint(x, pltpu.HBM) for x in (q, c)))
-    rows = other_core(rows)
     near = pl.pallas_call(
         mask_near,
         in_specs=[vmem] * 2,
         out_specs=vmem,
         out_shape=jax.ShapeDtypeStruct((2 * tok, tok), jnp.float32),
         compiler_params=small,
-        cost_estimate=pl.CostEstimate(flops=MASK_FLOPS, bytes_accessed=0, transcendentals=0),
+        cost_estimate=pl.CostEstimate(flops=NEAR_FLOPS, bytes_accessed=0, transcendentals=0),
         name="mask_near",
     )(ids, one)
-    one, rows, near = lax.optimization_barrier((one, rows, near))
+    one, near = lax.optimization_barrier((one, near))
     relay = shifted(one, 1, (1,))
-    place = jnp.stack([core, y_lo, (me % ROW < 1).astype(core.dtype), (me % ROW < 2).astype(core.dtype)])
+    rows = other_core(rows)
+    place = jnp.stack([core, core, (me % ROW < 1).astype(core.dtype), (me % ROW < 2).astype(core.dtype)])
     place = place.astype(jnp.int32)
     far = pl.pallas_call(
         mask_far,
@@ -256,6 +254,7 @@
         out_specs=vmem,
         out_shape=jax.ShapeDtypeStruct((tok, tok), jnp.float32),
         compiler_params=small,
+        cost_estimate=pl.CostEstimate(flops=FAR_FLOPS, bytes_accessed=0, transcendentals=0),
         name="mask_far",
     )(ids, two, relay)
     own_q, other_q, part = pl.pallas_call(
@@ -271,10 +270,11 @@
         compiler_params=pltpu.CompilerParams(vmem_limit_bytes=24 * 1024 * 1024),
         name="attend",
     )(place, near, far, q, c, rows, keys, values, one, two, relay)
-    shares = [to_owner(part[step], step) for step in range(4)]
-    total = sum(share[:tok].astype(jnp.float32) for share in shares)
-    back = sum(share[tok:].astype(jnp.float32) for share in shares).astype(jnp.bfloat16)
-    back = returned(back)
+    chips = [[s for s in range(8) if s % 2 == parity] for parity in range(2)]
+    shares = lax.all_to_all(part, "section", 0, 0, axis_index_groups=chips)
+    back = returned(jnp.sum(shares[:, tok:].astype(jnp.float32), 0).astype(jnp.bfloat16))
+    total = to_owner(jnp.sum(shares[:, :tok].astype(jnp.float32), 0).astype(jnp.bfloat16))
+    back, total = lax.optimization_barrier((back, total))
     swapped = other_core(jnp.concatenate([other_q, jnp.where(core == 0, back[tok:], back[:tok])], 1))
     grad_q, grad_k, grad_v = pl.pallas_call(
         finish,

time: 58.5 us -> 55.7 us (0.952)
  the two profiles are of different devices: /device:TPU:199 before, /device:TPU:389 now
where the time goes in v8:
time: 55.7 us; the launch traced here: 55.3 us
  starting transfers between devices  24.6 us (44%)
  blocking collectives  15.2 us (27%)
  Pallas kernels  8.42 us (15%)
  waiting for transfers between devices  5.5 us (10%)
  between operations  0.82 us (1%)
  local copies, waits for them, and re-layouts  0.61 us (1%)
    ppermute x7, starting transfers between devices, permuted(): return lax.ppermute(x, AXES, found)  24.6 us
    all_to_all x1, blocking collectives, on_device(): shares = lax.all_to_all(part, 'section', 0, 0, axis_index_groups=chips)  15.2 us
    ppermute x7, waiting for transfers between devices, permuted(): return lax.ppermute(x, AXES, found)  5.5 us
    pallas_call x1, Pallas kernels, on_device(): pl.pallas_call(attend, grid=(2,), in_specs=[pl.BlockSpec(memory_space=plt...  5.13 us
    pallas_call x1, Pallas kernels, on_device(): pl.pallas_call(pack_rows, in_specs=[hbm] * 2, out_specs=vmem, out_shape=j...  1.21 us
  transfers between devices with their start and end apart: 7, of which 3 were waited for; matrix products, arithmetic and copies ran while one was open for 0% of the time, Pallas kernels for 3%

profile of v8, /device:TPU:389, one launch (start us, length us, event | category | flops | bytes accessed | tf_op | source)
XLA Modules:
  0.0 55.3 jit_solution(11494479613342870525)
XLA Ops:
  0.6 0.9 %pack_halo.1 = bf16[528,128]{1,0:T(8,128)(2,1)S(1)} custom-call(s32[1,128]{1,0:T(1,128)} %bitcast.13, bf16[128,512]{1,0:T(8,128)(2,1)} %k_ref.3, bf16[128,512]{1,0:T(8,128)(2,1)} %v_ref.3), custom_call_target="tpu_custom_call" | custom-call | tf_op jit(solution)/shard_map/pack_halo/pallas_call | solution.py:217
  1.5 2.8 %collective-permute-start = (bf16[528,128]{1,0:T(8,128)(2,1)S(1)}, bf16[528,128]{1,0:T(8,128)(2,1)S(1)}, u32[]{:S(2)}, u32[]{:S(2)}) collective-permute-start(bf16[528,128]{1,0:T(8,128)(2,1)S(1)} %pack_halo.1), channel_id=1, source_target_pairs={{0,1},{1,2},{2,3},{3,388},{4,5},{5,6},{6,7},{7,392},{8,9},{9,10},{... | collective-permute-start | bytes 405512 | tf_op jit(solution)/shard_map/ppermute | solution.py:32
  4.3 5.3 %collective-permute-start.1 = (bf16[528,128]{1,0:T(8,128)(2,1)S(1)}, bf16[528,128]{1,0:T(8,128)(2,1)S(1)}, u32[]{:S(2)}, u32[]{:S(2)}) collective-permute-start(bf16[528,128]{1,0:T(8,128)(2,1)S(1)} %pack_halo.1), channel_id=1, source_target_pairs={{0,2},{1,3},{2,388},{4,6},{5,7},{6,392},{8,10},{9,11},{10,396},{12... | collective-permute-start | bytes 405512 | tf_op jit(solution)/shard_map/ppermute | solution.py:32
  9.7 0.0 copy-start.4
  9.7 1.2 %pack_rows.1 = bf16[256,1280]{1,0:T(8,128)(2,1)S(1)} custom-call(bf16[128,2560]{1,0:T(8,128)(2,1)} %bitcast.9, bf16[128,2560]{1,0:T(8,128)(2,1)} %bitcast.11), custom_call_target="tpu_custom_call" | custom-call | tf_op jit(solution)/shard_map/pack_rows/pallas_call | solution.py:228
  10.9 3.1 %collective-permute-start.3 = (bf16[256,1280]{1,0:T(8,128)(2,1)S(1)}, bf16[256,1280]{1,0:T(8,128)(2,1)S(1)}, u32[]{:S(2)}, u32[]{:S(2)}) collective-permute-start(bf16[256,1280]{1,0:T(8,128)(2,1)S(1)} %pack_rows.1), channel_id=1, source_target_pairs={{0,64},{1,65},{2,66},{3,67},{4,68},{5,69},{6,70},{7,71},{8,72},{9,... | collective-permute-start | bytes 1966088 | tf_op jit(solution)/shard_map/ppermute | solution.py:32
  14.1 0.0 collective-permute-done.one_ref
  14.1 0.0 copy-done.4
  14.1 0.2 mask_near.1.near_ref
  14.3 0.7 %collective-permute-start.2 = (bf16[528,128]{1,0:T(8,128)(2,1)S(1)}, bf16[528,128]{1,0:T(8,128)(2,1)S(1)}, u32[]{:S(2)}, u32[]{:S(2)}) collective-permute-start(bf16[528,128]{1,0:T(8,128)(2,1)S(1)} %collective-permute-done.one_ref), channel_id=1, source_target_pairs={{0,1},{4,5},{8,9},{12,13},{16,17},{20,21},{24,25},{28,29},{32,33},... | collective-permute-start | bytes 405512 | tf_op jit(solution)/shard_map/ppermute | solution.py:32
  15.0 0.1 pad_add_fusion.place_ref
  15.0 0.0 copy-start
  15.0 0.0 copy-start.1
  15.0 0.0 copy-start.2
  15.0 0.0 copy-start.3
  15.0 0.0 collective-permute-done.1.two_ref
  15.1 0.0 collective-permute-done.2.relay_ref
  15.1 0.2 mask_far.1.far_ref
  15.2 0.5 collective-permute-done.3.oqc_ref
  15.8 0.4 copy-done
  16.1 0.2 copy-done.1
  16.3 0.0 copy-done.2
  16.3 0.0 copy-done.3
  16.4 5.1 %attend.1 = (bf16[128,1280]{1,0:T(8,128)(2,1)S(1)}, bf16[128,1280]{1,0:T(8,128)(2,1)S(1)}, bf16[4,384,128]{2,1,0:T(8,128)(2,1)S(1)}) custom-call(s32[4]{0:T(128)S(1)} %pad_add_fusion.place_ref, f32[256,128]{1,0:T(8,128)S(1)} %mask_near.1.near_ref, f32[128,128]{1,0:T(8,128)S(1)} %mask_far.1.far_ref, bf16[128,2560]{1,0:T(8,128)(2,1)S(1)} %bitcast.10, ...), custom_call_target="tpu_custom_call" | custom-call | tf_op jit(solution)/shard_map/attend/pallas_call | solution.py:260
  21.5 15.2 %all_to_all.5 = bf16[4,384,128]{2,1,0:T(8,128)(2,1)S(1)} all-to-all(bf16[4,384,128]{2,1,0:T(8,128)(2,1)S(1)} %get-tuple-element.19), channel_id=1, replica_groups={{0,128,256,384},{64,192,320,448},{1,129,257,385},{65,193,321,449},{2,13..., dimensions={0} | all-to-all | bytes 786432 | tf_op jit(solution)/shard_map/all_to_all | solution.py:274
  36.8 8.8 %collective-permute-start.4 = (bf16[256,128]{1,0:T(8,128)(2,1)S(1)}, bf16[256,128]{1,0:T(8,128)(2,1)S(1)}, u32[]{:S(2)}, u32[]{:S(2)}) collective-permute-start(bf16[256,128]{1,0:T(8,128)(2,1)S(1)} %slice_reduce_fusion), channel_id=1, source_target_pairs={{1,0},{2,1},{3,2},{4,387},{5,4},{6,5},{7,6},{8,391},{9,8},{10,9},{... | collective-permute-start | bytes 196616 | tf_op jit(solution)/shard_map/ppermute | solution.py:32
  45.6 1.9 %collective-permute-start.5 = (bf16[128,128]{1,0:T(8,128)(2,1)S(1)}, bf16[128,128]{1,0:T(8,128)(2,1)S(1)}, u32[]{:S(2)}, u32[]{:S(2)}) collective-permute-start(bf16[128,128]{1,0:T(8,128)(2,1)S(1)} %slice_reduce_fusion.1), channel_id=1, source_target_pairs={{0,0},{1,1},{2,2},{3,3},{4,4},{5,5},{6,6},{7,7},{8,8},{9,9},{10,10... | collective-permute-start | bytes 98312 | tf_op jit(solution)/shard_map/ppermute | solution.py:32
  47.5 3.3 %collective-permute-done.5.own_ref = bf16[128,128]{1,0:T(8,128)(2,1)S(1)} collective-permute-done((bf16[128,128]{1,0:T(8,128)(2,1)S(1)}, bf16[128,128]{1,0:T(8,128)(2,1)S(1)}, u32[]{:S(2)}, u32[]{:S(2)}) %collective-permute-start.5) | collective-permute-done | bytes 32800 | tf_op jit(solution)/shard_map/ppermute | solution.py:32
  50.8 0.0 collective-permute-done.4.back_ref
  50.8 1.9 %collective-permute-start.6 = (bf16[128,1408]{1,0:T(8,128)(2,1)S(1)}, bf16[128,1408]{1,0:T(8,128)(2,1)S(1)}, u32[]{:S(2)}, u32[]{:S(2)}) collective-permute-start(bf16[128,1408]{1,0:T(8,128)(2,1)S(1)} %pad_maximum_fusion), channel_id=1, source_target_pairs={{0,64},{1,65},{2,66},{3,67},{4,68},{5,69},{6,70},{7,71},{8,72},{9,... | collective-permute-start | bytes 1081352 | tf_op jit(solution)/shard_map/ppermute | solution.py:32
  52.8 1.6 %collective-permute-done.6.swapped_ref = bf16[128,1408]{1,0:T(8,128)(2,1)S(1)} collective-permute-done((bf16[128,1408]{1,0:T(8,128)(2,1)S(1)}, bf16[128,1408]{1,0:T(8,128)(2,1)S(1)}, u32[]{:S(2)}, u32[]{:S(2)}) %collective-permute-start.6) | collective-permute-done | bytes 360480 | tf_op jit(solution)/shard_map/ppermute | solution.py:32
  54.4 0.9 %finish.1 = (bf16[128,2560]{1,0:T(8,128)(2,1)}, f32[64,128]{1,0:T(8,128)}, f32[64,128]{1,0:T(8,128)}) custom-call(bf16[128,128]{1,0:T(8,128)(2,1)S(1)} %collective-permute-done.5.own_ref, bf16[256,128]{1,0:T(8,128)(2,1)S(1)} %collective-permute-done.4.back_ref, bf16[128,1408]{1,0:T(8,128)(2,1)S(1)} %collective-permute-done.6.swapped_ref, ...), custom_call_target="tpu_custom_call" | custom-call | tf_op jit(solution)/shard_map/finish/pallas_call | solution.py:279
  (4 shorter events, 0.1 us)
Async XLA Ops:
  1.5 12.6 %collective-permute-start = (bf16[528,128]{1,0:T(8,128)(2,1)S(1)}, bf16[528,128]{1,0:T(8,128)(2,1)S(1)}, u32[]{:S(2)}, u32[]{:S(2)}) collective-permute-start(bf16[528,128]{1,0:T(8,128)(2,1)S(1)} %pack_halo.1), channel_id=1, source_target_pairs={{0,1},{1,2},{2,3},{3,388},{4,5},{5,6},{6,7},{7,392},{8,9},{9,10},{... | collective-permute-start | bytes 405512 | tf_op jit(solution)/shard_map/ppermute | solution.py:32
  4.3 10.7 %collective-permute-start.1 = (bf16[528,128]{1,0:T(8,128)(2,1)S(1)}, bf16[528,128]{1,0:T(8,128)(2,1)S(1)}, u32[]{:S(2)}, u32[]{:S(2)}) collective-permute-start(bf16[528,128]{1,0:T(8,128)(2,1)S(1)} %pack_halo.1), channel_id=1, source_target_pairs={{0,2},{1,3},{2,388},{4,6},{5,7},{6,392},{8,10},{9,11},{10,396},{12... | collective-permute-start | bytes 405512 | tf_op jit(solution)/shard_map/ppermute | solution.py:32
  9.7 4.4 %copy-start.4 = (s32[128]{0:T(128)S(1)}, s32[128]{0:T(128)}, u32[]{:S(2)}) copy-start(s32[128]{0:T(128)} %param.9) | copy-start | bytes 1540
  10.9 4.9 %collective-permute-start.3 = (bf16[256,1280]{1,0:T(8,128)(2,1)S(1)}, bf16[256,1280]{1,0:T(8,128)(2,1)S(1)}, u32[]{:S(2)}, u32[]{:S(2)}) collective-permute-start(bf16[256,1280]{1,0:T(8,128)(2,1)S(1)} %pack_rows.1), channel_id=1, source_target_pairs={{0,64},{1,65},{2,66},{3,67},{4,68},{5,69},{6,70},{7,71},{8,72},{9,... | collective-permute-start | bytes 1966088 | tf_op jit(solution)/shard_map/ppermute | solution.py:32
  14.3 0.8 %collective-permute-start.2 = (bf16[528,128]{1,0:T(8,128)(2,1)S(1)}, bf16[528,128]{1,0:T(8,128)(2,1)S(1)}, u32[]{:S(2)}, u32[]{:S(2)}) collective-permute-start(bf16[528,128]{1,0:T(8,128)(2,1)S(1)} %collective-permute-done.one_ref), channel_id=1, source_target_pairs={{0,1},{4,5},{8,9},{12,13},{16,17},{20,21},{24,25},{28,29},{32,33},... | collective-permute-start | bytes 405512 | tf_op jit(solution)/shard_map/ppermute | solution.py:32
  15.0 1.1 %copy-start = (bf16[1,128,2560]{2,1,0:T(8,128)(2,1)S(1)}, bf16[1,128,2560]{2,1,0:T(8,128)(2,1)}, u32[]{:S(2)}) copy-start(bf16[1,128,2560]{2,1,0:T(8,128)(2,1)} %param.5) | copy-start | bytes 1966084
  15.0 1.3 %copy-start.1 = (bf16[1,128,2560]{2,1,0:T(8,128)(2,1)S(1)}, bf16[1,128,2560]{2,1,0:T(8,128)(2,1)}, u32[]{:S(2)}) copy-start(bf16[1,128,2560]{2,1,0:T(8,128)(2,1)} %param.8) | copy-start | bytes 1966084
  15.0 1.3 %copy-start.2 = (bf16[128,512]{1,0:T(8,128)(2,1)S(1)}, bf16[128,512]{1,0:T(8,128)(2,1)}, u32[]{:S(2)}) copy-start(bf16[128,512]{1,0:T(8,128)(2,1)} %k_ref.3) | copy-start | bytes 393220
  15.0 1.3 %copy-start.3 = (bf16[128,512]{1,0:T(8,128)(2,1)S(1)}, bf16[128,512]{1,0:T(8,128)(2,1)}, u32[]{:S(2)}) copy-start(bf16[128,512]{1,0:T(8,128)(2,1)} %v_ref.3) | copy-start | bytes 393220
  36.8 14.0 %collective-permute-start.4 = (bf16[256,128]{1,0:T(8,128)(2,1)S(1)}, bf16[256,128]{1,0:T(8,128)(2,1)S(1)}, u32[]{:S(2)}, u32[]{:S(2)}) collective-permute-start(bf16[256,128]{1,0:T(8,128)(2,1)S(1)} %slice_reduce_fusion), channel_id=1, source_target_pairs={{1,0},{2,1},{3,2},{4,387},{5,4},{6,5},{7,6},{8,391},{9,8},{10,9},{... | collective-permute-start | bytes 196616 | tf_op jit(solution)/shard_map/ppermute | solution.py:32
  45.6 5.2 %collective-permute-start.5 = (bf16[128,128]{1,0:T(8,128)(2,1)S(1)}, bf16[128,128]{1,0:T(8,128)(2,1)S(1)}, u32[]{:S(2)}, u32[]{:S(2)}) collective-permute-start(bf16[128,128]{1,0:T(8,128)(2,1)S(1)} %slice_reduce_fusion.1), channel_id=1, source_target_pairs={{0,0},{1,1},{2,2},{3,3},{4,4},{5,5},{6,6},{7,7},{8,8},{9,9},{10,10... | collective-permute-start | bytes 98312 | tf_op jit(solution)/shard_map/ppermute | solution.py:32
  50.8 3.6 %collective-permute-start.6 = (bf16[128,1408]{1,0:T(8,128)(2,1)S(1)}, bf16[128,1408]{1,0:T(8,128)(2,1)S(1)}, u32[]{:S(2)}, u32[]{:S(2)}) collective-permute-start(bf16[128,1408]{1,0:T(8,128)(2,1)S(1)} %pad_maximum_fusion), channel_id=1, source_target_pairs={{0,64},{1,65},{2,66},{3,67},{4,68},{5,69},{6,70},{7,71},{8,72},{9,... | collective-permute-start | bytes 1081352 | tf_op jit(solution)/shard_map/ppermute | solution.py:32

commit v9 on v8

--- a/solution.py
+++ b/solution.py
@@ -123,51 +123,57 @@
 def attend(
     place_ref, near_ref, far_ref, q_ref, c_ref, oqc_ref, k_ref, v_ref, one_ref, two_ref, relay_ref, dq_ref, odq_ref, part_ref
 ):
-    slot = pl.program_id(0)
+    for slot in range(2):
+        attend_slot(
+            slot, place_ref, near_ref, far_ref, q_ref, c_ref, oqc_ref, k_ref, v_ref, one_ref, two_ref, relay_ref,
+            dq_ref, odq_ref, part_ref,
+        )
+
+
+def attend_slot(
+    slot, place_ref, near_ref, far_ref, q_ref, c_ref, oqc_ref, k_ref, v_ref, one_ref, two_ref, relay_ref,
+    dq_ref, odq_ref, part_ref,
+):
     group = group_of(place_ref[0], slot)
 
-    def lanes(start, size=DH):
-        return pl.ds(pl.multiple_of(start, DH), size)
+    def lanes(start):
+        return pl.ds(pl.multiple_of(start, DH), DH)
 
     def rows(i):
-        return pl.ds(pl.multiple_of((2 * slot + i) * TOK, TOK), TOK)
+        return slice((2 * slot + i) * TOK, (2 * slot + i + 1) * TOK)
 
     keys, values = [
         jnp.concatenate([ref[:, lanes(group * DH)], one_ref[rows(i)], two_ref[rows(i)] + relay_ref[rows(i)]], 0)
         for i, ref in enumerate((k_ref, v_ref))
     ]
     bias = jnp.concatenate([near_ref[...], far_ref[...]], 0)
-    grad_k = jnp.zeros((3 * TOK, DH), jnp.float32)
-    grad_v = jnp.zeros((3 * TOK, DH), jnp.float32)
-    for mine in (True, False):
-        start = (group if mine else slot) * WIDE
-        queries, cots = [], []
-        for h in range(RATIO):
-            at = lanes(start + h * DH)
-            queries.append(q_ref[:, at] if mine else oqc_ref[:TOK, at])
-            cots.append(c_ref[:, at] if mine else oqc_ref[TOK:, at])
-        queries, cots = jnp.concatenate(queries, 0), jnp.concatenate(cots, 0)
-        scores = lax.dot_general(keys, queries, NT, preferred_element_type=jnp.float32)
-        grad_probs = lax.dot_general(values, cots, NT, preferred_element_type=jnp.float32)
-        probs_low, scaled_low = [], []
-        for h in range(RATIO):
-            at = slice(h * TOK, (h + 1) * TOK)
-            s = scores[:, at] * (SCALE * LOG2E) + bias
-            e = jnp.exp2(s - jnp.max(s, 0, keepdims=True))
-            p = e * (1.0 / jnp.sum(e, 0, keepdims=True))
-            low = p.astype(jnp.bfloat16)
-            g = grad_probs[:, at]
-            dot = jnp.sum(low.astype(jnp.float32) * g, 0, keepdims=True)
-            probs_low.append(low)
-            scaled_low.append((p * (g - dot) * SCALE).astype(jnp.bfloat16))
-        probs_low = jnp.concatenate(probs_low, 1)
-        scaled_low = jnp.concatenate(scaled_low, 1)
-        grad_v += jnp.dot(probs_low, cots, preferred_element_type=jnp.float32)
-        grad_k += jnp.dot(scaled_low, queries, preferred_element_type=jnp.float32)
-        grad_q = lax.dot_general(keys, scaled_low, TN, preferred_element_type=jnp.float32)
-        out = dq_ref if mine else odq_ref
-        for h in range(RATIO):
-            out[:, lanes(slot * WIDE + h * DH)] = grad_q[:, h * TOK : (h + 1) * TOK].T.astype(jnp.bfloat16)
+    queries, cots = [], []
+    for h in range(RATIO):
+        queries.append(q_ref[:, lanes(group * WIDE + h * DH)])
+        cots.append(c_ref[:, lanes(group * WIDE + h * DH)])
+    for h in range(RATIO):
+        queries.append(oqc_ref[:TOK, lanes(slot * WIDE + h * DH)])
+        cots.append(oqc_ref[TOK:, lanes(slot * WIDE + h * DH)])
+    queries, cots = jnp.concatenate(queries, 0), jnp.concatenate(cots, 0)
+    scores = lax.dot_general(keys, queries, NT, preferred_element_type=jnp.float32)
+    grad_probs = lax.dot_general(values, cots, NT, preferred_element_type=jnp.float32)
+    probs_low, scaled_low = [], []
+    for h in range(2 * RATIO):
+        at = slice(h * TOK, (h + 1) * TOK)
+        s = scores[:, at] * (SCALE * LOG2E) + bias
+        e = jnp.exp2(s - jnp.max(s, 0, keepdims=True))
+        p = e * (1.0 / jnp.sum(e, 0, keepdims=True))
+        g = grad_probs[:, at]
+        dot = jnp.sum(p * g, 0, keepdims=True)
+        probs_low.append(p.astype(jnp.bfloat16))
+        scaled_low.append((p * (g - dot) * SCALE).astype(jnp.bfloat16))
+    probs_low, scaled_low = jnp.concatenate(probs_low, 1), jnp.concatenate(scaled_low, 1)
+    grad_v = jnp.dot(probs_low, cots, preferred_element_type=jnp.float32)
+    grad_k = jnp.dot(scaled_low, queries, preferred_element_type=jnp.float32)
+    grad_q = lax.dot_general(keys, scaled_low, TN, preferred_element_type=jnp.float32).astype(jnp.bfloat16)
+    for h in range(2 * RATIO):
+        out = dq_ref if h < RATIO else odq_ref
+        out[:, lanes(slot * WIDE + h % RATIO * DH)] = grad_q[:, h * TOK : (h + 1) * TOK].T
     half = DH // 2
     grad_k = grad_k.astype(jnp.bfloat16)
     grad_v = grad_v.astype(jnp.bfloat16)
@@ -259,7 +265,6 @@
     )(ids, two, relay)
     own_q, other_q, part = pl.pallas_call(
         attend,
-        grid=(2,),
         in_specs=[pl.BlockSpec(memory_space=pltpu.SMEM)] + [vmem] * 10,
         out_specs=(vmem,) * 3,
         out_shape=(

time: 55.7 us -> 54.9 us (0.986)
  the two profiles are of different devices: /device:TPU:389 before, /device:TPU:5 now
where the time goes in v9:
time: 54.9 us; the launch traced here: 54.5 us
  starting transfers between devices  24.5 us (45%)
  blocking collectives  15.3 us (28%)
  Pallas kernels  7.59 us (14%)
  waiting for transfers between devices  5.5 us (10%)
  between operations  0.81 us (1%)
  local copies, waits for them, and re-layouts  0.61 us (1%)
    ppermute x7, starting transfers between devices, permuted(): return lax.ppermute(x, AXES, found)  24.5 us
    all_to_all x1, blocking collectives, on_device(): shares = lax.all_to_all(part, 'section', 0, 0, axis_index_groups=chips)  15.3 us
    ppermute x7, waiting for transfers between devices, permuted(): return lax.ppermute(x, AXES, found)  5.5 us
    pallas_call x1, Pallas kernels, on_device(): pl.pallas_call(attend, in_specs=[pl.BlockSpec(memory_space=pltpu.SMEM)] +...  4.3 us
    pallas_call x1, Pallas kernels, on_device(): pl.pallas_call(pack_rows, in_specs=[hbm] * 2, out_specs=vmem, out_shape=j...  1.21 us
  transfers between devices with their start and end apart: 7, of which 3 were waited for; matrix products, arithmetic and copies ran while one was open for 0% of the time, Pallas kernels for 3%

profile of v9, /device:TPU:5, one launch (start us, length us, event | category | flops | bytes accessed | tf_op | source)
XLA Modules:
  0.0 54.5 jit_solution(7851512975544553303)
XLA Ops:
  0.6 0.9 %pack_halo.1 = bf16[528,128]{1,0:T(8,128)(2,1)S(1)} custom-call(s32[1,128]{1,0:T(1,128)} %bitcast.13, bf16[128,512]{1,0:T(8,128)(2,1)} %k_ref.3, bf16[128,512]{1,0:T(8,128)(2,1)} %v_ref.3), custom_call_target="tpu_custom_call" | custom-call | tf_op jit(solution)/shard_map/pack_halo/pallas_call | solution.py:223
  1.5 2.8 %collective-permute-start = (bf16[528,128]{1,0:T(8,128)(2,1)S(1)}, bf16[528,128]{1,0:T(8,128)(2,1)S(1)}, u32[]{:S(2)}, u32[]{:S(2)}) collective-permute-start(bf16[528,128]{1,0:T(8,128)(2,1)S(1)} %pack_halo.1), channel_id=1, source_target_pairs={{0,1},{1,2},{2,3},{3,388},{4,5},{5,6},{6,7},{7,392},{8,9},{9,10},{... | collective-permute-start | bytes 405512 | tf_op jit(solution)/shard_map/ppermute | solution.py:32
  4.3 5.3 %collective-permute-start.1 = (bf16[528,128]{1,0:T(8,128)(2,1)S(1)}, bf16[528,128]{1,0:T(8,128)(2,1)S(1)}, u32[]{:S(2)}, u32[]{:S(2)}) collective-permute-start(bf16[528,128]{1,0:T(8,128)(2,1)S(1)} %pack_halo.1), channel_id=1, source_target_pairs={{0,2},{1,3},{2,388},{4,6},{5,7},{6,392},{8,10},{9,11},{10,396},{12... | collective-permute-start | bytes 405512 | tf_op jit(solution)/shard_map/ppermute | solution.py:32
  9.7 0.0 copy-start.4
  9.7 1.2 %pack_rows.1 = bf16[256,1280]{1,0:T(8,128)(2,1)S(1)} custom-call(bf16[128,2560]{1,0:T(8,128)(2,1)} %bitcast.9, bf16[128,2560]{1,0:T(8,128)(2,1)} %bitcast.11), custom_call_target="tpu_custom_call" | custom-call | tf_op jit(solution)/shard_map/pack_rows/pallas_call | solution.py:234
  10.9 3.1 %collective-permute-start.3 = (bf16[256,1280]{1,0:T(8,128)(2,1)S(1)}, bf16[256,1280]{1,0:T(8,128)(2,1)S(1)}, u32[]{:S(2)}, u32[]{:S(2)}) collective-permute-start(bf16[256,1280]{1,0:T(8,128)(2,1)S(1)} %pack_rows.1), channel_id=1, source_target_pairs={{0,64},{1,65},{2,66},{3,67},{4,68},{5,69},{6,70},{7,71},{8,72},{9,... | collective-permute-start | bytes 1966088 | tf_op jit(solution)/shard_map/ppermute | solution.py:32
  14.1 0.0 collective-permute-done.one_ref
  14.1 0.0 copy-done.4
  14.1 0.2 mask_near.1.near_ref
  14.3 0.7 %collective-permute-start.2 = (bf16[528,128]{1,0:T(8,128)(2,1)S(1)}, bf16[528,128]{1,0:T(8,128)(2,1)S(1)}, u32[]{:S(2)}, u32[]{:S(2)}) collective-permute-start(bf16[528,128]{1,0:T(8,128)(2,1)S(1)} %collective-permute-done.one_ref), channel_id=1, source_target_pairs={{0,1},{4,5},{8,9},{12,13},{16,17},{20,21},{24,25},{28,29},{32,33},... | collective-permute-start | bytes 405512 | tf_op jit(solution)/shard_map/ppermute | solution.py:32
  15.0 0.1 pad_add_fusion.place_ref
  15.0 0.0 copy-start
  15.0 0.0 copy-start.1
  15.0 0.0 copy-start.2
  15.0 0.0 copy-start.3
  15.0 0.0 collective-permute-done.1.two_ref
  15.1 0.0 collective-permute-done.2.relay_ref
  15.1 0.2 mask_far.1.far_ref
  15.2 0.5 collective-permute-done.3.oqc_ref
  15.8 0.4 copy-done
  16.1 0.2 copy-done.1
  16.3 0.0 copy-done.2
  16.3 0.0 copy-done.3
  16.4 4.3 %attend.1 = (bf16[128,1280]{1,0:T(8,128)(2,1)S(1)}, bf16[128,1280]{1,0:T(8,128)(2,1)S(1)}, bf16[4,384,128]{2,1,0:T(8,128)(2,1)S(1)}) custom-call(s32[4]{0:T(128)S(1)} %pad_add_fusion.place_ref, f32[256,128]{1,0:T(8,128)S(1)} %mask_near.1.near_ref, f32[128,128]{1,0:T(8,128)S(1)} %mask_far.1.far_ref, bf16[128,2560]{1,0:T(8,128)(2,1)S(1)} %bitcast.10, ...), custom_call_target="tpu_custom_call" | custom-call | tf_op jit(solution)/shard_map/attend/pallas_call | solution.py:266
  20.7 15.3 %all_to_all.5 = bf16[4,384,128]{2,1,0:T(8,128)(2,1)S(1)} all-to-all(bf16[4,384,128]{2,1,0:T(8,128)(2,1)S(1)} %get-tuple-element.19), channel_id=1, replica_groups={{0,128,256,384},{64,192,320,448},{1,129,257,385},{65,193,321,449},{2,13..., dimensions={0} | all-to-all | bytes 786432 | tf_op jit(solution)/shard_map/all_to_all | solution.py:279
  36.0 8.7 %collective-permute-start.4 = (bf16[256,128]{1,0:T(8,128)(2,1)S(1)}, bf16[256,128]{1,0:T(8,128)(2,1)S(1)}, u32[]{:S(2)}, u32[]{:S(2)}) collective-permute-start(bf16[256,128]{1,0:T(8,128)(2,1)S(1)} %slice_reduce_fusion), channel_id=1, source_target_pairs={{1,0},{2,1},{3,2},{4,387},{5,4},{6,5},{7,6},{8,391},{9,8},{10,9},{... | collective-permute-start | bytes 196616 | tf_op jit(solution)/shard_map/ppermute | solution.py:32
  44.7 1.9 %collective-permute-start.5 = (bf16[128,128]{1,0:T(8,128)(2,1)S(1)}, bf16[128,128]{1,0:T(8,128)(2,1)S(1)}, u32[]{:S(2)}, u32[]{:S(2)}) collective-permute-start(bf16[128,128]{1,0:T(8,128)(2,1)S(1)} %slice_reduce_fusion.1), channel_id=1, source_target_pairs={{0,0},{1,1},{2,2},{3,3},{4,4},{5,5},{6,6},{7,7},{8,8},{9,9},{10,10... | collective-permute-start | bytes 98312 | tf_op jit(solution)/shard_map/ppermute | solution.py:32
  46.6 3.3 %collective-permute-done.5.own_ref = bf16[128,128]{1,0:T(8,128)(2,1)S(1)} collective-permute-done((bf16[128,128]{1,0:T(8,128)(2,1)S(1)}, bf16[128,128]{1,0:T(8,128)(2,1)S(1)}, u32[]{:S(2)}, u32[]{:S(2)}) %collective-permute-start.5) | collective-permute-done | bytes 32800 | tf_op jit(solution)/shard_map/ppermute | solution.py:32
  49.9 0.0 collective-permute-done.4.back_ref
  50.0 1.9 %collective-permute-start.6 = (bf16[128,1408]{1,0:T(8,128)(2,1)S(1)}, bf16[128,1408]{1,0:T(8,128)(2,1)S(1)}, u32[]{:S(2)}, u32[]{:S(2)}) collective-permute-start(bf16[128,1408]{1,0:T(8,128)(2,1)S(1)} %pad_maximum_fusion), channel_id=1, source_target_pairs={{0,64},{1,65},{2,66},{3,67},{4,68},{5,69},{6,70},{7,71},{8,72},{9,... | collective-permute-start | bytes 1081352 | tf_op jit(solution)/shard_map/ppermute | solution.py:32
  51.9 1.6 %collective-permute-done.6.swapped_ref = bf16[128,1408]{1,0:T(8,128)(2,1)S(1)} collective-permute-done((bf16[128,1408]{1,0:T(8,128)(2,1)S(1)}, bf16[128,1408]{1,0:T(8,128)(2,1)S(1)}, u32[]{:S(2)}, u32[]{:S(2)}) %collective-permute-start.6) | collective-permute-done | bytes 360480 | tf_op jit(solution)/shard_map/ppermute | solution.py:32
  53.6 0.9 %finish.1 = (bf16[128,2560]{1,0:T(8,128)(2,1)}, f32[64,128]{1,0:T(8,128)}, f32[64,128]{1,0:T(8,128)}) custom-call(bf16[128,128]{1,0:T(8,128)(2,1)S(1)} %collective-permute-done.5.own_ref, bf16[256,128]{1,0:T(8,128)(2,1)S(1)} %collective-permute-done.4.back_ref, bf16[128,1408]{1,0:T(8,128)(2,1)S(1)} %collective-permute-done.6.swapped_ref, ...), custom_call_target="tpu_custom_call" | custom-call | tf_op jit(solution)/shard_map/finish/pallas_call | solution.py:284
  (4 shorter events, 0.1 us)
Async XLA Ops:
  1.5 12.6 %collective-permute-start = (bf16[528,128]{1,0:T(8,128)(2,1)S(1)}, bf16[528,128]{1,0:T(8,128)(2,1)S(1)}, u32[]{:S(2)}, u32[]{:S(2)}) collective-permute-start(bf16[528,128]{1,0:T(8,128)(2,1)S(1)} %pack_halo.1), channel_id=1, source_target_pairs={{0,1},{1,2},{2,3},{3,388},{4,5},{5,6},{6,7},{7,392},{8,9},{9,10},{... | collective-permute-start | bytes 405512 | tf_op jit(solution)/shard_map/ppermute | solution.py:32
  4.3 10.7 %collective-permute-start.1 = (bf16[528,128]{1,0:T(8,128)(2,1)S(1)}, bf16[528,128]{1,0:T(8,128)(2,1)S(1)}, u32[]{:S(2)}, u32[]{:S(2)}) collective-permute-start(bf16[528,128]{1,0:T(8,128)(2,1)S(1)} %pack_halo.1), channel_id=1, source_target_pairs={{0,2},{1,3},{2,388},{4,6},{5,7},{6,392},{8,10},{9,11},{10,396},{12... | collective-permute-start | bytes 405512 | tf_op jit(solution)/shard_map/ppermute | solution.py:32
  9.7 4.4 %copy-start.4 = (s32[128]{0:T(128)S(1)}, s32[128]{0:T(128)}, u32[]{:S(2)}) copy-start(s32[128]{0:T(128)} %param.9) | copy-start | bytes 1540
  10.9 4.9 %collective-permute-start.3 = (bf16[256,1280]{1,0:T(8,128)(2,1)S(1)}, bf16[256,1280]{1,0:T(8,128)(2,1)S(1)}, u32[]{:S(2)}, u32[]{:S(2)}) collective-permute-start(bf16[256,1280]{1,0:T(8,128)(2,1)S(1)} %pack_rows.1), channel_id=1, source_target_pairs={{0,64},{1,65},{2,66},{3,67},{4,68},{5,69},{6,70},{7,71},{8,72},{9,... | collective-permute-start | bytes 1966088 | tf_op jit(solution)/shard_map/ppermute | solution.py:32
  14.3 0.8 %collective-permute-start.2 = (bf16[528,128]{1,0:T(8,128)(2,1)S(1)}, bf16[528,128]{1,0:T(8,128)(2,1)S(1)}, u32[]{:S(2)}, u32[]{:S(2)}) collective-permute-start(bf16[528,128]{1,0:T(8,128)(2,1)S(1)} %collective-permute-done.one_ref), channel_id=1, source_target_pairs={{0,1},{4,5},{8,9},{12,13},{16,17},{20,21},{24,25},{28,29},{32,33},... | collective-permute-start | bytes 405512 | tf_op jit(solution)/shard_map/ppermute | solution.py:32
  15.0 1.1 %copy-start = (bf16[1,128,2560]{2,1,0:T(8,128)(2,1)S(1)}, bf16[1,128,2560]{2,1,0:T(8,128)(2,1)}, u32[]{:S(2)}) copy-start(bf16[1,128,2560]{2,1,0:T(8,128)(2,1)} %param.5) | copy-start | bytes 1966084
  15.0 1.3 %copy-start.1 = (bf16[1,128,2560]{2,1,0:T(8,128)(2,1)S(1)}, bf16[1,128,2560]{2,1,0:T(8,128)(2,1)}, u32[]{:S(2)}) copy-start(bf16[1,128,2560]{2,1,0:T(8,128)(2,1)} %param.8) | copy-start | bytes 1966084
  15.0 1.3 %copy-start.2 = (bf16[128,512]{1,0:T(8,128)(2,1)S(1)}, bf16[128,512]{1,0:T(8,128)(2,1)}, u32[]{:S(2)}) copy-start(bf16[128,512]{1,0:T(8,128)(2,1)} %k_ref.3) | copy-start | bytes 393220
  15.0 1.3 %copy-start.3 = (bf16[128,512]{1,0:T(8,128)(2,1)S(1)}, bf16[128,512]{1,0:T(8,128)(2,1)}, u32[]{:S(2)}) copy-start(bf16[128,512]{1,0:T(8,128)(2,1)} %v_ref.3) | copy-start | bytes 393220
  36.0 14.0 %collective-permute-start.4 = (bf16[256,128]{1,0:T(8,128)(2,1)S(1)}, bf16[256,128]{1,0:T(8,128)(2,1)S(1)}, u32[]{:S(2)}, u32[]{:S(2)}) collective-permute-start(bf16[256,128]{1,0:T(8,128)(2,1)S(1)} %slice_reduce_fusion), channel_id=1, source_target_pairs={{1,0},{2,1},{3,2},{4,387},{5,4},{6,5},{7,6},{8,391},{9,8},{10,9},{... | collective-permute-start | bytes 196616 | tf_op jit(solution)/shard_map/ppermute | solution.py:32
  44.7 5.2 %collective-permute-start.5 = (bf16[128,128]{1,0:T(8,128)(2,1)S(1)}, bf16[128,128]{1,0:T(8,128)(2,1)S(1)}, u32[]{:S(2)}, u32[]{:S(2)}) collective-permute-start(bf16[128,128]{1,0:T(8,128)(2,1)S(1)} %slice_reduce_fusion.1), channel_id=1, source_target_pairs={{0,0},{1,1},{2,2},{3,3},{4,4},{5,5},{6,6},{7,7},{8,8},{9,9},{10,10... | collective-permute-start | bytes 98312 | tf_op jit(solution)/shard_map/ppermute | solution.py:32
  50.0 3.6 %collective-permute-start.6 = (bf16[128,1408]{1,0:T(8,128)(2,1)S(1)}, bf16[128,1408]{1,0:T(8,128)(2,1)S(1)}, u32[]{:S(2)}, u32[]{:S(2)}) collective-permute-start(bf16[128,1408]{1,0:T(8,128)(2,1)S(1)} %pad_maximum_fusion), channel_id=1, source_target_pairs={{0,64},{1,65},{2,66},{3,67},{4,68},{5,69},{6,70},{7,71},{8,72},{9,... | collective-permute-start | bytes 1081352 | tf_op jit(solution)/shard_map/ppermute | solution.py:32

commit v10 on v9

--- a/solution.py
+++ b/solution.py
@@ -14,8 +14,9 @@
 SCALE = DH ** (-0.5)
 LOG2E = 1.4426950408889634
 NEG = -1e30
-FAR_FLOPS = 1 << 31
-NEAR_FLOPS = 1 << 33
+FAR_FLOPS = 1 << 33
+NEAR_FLOPS = 1 << 30
+ADD_FLOPS = 17 << 27
 AXES = ("section", "ctx")
 NT = (((1,), (1,)), ((), ()))
 TN = (((0,), (0,)), ((), ()))
@@ -32,10 +33,8 @@
     return lax.ppermute(x, AXES, found)
 
 
-def shifted(x, by, places=range(ROW)):
+def shifted(x, by):
     def target(s, c):
-        if (c + by) % ROW not in places:
-            return (s, -1)
         leaves = c // ROW != (c + by) // ROW
         return ((3 - s // 2) * 2 + s % 2 if leaves else s, c + by)
 
@@ -98,9 +97,9 @@
     run(copies)
 
 
-def halo_mask(ids, *halos):
+def halo_mask(ids, halo):
     first = ids[:, 0:1]
-    before = sum(halo[4 * TOK :].astype(jnp.float32)[0:1] for halo in halos)
+    before = halo[4 * TOK :].astype(jnp.float32)[0:1]
     held = jnp.sum(jnp.where(before == first + 1.0, 1.0, 0.0), -1, keepdims=True)
     row = lax.broadcasted_iota(jnp.int32, (TOK, TOK), 0).astype(jnp.float32)
     wide = jnp.broadcast_to(ids, (TOK, TOK))
@@ -116,22 +115,22 @@
     out_ref[TOK:] = halo_mask(ids, one_ref)
 
 
-def mask_far(ids_ref, two_ref, relay_ref, out_ref):
-    out_ref[...] = halo_mask(ids_ref[...].astype(jnp.float32), two_ref, relay_ref)
+def mask_far(ids_ref, two_ref, out_ref):
+    out_ref[...] = halo_mask(ids_ref[...].astype(jnp.float32), two_ref)
 
 
 def attend(
-    place_ref, near_ref, far_ref, q_ref, c_ref, oqc_ref, k_ref, v_ref, one_ref, two_ref, relay_ref, dq_ref, odq_ref, part_ref
+    place_ref, near_ref, far_ref, q_ref, c_ref, oqc_ref, k_ref, v_ref, one_ref, two_ref, dq_ref, odq_ref, part_ref
 ):
     for slot in range(2):
         attend_slot(
-            slot, place_ref, near_ref, far_ref, q_ref, c_ref, oqc_ref, k_ref, v_ref, one_ref, two_ref, relay_ref,
+            slot, place_ref, near_ref, far_ref, q_ref, c_ref, oqc_ref, k_ref, v_ref, one_ref, two_ref,
             dq_ref, odq_ref, part_ref,
         )
 
 
 def attend_slot(
-    slot, place_ref, near_ref, far_ref, q_ref, c_ref, oqc_ref, k_ref, v_ref, one_ref, two_ref, relay_ref,
+    slot, place_ref, near_ref, far_ref, q_ref, c_ref, oqc_ref, k_ref, v_ref, one_ref, two_ref,
     dq_ref, odq_ref, part_ref,
 ):
     group = group_of(place_ref[0], slot)
@@ -143,7 +142,7 @@
         return slice((2 * slot + i) * TOK, (2 * slot + i + 1) * TOK)
 
     keys, values = [
-        jnp.concatenate([ref[:, lanes(group * DH)], one_ref[rows(i)], two_ref[rows(i)] + relay_ref[rows(i)]], 0)
+        jnp.concatenate([ref[:, lanes(group * DH)], one_ref[rows(i)], two_ref[rows(i)]], 0)
         for i, ref in enumerate((k_ref, v_ref))
     ]
     bias = jnp.concatenate([near_ref[...], far_ref[...]], 0)
@@ -189,7 +188,13 @@
             part_ref[carrier, at, :] = shares[side][block * TOK : (block + 1) * TOK]
 
 
-def finish(own_ref, back_ref, swapped_ref, own_q_ref, dq_ref, dk_ref, dv_ref, total_ref, sems):
+def add_up(own_ref, back_ref, swapped_ref, out_ref):
+    core = lax.axis_index("section") % 2
+    mine = back_ref[pl.ds(pl.multiple_of(core * TOK, TOK), TOK), :]
+    out_ref[...] = sum(x.astype(jnp.float32) for x in (own_ref[...], mine, swapped_ref[...])).T
+
+
+def finish(total_ref, own_q_ref, swapped_ref, dq_ref, dk_ref, dv_ref, sems):
     core = lax.axis_index("section") % 2
     half = DH // 2
     copies = []
@@ -197,16 +202,9 @@
         for slot, group in enumerate(core_groups(core if i == 0 else 1 - core)):
             src = ref.at[:, pl.ds(slot * WIDE, WIDE)]
             copies.append(pltpu.make_async_copy(src, dq_ref.at[:, columns(group, WIDE)], sems.at[2 * i + slot]))
-    for copy in copies:
-        copy.start()
-    mine = back_ref[pl.ds(pl.multiple_of(core * TOK, TOK), TOK), :]
-    total = own_ref[...].astype(jnp.float32) + mine.astype(jnp.float32) + swapped_ref[:, 2 * WIDE :].astype(jnp.float32)
-    total_ref[...] = total.T
     for i, ref in enumerate((dk_ref, dv_ref)):
         copies.append(pltpu.make_async_copy(total_ref.at[pl.ds(i * half, half)], ref, sems.at[4 + i]))
-        copies[-1].start()
-    for copy in copies:
-        copy.wait()
+    run(copies)
 
 
 def on_device(queries, keys, values, cotangent, segment_ids):
@@ -229,7 +227,7 @@
         compiler_params=small,
         name="pack_halo",
     )(*(pltpu.with_memory_space_constraint(x, pltpu.HBM) for x in (ids, keys, values)))
-    one, two = shifted(sent, 1), shifted(sent, 2, (0, 2, 3))
+    one, two = shifted(sent, 1), shifted(sent, 2)
     q, c, _ = lax.optimization_barrier((q, c, sent))
     rows = pl.pallas_call(
         pack_rows,
@@ -249,23 +247,21 @@
         cost_estimate=pl.CostEstimate(flops=NEAR_FLOPS, bytes_accessed=0, transcendentals=0),
         name="mask_near",
     )(ids, one)
-    one, near = lax.optimization_barrier((one, near))
-    relay = shifted(one, 1, (1,))
     rows = other_core(rows)
     place = jnp.stack([core, core, (me % ROW < 1).astype(core.dtype), (me % ROW < 2).astype(core.dtype)])
     place = place.astype(jnp.int32)
     far = pl.pallas_call(
         mask_far,
-        in_specs=[vmem] * 3,
+        in_specs=[vmem] * 2,
         out_specs=vmem,
         out_shape=jax.ShapeDtypeStruct((tok, tok), jnp.float32),
         compiler_params=small,
         cost_estimate=pl.CostEstimate(flops=FAR_FLOPS, bytes_accessed=0, transcendentals=0),
         name="mask_far",
-    )(ids, two, relay)
+    )(ids, two)
     own_q, other_q, part = pl.pallas_call(
         attend,
-        in_specs=[pl.BlockSpec(memory_space=pltpu.SMEM)] + [vmem] * 10,
+        in_specs=[pl.BlockSpec(memory_space=pltpu.SMEM)] + [vmem] * 9,
         out_specs=(vmem,) * 3,
         out_shape=(
             jax.ShapeDtypeStruct((tok, 2 * WIDE), jnp.bfloat16),
@@ -274,26 +270,37 @@
         ),
         compiler_params=pltpu.CompilerParams(vmem_limit_bytes=24 * 1024 * 1024),
         name="attend",
-    )(place, near, far, q, c, rows, keys, values, one, two, relay)
+    )(place, near, far, q, c, rows, keys, values, one, two)
     chips = [[s for s in range(8) if s % 2 == parity] for parity in range(2)]
     shares = lax.all_to_all(part, "section", 0, 0, axis_index_groups=chips)
+    other_q, shares = lax.optimization_barrier((other_q, shares))
     back = returned(jnp.sum(shares[:, tok:].astype(jnp.float32), 0).astype(jnp.bfloat16))
     total = to_owner(jnp.sum(shares[:, :tok].astype(jnp.float32), 0).astype(jnp.bfloat16))
     back, total = lax.optimization_barrier((back, total))
-    swapped = other_core(jnp.concatenate([other_q, jnp.where(core == 0, back[tok:], back[:tok])], 1))
+    swapped = other_core(jnp.where(core == 0, back[tok:], back[:tok]))
+    swapped_q = other_core(other_q)
+    total = pl.pallas_call(
+        add_up,
+        in_specs=[vmem] * 3,
+        out_specs=vmem,
+        out_shape=jax.ShapeDtypeStruct((DH, tok), jnp.float32),
+        compiler_params=small,
+        cost_estimate=pl.CostEstimate(flops=ADD_FLOPS, bytes_accessed=0, transcendentals=0),
+        name="add_up",
+    )(total, back, swapped)
     grad_q, grad_k, grad_v = pl.pallas_call(
         finish,
-        in_specs=[vmem] * 4,
+        in_specs=[vmem] * 3,
         out_specs=(hbm, hbm, hbm),
         out_shape=(
             jax.ShapeDtypeStruct(q.shape, jnp.bfloat16),
             jax.ShapeDtypeStruct((DH // 2, tok), jnp.float32),
             jax.ShapeDtypeStruct((DH // 2, tok), jnp.float32),
         ),
-        scratch_shapes=[pltpu.VMEM((DH, tok), jnp.float32), pltpu.SemaphoreType.DMA((6,))],
+        scratch_shapes=[pltpu.SemaphoreType.DMA((6,))],
         compiler_params=small,
         name="finish",
-    )(total, back, swapped, own_q)
+    )(total, own_q, swapped_q)
     return (grad_q[None], grad_k.T, grad_v.T)
 
 

time: 54.9 us -> 54.7 us (level)
  the two profiles are of different devices: /device:TPU:5 before, /device:TPU:261 now
where the time goes in v10:
time: 54.7 us; the launch traced here: 54.2 us
  starting transfers between devices  26.2 us (48%)
  blocking collectives  15.1 us (28%)
  Pallas kernels  7.66 us (14%)
  waiting for transfers between devices  3.19 us (6%)
  local copies, waits for them, and re-layouts  1.07 us (2%)
  between operations  0.82 us (1%)
    ppermute x7, starting transfers between devices, permuted(): return lax.ppermute(x, AXES, found)  26.2 us
    all_to_all x1, blocking collectives, on_device(): shares = lax.all_to_all(part, 'section', 0, 0, axis_index_groups=chips)  15.1 us
    pallas_call x1, Pallas kernels, on_device(): pl.pallas_call(attend, in_specs=[pl.BlockSpec(memory_space=pltpu.SMEM)] +...  4.26 us
    ppermute x7, waiting for transfers between devices, permuted(): return lax.ppermute(x, AXES, found)  3.19 us
    pallas_call x1, Pallas kernels, on_device(): pl.pallas_call(pack_rows, in_specs=[hbm] * 2, out_specs=vmem, out_shape=j...  1.21 us
  transfers between devices with their start and end apart: 7, of which 3 were waited for; matrix products, arithmetic and copies ran while one was open for 0% of the time, Pallas kernels for 3%

profile of v10, /device:TPU:261, one launch (start us, length us, event | category | flops | bytes accessed | tf_op | source)
XLA Modules:
  0.0 54.2 jit_solution(17184609506455482844)
XLA Ops:
  0.6 0.9 %pack_halo.1 = bf16[528,128]{1,0:T(8,128)(2,1)S(1)} custom-call(s32[1,128]{1,0:T(1,128)} %bitcast.13, bf16[128,512]{1,0:T(8,128)(2,1)} %k_ref.3, bf16[128,512]{1,0:T(8,128)(2,1)} %v_ref.3), custom_call_target="tpu_custom_call" | custom-call | tf_op jit(solution)/shard_map/pack_halo/pallas_call | solution.py:221
  1.5 2.8 %collective-permute-start = (bf16[528,128]{1,0:T(8,128)(2,1)S(1)}, bf16[528,128]{1,0:T(8,128)(2,1)S(1)}, u32[]{:S(2)}, u32[]{:S(2)}) collective-permute-start(bf16[528,128]{1,0:T(8,128)(2,1)S(1)} %pack_halo.1), channel_id=1, source_target_pairs={{0,1},{1,2},{2,3},{3,388},{4,5},{5,6},{6,7},{7,392},{8,9},{9,10},{... | collective-permute-start | bytes 405512 | tf_op jit(solution)/shard_map/ppermute | solution.py:33
  4.3 5.3 %collective-permute-start.1 = (bf16[528,128]{1,0:T(8,128)(2,1)S(1)}, bf16[528,128]{1,0:T(8,128)(2,1)S(1)}, u32[]{:S(2)}, u32[]{:S(2)}) collective-permute-start(bf16[528,128]{1,0:T(8,128)(2,1)S(1)} %pack_halo.1), channel_id=1, source_target_pairs={{0,2},{1,3},{2,388},{3,389},{4,6},{5,7},{6,392},{7,393},{8,10},{9,... | collective-permute-start | bytes 405512 | tf_op jit(solution)/shard_map/ppermute | solution.py:33
  9.7 1.2 %pack_rows.1 = bf16[256,1280]{1,0:T(8,128)(2,1)S(1)} custom-call(bf16[128,2560]{1,0:T(8,128)(2,1)} %bitcast.9, bf16[128,2560]{1,0:T(8,128)(2,1)} %bitcast.11), custom_call_target="tpu_custom_call" | custom-call | tf_op jit(solution)/shard_map/pack_rows/pallas_call | solution.py:232
  10.9 3.1 %collective-permute-start.2 = (bf16[256,1280]{1,0:T(8,128)(2,1)S(1)}, bf16[256,1280]{1,0:T(8,128)(2,1)S(1)}, u32[]{:S(2)}, u32[]{:S(2)}) collective-permute-start(bf16[256,1280]{1,0:T(8,128)(2,1)S(1)} %pack_rows.1), channel_id=1, source_target_pairs={{0,64},{1,65},{2,66},{3,67},{4,68},{5,69},{6,70},{7,71},{8,72},{9,... | collective-permute-start | bytes 1966088 | tf_op jit(solution)/shard_map/ppermute | solution.py:33
  14.1 0.0 copy-start.4
  14.1 0.1 pad_add_fusion.place_ref
  14.2 0.0 collective-permute-done.one_ref
  14.2 0.6 %copy-done.4 = s32[128]{0:T(128)S(1)} copy-done((s32[128]{0:T(128)S(1)}, s32[128]{0:T(128)}, u32[]{:S(2)}) %copy-start.4) | copy-done | bytes 536
  14.7 0.2 mask_near.1.near_ref
  14.9 0.0 copy-start
  14.9 0.0 copy-start.1
  14.9 0.0 copy-start.2
  14.9 0.0 copy-start.3
  14.9 0.0 collective-permute-done.1.two_ref
  15.0 0.2 mask_far.1.far_ref
  15.1 0.6 %collective-permute-done.2.oqc_ref = bf16[256,1280]{1,0:T(8,128)(2,1)S(1)} collective-permute-done((bf16[256,1280]{1,0:T(8,128)(2,1)S(1)}, bf16[256,1280]{1,0:T(8,128)(2,1)S(1)}, u32[]{:S(2)}, u32[]{:S(2)}) %collective-permute-start.2) | collective-permute-done | bytes 655392 | tf_op jit(solution)/shard_map/ppermute | solution.py:33
  15.8 0.2 copy-done
  16.0 0.2 copy-done.1
  16.2 0.0 copy-done.2
  16.2 0.0 copy-done.3
  16.2 4.3 %attend.1 = (bf16[128,1280]{1,0:T(8,128)(2,1)S(1)}, bf16[128,1280]{1,0:T(8,128)(2,1)S(1)}, bf16[4,384,128]{2,1,0:T(8,128)(2,1)S(1)}) custom-call(s32[4]{0:T(128)S(1)} %pad_add_fusion.place_ref, f32[256,128]{1,0:T(8,128)S(1)} %mask_near.1.near_ref, f32[128,128]{1,0:T(8,128)S(1)} %mask_far.1.far_ref, bf16[128,2560]{1,0:T(8,128)(2,1)S(1)} %bitcast.10, ...), custom_call_target="tpu_custom_call" | custom-call | tf_op jit(solution)/shard_map/attend/pallas_call | solution.py:262
  20.5 15.1 %all_to_all.5 = bf16[4,384,128]{2,1,0:T(8,128)(2,1)S(1)} all-to-all(bf16[4,384,128]{2,1,0:T(8,128)(2,1)S(1)} %get-tuple-element.18), channel_id=1, replica_groups={{0,128,256,384},{64,192,320,448},{1,129,257,385},{65,193,321,449},{2,13..., dimensions={0} | all-to-all | bytes 786432 | tf_op jit(solution)/shard_map/all_to_all | solution.py:275
  35.7 9.2 %collective-permute-start.3 = (bf16[256,128]{1,0:T(8,128)(2,1)S(1)}, bf16[256,128]{1,0:T(8,128)(2,1)S(1)}, u32[]{:S(2)}, u32[]{:S(2)}) collective-permute-start(bf16[256,128]{1,0:T(8,128)(2,1)S(1)} %slice_reduce_fusion), channel_id=1, source_target_pairs={{1,0},{2,1},{3,2},{4,387},{5,4},{6,5},{7,6},{8,391},{9,8},{10,9},{... | collective-permute-start | bytes 196616 | tf_op jit(solution)/shard_map/ppermute | solution.py:33
  44.9 1.9 %collective-permute-start.4 = (bf16[128,128]{1,0:T(8,128)(2,1)S(1)}, bf16[128,128]{1,0:T(8,128)(2,1)S(1)}, u32[]{:S(2)}, u32[]{:S(2)}) collective-permute-start(bf16[128,128]{1,0:T(8,128)(2,1)S(1)} %slice_reduce_fusion.1), channel_id=1, source_target_pairs={{0,0},{1,1},{2,2},{3,3},{4,4},{5,5},{6,6},{7,7},{8,8},{9,9},{10,10... | collective-permute-start | bytes 98312 | tf_op jit(solution)/shard_map/ppermute | solution.py:33
  46.8 1.9 %collective-permute-start.6 = (bf16[128,1280]{1,0:T(8,128)(2,1)S(1)}, bf16[128,1280]{1,0:T(8,128)(2,1)S(1)}, u32[]{:S(2)}, u32[]{:S(2)}) collective-permute-start(bf16[128,1280]{1,0:T(8,128)(2,1)S(1)} %get-tuple-element.23), channel_id=1, source_target_pairs={{0,64},{1,65},{2,66},{3,67},{4,68},{5,69},{6,70},{7,71},{8,72},{9,... | collective-permute-start | bytes 983048 | tf_op jit(solution)/shard_map/ppermute | solution.py:33
  48.7 1.4 %collective-permute-done.4.own_ref = bf16[128,128]{1,0:T(8,128)(2,1)S(1)} collective-permute-done((bf16[128,128]{1,0:T(8,128)(2,1)S(1)}, bf16[128,128]{1,0:T(8,128)(2,1)S(1)}, u32[]{:S(2)}, u32[]{:S(2)}) %collective-permute-start.4) | collective-permute-done | bytes 32800 | tf_op jit(solution)/shard_map/ppermute | solution.py:33
  50.1 0.0 collective-permute-done.3.back_ref
  50.1 1.9 %collective-permute-start.5 = (bf16[128,128]{1,0:T(8,128)(2,1)S(1)}, bf16[128,128]{1,0:T(8,128)(2,1)S(1)}, u32[]{:S(2)}, u32[]{:S(2)}) collective-permute-start(bf16[128,128]{1,0:T(8,128)(2,1)S(1)} %slice_select_fusion), channel_id=1, source_target_pairs={{0,64},{1,65},{2,66},{3,67},{4,68},{5,69},{6,70},{7,71},{8,72},{9,... | collective-permute-start | bytes 98312 | tf_op jit(solution)/shard_map/ppermute | solution.py:33
  52.0 1.2 %collective-permute-done.5.swapped_ref = bf16[128,128]{1,0:T(8,128)(2,1)S(1)} collective-permute-done((bf16[128,128]{1,0:T(8,128)(2,1)S(1)}, bf16[128,128]{1,0:T(8,128)(2,1)S(1)}, u32[]{:S(2)}, u32[]{:S(2)}) %collective-permute-start.5) | collective-permute-done | bytes 32800 | tf_op jit(solution)/shard_map/ppermute | solution.py:33
  53.2 0.1 add_up.1.total_ref
  53.3 0.0 collective-permute-done.6.swapped_ref
  53.3 0.9 %finish.1 = (bf16[128,2560]{1,0:T(8,128)(2,1)}, f32[64,128]{1,0:T(8,128)}, f32[64,128]{1,0:T(8,128)}) custom-call(f32[128,128]{1,0:T(8,128)S(1)} %add_up.1.total_ref, bf16[128,1280]{1,0:T(8,128)(2,1)S(1)} %get-tuple-element.22.own_q_ref, bf16[128,1280]{1,0:T(8,128)(2,1)S(1)} %collective-permute-done.6.swapped_ref), custom_call_target="tpu_custom_call" | custom-call | tf_op jit(solution)/shard_map/finish/pallas_call | solution.py:291
  (3 shorter events, 0.1 us)
Async XLA Ops:
  1.5 12.7 %collective-permute-start = (bf16[528,128]{1,0:T(8,128)(2,1)S(1)}, bf16[528,128]{1,0:T(8,128)(2,1)S(1)}, u32[]{:S(2)}, u32[]{:S(2)}) collective-permute-start(bf16[528,128]{1,0:T(8,128)(2,1)S(1)} %pack_halo.1), channel_id=1, source_target_pairs={{0,1},{1,2},{2,3},{3,388},{4,5},{5,6},{6,7},{7,392},{8,9},{9,10},{... | collective-permute-start | bytes 405512 | tf_op jit(solution)/shard_map/ppermute | solution.py:33
  4.3 10.6 %collective-permute-start.1 = (bf16[528,128]{1,0:T(8,128)(2,1)S(1)}, bf16[528,128]{1,0:T(8,128)(2,1)S(1)}, u32[]{:S(2)}, u32[]{:S(2)}) collective-permute-start(bf16[528,128]{1,0:T(8,128)(2,1)S(1)} %pack_halo.1), channel_id=1, source_target_pairs={{0,2},{1,3},{2,388},{3,389},{4,6},{5,7},{6,392},{7,393},{8,10},{9,... | collective-permute-start | bytes 405512 | tf_op jit(solution)/shard_map/ppermute | solution.py:33
  10.9 4.9 %collective-permute-start.2 = (bf16[256,1280]{1,0:T(8,128)(2,1)S(1)}, bf16[256,1280]{1,0:T(8,128)(2,1)S(1)}, u32[]{:S(2)}, u32[]{:S(2)}) collective-permute-start(bf16[256,1280]{1,0:T(8,128)(2,1)S(1)} %pack_rows.1), channel_id=1, source_target_pairs={{0,64},{1,65},{2,66},{3,67},{4,68},{5,69},{6,70},{7,71},{8,72},{9,... | collective-permute-start | bytes 1966088 | tf_op jit(solution)/shard_map/ppermute | solution.py:33
  14.1 0.7 %copy-start.4 = (s32[128]{0:T(128)S(1)}, s32[128]{0:T(128)}, u32[]{:S(2)}) copy-start(s32[128]{0:T(128)} %param.9) | copy-start | bytes 1540
  14.9 1.1 %copy-start = (bf16[1,128,2560]{2,1,0:T(8,128)(2,1)S(1)}, bf16[1,128,2560]{2,1,0:T(8,128)(2,1)}, u32[]{:S(2)}) copy-start(bf16[1,128,2560]{2,1,0:T(8,128)(2,1)} %param.5) | copy-start | bytes 1966084
  14.9 1.3 %copy-start.1 = (bf16[1,128,2560]{2,1,0:T(8,128)(2,1)S(1)}, bf16[1,128,2560]{2,1,0:T(8,128)(2,1)}, u32[]{:S(2)}) copy-start(bf16[1,128,2560]{2,1,0:T(8,128)(2,1)} %param.8) | copy-start | bytes 1966084
  14.9 1.3 %copy-start.2 = (bf16[128,512]{1,0:T(8,128)(2,1)S(1)}, bf16[128,512]{1,0:T(8,128)(2,1)}, u32[]{:S(2)}) copy-start(bf16[128,512]{1,0:T(8,128)(2,1)} %k_ref.3) | copy-start | bytes 393220
  14.9 1.3 %copy-start.3 = (bf16[128,512]{1,0:T(8,128)(2,1)S(1)}, bf16[128,512]{1,0:T(8,128)(2,1)}, u32[]{:S(2)}) copy-start(bf16[128,512]{1,0:T(8,128)(2,1)} %v_ref.3) | copy-start | bytes 393220
  35.7 14.4 %collective-permute-start.3 = (bf16[256,128]{1,0:T(8,128)(2,1)S(1)}, bf16[256,128]{1,0:T(8,128)(2,1)S(1)}, u32[]{:S(2)}, u32[]{:S(2)}) collective-permute-start(bf16[256,128]{1,0:T(8,128)(2,1)S(1)} %slice_reduce_fusion), channel_id=1, source_target_pairs={{1,0},{2,1},{3,2},{4,387},{5,4},{6,5},{7,6},{8,391},{9,8},{10,9},{... | collective-permute-start | bytes 196616 | tf_op jit(solution)/shard_map/ppermute | solution.py:33
  44.9 5.2 %collective-permute-start.4 = (bf16[128,128]{1,0:T(8,128)(2,1)S(1)}, bf16[128,128]{1,0:T(8,128)(2,1)S(1)}, u32[]{:S(2)}, u32[]{:S(2)}) collective-permute-start(bf16[128,128]{1,0:T(8,128)(2,1)S(1)} %slice_reduce_fusion.1), channel_id=1, source_target_pairs={{0,0},{1,1},{2,2},{3,3},{4,4},{5,5},{6,6},{7,7},{8,8},{9,9},{10,10... | collective-permute-start | bytes 98312 | tf_op jit(solution)/shard_map/ppermute | solution.py:33
  46.8 6.5 %collective-permute-start.6 = (bf16[128,1280]{1,0:T(8,128)(2,1)S(1)}, bf16[128,1280]{1,0:T(8,128)(2,1)S(1)}, u32[]{:S(2)}, u32[]{:S(2)}) collective-permute-start(bf16[128,1280]{1,0:T(8,128)(2,1)S(1)} %get-tuple-element.23), channel_id=1, source_target_pairs={{0,64},{1,65},{2,66},{3,67},{4,68},{5,69},{6,70},{7,71},{8,72},{9,... | collective-permute-start | bytes 983048 | tf_op jit(solution)/shard_map/ppermute | solution.py:33
  50.1 3.1 %collective-permute-start.5 = (bf16[128,128]{1,0:T(8,128)(2,1)S(1)}, bf16[128,128]{1,0:T(8,128)(2,1)S(1)}, u32[]{:S(2)}, u32[]{:S(2)}) collective-permute-start(bf16[128,128]{1,0:T(8,128)(2,1)S(1)} %slice_select_fusion), channel_id=1, source_target_pairs={{0,64},{1,65},{2,66},{3,67},{4,68},{5,69},{6,70},{7,71},{8,72},{9,... | collective-permute-start | bytes 98312 | tf_op jit(solution)/shard_map/ppermute | solution.py:33

commit v11 on v10

--- a/solution.py
+++ b/solution.py
@@ -36,7 +36,8 @@
 def shifted(x, by):
     def target(s, c):
         leaves = c // ROW != (c + by) // ROW
-        return ((3 - s // 2) * 2 + s % 2 if leaves else s, c + by)
+        crossed = (3 - s // 2) * 2 + s % 2 if by == 1 else s ^ 4
+        return (crossed if leaves else s, c + by)
 
     return permuted(x, target)
 

time: 54.7 us -> 54.7 us (level)
  starting transfers between devices: 26.2 us -> 27.1 us
  blocking collectives: 15.1 us -> 14.3 us
    ppermute x7, starting transfers between devices: 26.2 us -> 27.1 us  [permuted(): return lax.ppermute(x, AXES, found)]
    all_to_all x1, blocking collectives: 15.1 us -> 14.3 us  [on_device(): shares = lax.all_to_all(part, 'section', 0, 0, axis_index_groups=chips)]
where the time goes in v11:
time: 54.7 us; the launch traced here: 54.2 us
  starting transfers between devices  27.1 us (50%)
  blocking collectives  14.3 us (26%)
  Pallas kernels  7.66 us (14%)
  waiting for transfers between devices  3.36 us (6%)
  local copies, waits for them, and re-layouts  0.91 us (2%)
  between operations  0.82 us (1%)
    ppermute x7, starting transfers between devices, permuted(): return lax.ppermute(x, AXES, found)  27.1 us
    all_to_all x1, blocking collectives, on_device(): shares = lax.all_to_all(part, 'section', 0, 0, axis_index_groups=chips)  14.3 us
    pallas_call x1, Pallas kernels, on_device(): pl.pallas_call(attend, in_specs=[pl.BlockSpec(memory_space=pltpu.SMEM)] +...  4.26 us
    ppermute x7, waiting for transfers between devices, permuted(): return lax.ppermute(x, AXES, found)  3.36 us
    pallas_call x1, Pallas kernels, on_device(): pl.pallas_call(pack_rows, in_specs=[hbm] * 2, out_specs=vmem, out_shape=j...  1.21 us
  transfers between devices with their start and end apart: 7, of which 3 were waited for; matrix products, arithmetic and copies ran while one was open for 0% of the time, Pallas kernels for 3%

profile of v11, /device:TPU:261, one launch (start us, length us, event | category | flops | bytes accessed | tf_op | source)
XLA Modules:
  0.0 54.2 jit_solution(9569766033263563359)
XLA Ops:
  0.6 0.9 %pack_halo.1 = bf16[528,128]{1,0:T(8,128)(2,1)S(1)} custom-call(s32[1,128]{1,0:T(1,128)} %bitcast.13, bf16[128,512]{1,0:T(8,128)(2,1)} %k_ref.3, bf16[128,512]{1,0:T(8,128)(2,1)} %v_ref.3), custom_call_target="tpu_custom_call" | custom-call | tf_op jit(solution)/shard_map/pack_halo/pallas_call | solution.py:222
  1.5 2.8 %collective-permute-start = (bf16[528,128]{1,0:T(8,128)(2,1)S(1)}, bf16[528,128]{1,0:T(8,128)(2,1)S(1)}, u32[]{:S(2)}, u32[]{:S(2)}) collective-permute-start(bf16[528,128]{1,0:T(8,128)(2,1)S(1)} %pack_halo.1), channel_id=1, source_target_pairs={{0,1},{1,2},{2,3},{3,388},{4,5},{5,6},{6,7},{7,392},{8,9},{9,10},{... | collective-permute-start | bytes 405512 | tf_op jit(solution)/shard_map/ppermute | solution.py:33
  4.3 6.1 %collective-permute-start.1 = (bf16[528,128]{1,0:T(8,128)(2,1)S(1)}, bf16[528,128]{1,0:T(8,128)(2,1)S(1)}, u32[]{:S(2)}, u32[]{:S(2)}) collective-permute-start(bf16[528,128]{1,0:T(8,128)(2,1)S(1)} %pack_halo.1), channel_id=1, source_target_pairs={{0,2},{1,3},{2,260},{3,261},{4,6},{5,7},{6,264},{7,265},{8,10},{9,... | collective-permute-start | bytes 405512 | tf_op jit(solution)/shard_map/ppermute | solution.py:33
  10.5 1.2 %pack_rows.1 = bf16[256,1280]{1,0:T(8,128)(2,1)S(1)} custom-call(bf16[128,2560]{1,0:T(8,128)(2,1)} %bitcast.9, bf16[128,2560]{1,0:T(8,128)(2,1)} %bitcast.11), custom_call_target="tpu_custom_call" | custom-call | tf_op jit(solution)/shard_map/pack_rows/pallas_call | solution.py:233
  11.7 3.1 %collective-permute-start.2 = (bf16[256,1280]{1,0:T(8,128)(2,1)S(1)}, bf16[256,1280]{1,0:T(8,128)(2,1)S(1)}, u32[]{:S(2)}, u32[]{:S(2)}) collective-permute-start(bf16[256,1280]{1,0:T(8,128)(2,1)S(1)} %pack_rows.1), channel_id=1, source_target_pairs={{0,64},{1,65},{2,66},{3,67},{4,68},{5,69},{6,70},{7,71},{8,72},{9,... | collective-permute-start | bytes 1966088 | tf_op jit(solution)/shard_map/ppermute | solution.py:33
  14.9 0.0 copy-start.4
  14.9 0.1 pad_add_fusion.place_ref
  15.0 0.0 collective-permute-done.one_ref
  15.0 0.6 %copy-done.4 = s32[128]{0:T(128)S(1)} copy-done((s32[128]{0:T(128)S(1)}, s32[128]{0:T(128)}, u32[]{:S(2)}) %copy-start.4) | copy-done | bytes 536
  15.5 0.2 mask_near.1.near_ref
  15.7 0.0 copy-start
  15.7 0.0 copy-start.1
  15.7 0.0 copy-start.2
  15.7 0.0 copy-start.3
  15.7 0.8 %collective-permute-done.1.two_ref = bf16[528,128]{1,0:T(8,128)(2,1)S(1)} collective-permute-done((bf16[528,128]{1,0:T(8,128)(2,1)S(1)}, bf16[528,128]{1,0:T(8,128)(2,1)S(1)}, u32[]{:S(2)}, u32[]{:S(2)}) %collective-permute-start.1) | collective-permute-done | bytes 135200 | tf_op jit(solution)/shard_map/ppermute | solution.py:33
  16.5 0.2 mask_far.1.far_ref
  16.7 0.0 collective-permute-done.2.oqc_ref
  16.7 0.1 copy-done
  16.8 0.2 copy-done.1
  17.0 0.0 copy-done.2
  17.0 0.0 copy-done.3
  17.0 4.3 %attend.1 = (bf16[128,1280]{1,0:T(8,128)(2,1)S(1)}, bf16[128,1280]{1,0:T(8,128)(2,1)S(1)}, bf16[4,384,128]{2,1,0:T(8,128)(2,1)S(1)}) custom-call(s32[4]{0:T(128)S(1)} %pad_add_fusion.place_ref, f32[256,128]{1,0:T(8,128)S(1)} %mask_near.1.near_ref, f32[128,128]{1,0:T(8,128)S(1)} %mask_far.1.far_ref, bf16[128,2560]{1,0:T(8,128)(2,1)S(1)} %bitcast.10, ...), custom_call_target="tpu_custom_call" | custom-call | tf_op jit(solution)/shard_map/attend/pallas_call | solution.py:263
  21.3 14.3 %all_to_all.5 = bf16[4,384,128]{2,1,0:T(8,128)(2,1)S(1)} all-to-all(bf16[4,384,128]{2,1,0:T(8,128)(2,1)S(1)} %get-tuple-element.18), channel_id=1, replica_groups={{0,128,256,384},{64,192,320,448},{1,129,257,385},{65,193,321,449},{2,13..., dimensions={0} | all-to-all | bytes 786432 | tf_op jit(solution)/shard_map/all_to_all | solution.py:276
  35.6 9.2 %collective-permute-start.3 = (bf16[256,128]{1,0:T(8,128)(2,1)S(1)}, bf16[256,128]{1,0:T(8,128)(2,1)S(1)}, u32[]{:S(2)}, u32[]{:S(2)}) collective-permute-start(bf16[256,128]{1,0:T(8,128)(2,1)S(1)} %slice_reduce_fusion), channel_id=1, source_target_pairs={{1,0},{2,1},{3,2},{4,387},{5,4},{6,5},{7,6},{8,391},{9,8},{10,9},{... | collective-permute-start | bytes 196616 | tf_op jit(solution)/shard_map/ppermute | solution.py:33
  44.9 1.9 %collective-permute-start.4 = (bf16[128,128]{1,0:T(8,128)(2,1)S(1)}, bf16[128,128]{1,0:T(8,128)(2,1)S(1)}, u32[]{:S(2)}, u32[]{:S(2)}) collective-permute-start(bf16[128,128]{1,0:T(8,128)(2,1)S(1)} %slice_reduce_fusion.1), channel_id=1, source_target_pairs={{0,0},{1,1},{2,2},{3,3},{4,4},{5,5},{6,6},{7,7},{8,8},{9,9},{10,10... | collective-permute-start | bytes 98312 | tf_op jit(solution)/shard_map/ppermute | solution.py:33
  46.8 1.9 %collective-permute-start.6 = (bf16[128,1280]{1,0:T(8,128)(2,1)S(1)}, bf16[128,1280]{1,0:T(8,128)(2,1)S(1)}, u32[]{:S(2)}, u32[]{:S(2)}) collective-permute-start(bf16[128,1280]{1,0:T(8,128)(2,1)S(1)} %get-tuple-element.23), channel_id=1, source_target_pairs={{0,64},{1,65},{2,66},{3,67},{4,68},{5,69},{6,70},{7,71},{8,72},{9,... | collective-permute-start | bytes 983048 | tf_op jit(solution)/shard_map/ppermute | solution.py:33
  48.7 1.4 %collective-permute-done.4.own_ref = bf16[128,128]{1,0:T(8,128)(2,1)S(1)} collective-permute-done((bf16[128,128]{1,0:T(8,128)(2,1)S(1)}, bf16[128,128]{1,0:T(8,128)(2,1)S(1)}, u32[]{:S(2)}, u32[]{:S(2)}) %collective-permute-start.4) | collective-permute-done | bytes 32800 | tf_op jit(solution)/shard_map/ppermute | solution.py:33
  50.1 0.0 collective-permute-done.3.back_ref
  50.1 1.9 %collective-permute-start.5 = (bf16[128,128]{1,0:T(8,128)(2,1)S(1)}, bf16[128,128]{1,0:T(8,128)(2,1)S(1)}, u32[]{:S(2)}, u32[]{:S(2)}) collective-permute-start(bf16[128,128]{1,0:T(8,128)(2,1)S(1)} %slice_select_fusion), channel_id=1, source_target_pairs={{0,64},{1,65},{2,66},{3,67},{4,68},{5,69},{6,70},{7,71},{8,72},{9,... | collective-permute-start | bytes 98312 | tf_op jit(solution)/shard_map/ppermute | solution.py:33
  52.0 1.2 %collective-permute-done.5.swapped_ref = bf16[128,128]{1,0:T(8,128)(2,1)S(1)} collective-permute-done((bf16[128,128]{1,0:T(8,128)(2,1)S(1)}, bf16[128,128]{1,0:T(8,128)(2,1)S(1)}, u32[]{:S(2)}, u32[]{:S(2)}) %collective-permute-start.5) | collective-permute-done | bytes 32800 | tf_op jit(solution)/shard_map/ppermute | solution.py:33
  53.2 0.1 add_up.1.total_ref
  53.3 0.0 collective-permute-done.6.swapped_ref
  53.3 0.9 %finish.1 = (bf16[128,2560]{1,0:T(8,128)(2,1)}, f32[64,128]{1,0:T(8,128)}, f32[64,128]{1,0:T(8,128)}) custom-call(f32[128,128]{1,0:T(8,128)S(1)} %add_up.1.total_ref, bf16[128,1280]{1,0:T(8,128)(2,1)S(1)} %get-tuple-element.22.own_q_ref, bf16[128,1280]{1,0:T(8,128)(2,1)S(1)} %collective-permute-done.6.swapped_ref), custom_call_target="tpu_custom_call" | custom-call | tf_op jit(solution)/shard_map/finish/pallas_call | solution.py:292
  (3 shorter events, 0.1 us)
Async XLA Ops:
  1.5 13.4 %collective-permute-start = (bf16[528,128]{1,0:T(8,128)(2,1)S(1)}, bf16[528,128]{1,0:T(8,128)(2,1)S(1)}, u32[]{:S(2)}, u32[]{:S(2)}) collective-permute-start(bf16[528,128]{1,0:T(8,128)(2,1)S(1)} %pack_halo.1), channel_id=1, source_target_pairs={{0,1},{1,2},{2,3},{3,388},{4,5},{5,6},{6,7},{7,392},{8,9},{9,10},{... | collective-permute-start | bytes 405512 | tf_op jit(solution)/shard_map/ppermute | solution.py:33
  4.3 12.2 %collective-permute-start.1 = (bf16[528,128]{1,0:T(8,128)(2,1)S(1)}, bf16[528,128]{1,0:T(8,128)(2,1)S(1)}, u32[]{:S(2)}, u32[]{:S(2)}) collective-permute-start(bf16[528,128]{1,0:T(8,128)(2,1)S(1)} %pack_halo.1), channel_id=1, source_target_pairs={{0,2},{1,3},{2,260},{3,261},{4,6},{5,7},{6,264},{7,265},{8,10},{9,... | collective-permute-start | bytes 405512 | tf_op jit(solution)/shard_map/ppermute | solution.py:33
  11.7 5.0 %collective-permute-start.2 = (bf16[256,1280]{1,0:T(8,128)(2,1)S(1)}, bf16[256,1280]{1,0:T(8,128)(2,1)S(1)}, u32[]{:S(2)}, u32[]{:S(2)}) collective-permute-start(bf16[256,1280]{1,0:T(8,128)(2,1)S(1)} %pack_rows.1), channel_id=1, source_target_pairs={{0,64},{1,65},{2,66},{3,67},{4,68},{5,69},{6,70},{7,71},{8,72},{9,... | collective-permute-start | bytes 1966088 | tf_op jit(solution)/shard_map/ppermute | solution.py:33
  14.9 0.7 %copy-start.4 = (s32[128]{0:T(128)S(1)}, s32[128]{0:T(128)}, u32[]{:S(2)}) copy-start(s32[128]{0:T(128)} %param.9) | copy-start | bytes 1540
  15.7 1.1 %copy-start = (bf16[1,128,2560]{2,1,0:T(8,128)(2,1)S(1)}, bf16[1,128,2560]{2,1,0:T(8,128)(2,1)}, u32[]{:S(2)}) copy-start(bf16[1,128,2560]{2,1,0:T(8,128)(2,1)} %param.5) | copy-start | bytes 1966084
  15.7 1.3 %copy-start.1 = (bf16[1,128,2560]{2,1,0:T(8,128)(2,1)S(1)}, bf16[1,128,2560]{2,1,0:T(8,128)(2,1)}, u32[]{:S(2)}) copy-start(bf16[1,128,2560]{2,1,0:T(8,128)(2,1)} %param.8) | copy-start | bytes 1966084
  15.7 1.3 %copy-start.2 = (bf16[128,512]{1,0:T(8,128)(2,1)S(1)}, bf16[128,512]{1,0:T(8,128)(2,1)}, u32[]{:S(2)}) copy-start(bf16[128,512]{1,0:T(8,128)(2,1)} %k_ref.3) | copy-start | bytes 393220
  15.7 1.3 %copy-start.3 = (bf16[128,512]{1,0:T(8,128)(2,1)S(1)}, bf16[128,512]{1,0:T(8,128)(2,1)}, u32[]{:S(2)}) copy-start(bf16[128,512]{1,0:T(8,128)(2,1)} %v_ref.3) | copy-start | bytes 393220
  35.6 14.5 %collective-permute-start.3 = (bf16[256,128]{1,0:T(8,128)(2,1)S(1)}, bf16[256,128]{1,0:T(8,128)(2,1)S(1)}, u32[]{:S(2)}, u32[]{:S(2)}) collective-permute-start(bf16[256,128]{1,0:T(8,128)(2,1)S(1)} %slice_reduce_fusion), channel_id=1, source_target_pairs={{1,0},{2,1},{3,2},{4,387},{5,4},{6,5},{7,6},{8,391},{9,8},{10,9},{... | collective-permute-start | bytes 196616 | tf_op jit(solution)/shard_map/ppermute | solution.py:33
  44.9 5.2 %collective-permute-start.4 = (bf16[128,128]{1,0:T(8,128)(2,1)S(1)}, bf16[128,128]{1,0:T(8,128)(2,1)S(1)}, u32[]{:S(2)}, u32[]{:S(2)}) collective-permute-start(bf16[128,128]{1,0:T(8,128)(2,1)S(1)} %slice_reduce_fusion.1), channel_id=1, source_target_pairs={{0,0},{1,1},{2,2},{3,3},{4,4},{5,5},{6,6},{7,7},{8,8},{9,9},{10,10... | collective-permute-start | bytes 98312 | tf_op jit(solution)/shard_map/ppermute | solution.py:33
  46.8 6.5 %collective-permute-start.6 = (bf16[128,1280]{1,0:T(8,128)(2,1)S(1)}, bf16[128,1280]{1,0:T(8,128)(2,1)S(1)}, u32[]{:S(2)}, u32[]{:S(2)}) collective-permute-start(bf16[128,1280]{1,0:T(8,128)(2,1)S(1)} %get-tuple-element.23), channel_id=1, source_target_pairs={{0,64},{1,65},{2,66},{3,67},{4,68},{5,69},{6,70},{7,71},{8,72},{9,... | collective-permute-start | bytes 983048 | tf_op jit(solution)/shard_map/ppermute | solution.py:33
  50.1 3.1 %collective-permute-start.5 = (bf16[128,128]{1,0:T(8,128)(2,1)S(1)}, bf16[128,128]{1,0:T(8,128)(2,1)S(1)}, u32[]{:S(2)}, u32[]{:S(2)}) collective-permute-start(bf16[128,128]{1,0:T(8,128)(2,1)S(1)} %slice_select_fusion), channel_id=1, source_target_pairs={{0,64},{1,65},{2,66},{3,67},{4,68},{5,69},{6,70},{7,71},{8,72},{9,... | collective-permute-start | bytes 98312 | tf_op jit(solution)/shard_map/ppermute | solution.py:33
